TPU v7x, 512 devices: a whole 4x8x8 slice. The times are simulated.
512 devices in a mesh: segment: 16 (over y, core), tile: 32 (over z, x).
Axes of the slice: x: 4, y: 8, z: 8, core: 2. Of those that a mesh axis runs over, the one named last changes fastest.
Arguments:
- tile_mask_amplitude: bfloat16 [512, 256, 256], P('tile', 'segment'), may hold values from -4 to 4
- tile_target_images: bfloat16 [512, 256, 256], P('tile', 'segment'), may hold values from 0 to 1
- spectra: float32 [12, 2, 31, 31], replicated, may hold values from -6 to 6
- slot_dose_scale: float32 [512], P('tile'), may hold values from 0.5 to 2
- slot_row: int32 [512], P('tile'), may hold values from -1 to 31, as said below
- side_source: int32 [512, 2], P('tile'), may hold values from -1 to 11, as said below
Outputs:
- corrected_mask: bfloat16 [512, 256, 256], P('tile', 'segment')
- resist_image: float32 [512, 256, 256], P('tile', 'segment')
Inputs may be any that keep to these rules, and one draw needn't show every extreme that they name: `slot_row`: in each tile owner's 16 slots the patterned tiles come first, with strictly rising tile rows below 32, and -1 marks the empty slots after them; every owner has at least 4 patterned tiles and at most 12, and some owner has exactly 12; every owner holds tile row 31. `side_source`: an entry names the slot of the neighbouring tile owner that holds the same tile row as this slot; it is -1 for empty slots, at the window's ends and where that tile is not patterned.
All inputs are finite; a program needn't handle non-finite values.
Results may differ from a plain program's by a relative error of at most 0.0075.
Values may be sent and summed in bfloat16 or wider, within the bound.
No kernel may reach another device: no remote copies, remote signals or barrier semaphores. Data moves between devices by JAX's collectives and lax.ppermute only.
A program may use at most 64 MiB of HBM per device.

v0:
```python
import math

import jax
import jax.numpy as jnp
from jax import lax
from jax.sharding import PartitionSpec as P

RB = 8
ITERS = 2


STEEPNESS = 1.5
THRESHOLD = 2.0
STEP_GAIN = 0.5


def passed_along(block, axis, distance):
    devices = range(lax.axis_size(axis))
    route = [(i - distance, i) for i in devices if i - distance in devices]
    return lax.ppermute(block, axis, route)


def with_halo(cells, sides, width):
    for axis, dim in sides:
        count = lax.axis_size(axis)
        head = lax.slice_in_dim(cells, 0, width, axis=dim)
        tail = lax.slice_in_dim(cells, cells.shape[dim] - width, cells.shape[dim], axis=dim)
        cells = jnp.concatenate(
            [
                lax.ppermute(tail, axis, [(i, (i + 1) % count) for i in range(count)]),
                cells,
                lax.ppermute(head, axis, [((i + 1) % count, i) for i in range(count)]),
            ],
            axis=dim,
        )
    return cells


def wave_tables(length, freq_count):
    position = jnp.arange(length, dtype=jnp.int32)
    frequency = jnp.arange(freq_count, dtype=jnp.int32) - freq_count // 2
    phase_index = position[:, None] * frequency[None, :] % length
    angle_rad = phase_index.astype(jnp.float32) * jnp.float32(2.0 * math.pi / length)
    return (jnp.cos(angle_rad), jnp.sin(angle_rad))


def transform_tables(length, freq_count):
    cosine, sine_part = wave_tables(length, freq_count)
    norm_scale = jnp.float32(1.0 / math.sqrt(length))
    forward_cols = jnp.concatenate([cosine * norm_scale, -(sine_part * norm_scale)], 1).astype(
        jnp.bfloat16
    )
    forward_rows = jnp.concatenate([cosine * norm_scale, sine_part * norm_scale], 1).astype(
        jnp.bfloat16
    )
    inverse_rows = jnp.concatenate([cosine, sine_part], 1).astype(jnp.bfloat16)
    cosine_low = cosine.T.astype(jnp.bfloat16)
    sine_low = sine_part.T.astype(jnp.bfloat16)
    inverse_cols = jnp.concatenate(
        [jnp.concatenate([cosine_low, sine_low], 1), jnp.concatenate([-sine_low, cosine_low], 1)], 0
    )
    return (forward_cols, forward_rows, inverse_rows, inverse_cols)


def blur_weights(radius):
    offsets = jnp.arange(2 * radius + 1, dtype=jnp.float32) - radius
    spread_width = radius / 2.0
    weights = jnp.exp(-offsets * offsets / (2.0 * spread_width * spread_width))
    return weights / jnp.sum(weights)


def spectrum_part(tile_rows, rows_table, forward_cols, freq_count):
    y_part = jnp.einsum(
        "nry,yb->nrb", tile_rows, forward_cols, preferred_element_type=jnp.float32
    ).astype(jnp.bfloat16)
    inner = jnp.einsum("ra,nrb->nab", rows_table, y_part, preferred_element_type=jnp.float32)
    real_part = inner[:, :freq_count, :freq_count] + inner[:, freq_count:, freq_count:]
    imag_part = inner[:, :freq_count, freq_count:] - inner[:, freq_count:, :freq_count]
    return jnp.stack([real_part, imag_part], 1)


def intensity_rows(spectrum, spectra, rows_inverse, inverse_cols, tile_edge):
    item_count = spectrum.shape[0]
    row_count = rows_inverse.shape[0]
    freq_count = spectra.shape[2]
    kernel_count = spectra.shape[0]
    block_len = 8
    spec_real = spectra[:, 0]
    spec_imag = spectra[:, 1]

    def one_block(spec_block):
        mask_real = spec_block[:, None, 0]
        mask_imag = spec_block[:, None, 1]
        prod_real = (spec_real * mask_real - spec_imag * mask_imag).astype(jnp.bfloat16)
        prod_imag = (spec_real * mask_imag + spec_imag * mask_real).astype(jnp.bfloat16)
        right_block = jnp.concatenate(
            [
                jnp.concatenate([prod_real, prod_imag], 3),
                jnp.concatenate([-prod_imag, prod_real], 3),
            ],
            2,
        )
        field_a = jnp.einsum(
            "ra,nkab->nkrb", rows_inverse, right_block, preferred_element_type=jnp.float32
        )
        field_a = (field_a * jnp.float32(1.0 / freq_count)).astype(jnp.bfloat16)
        field_full = jnp.einsum(
            "nkrb,by->nkry", field_a, inverse_cols, preferred_element_type=jnp.float32
        )
        squares = jnp.sum(field_full * field_full, axis=1)
        return (squares[..., :tile_edge] + squares[..., tile_edge:]) * jnp.float32(
            1.0 / kernel_count
        )

    grouped = spectrum.reshape(item_count // block_len, block_len, 2, freq_count, freq_count)
    return lax.map(one_block, grouped).reshape(item_count, row_count, tile_edge)


def pick_bands(received, source):
    valid = (source >= 0).astype(jnp.float32)
    taken = jnp.take(received, jnp.maximum(source, 0), axis=0)
    return taken * valid[:, None, None]


def body(tile_mask_amplitude, tile_target_images, spectra, slot_dose_scale, slot_row, side_source):
    slot_count, row_count, tile_edge = tile_mask_amplitude.shape
    freq_count = spectra.shape[2]
    segment_index = lax.axis_index("segment")
    last_segment = lax.axis_size("segment") - 1
    forward_cols, forward_rows, inverse_rows, inverse_cols = transform_tables(tile_edge, freq_count)
    rows_inverse = lax.dynamic_slice_in_dim(inverse_rows, segment_index * row_count, row_count, 0)
    weights = blur_weights(RB)
    weight = slot_dose_scale * (slot_row >= 0).astype(jnp.float32)
    slot_index = jnp.arange(slot_count, dtype=jnp.int32)
    prev_row = jnp.concatenate([jnp.full((1,), -7, jnp.int32), slot_row[:-1]])
    up_ok = (slot_index > 0) & (prev_row >= 0) & (slot_row >= 0) & (prev_row == slot_row - 1)
    down_ok = jnp.concatenate([up_ok[1:], jnp.zeros((1,), dtype=bool)])
    up_weight = up_ok.astype(jnp.float32)[:, None, None]
    down_weight = down_ok.astype(jnp.float32)[:, None, None]
    zero_rim = jnp.zeros((1, RB, tile_edge), jnp.float32)
    mask_now = tile_mask_amplitude
    resist = jnp.zeros((slot_count, row_count, tile_edge), jnp.float32)
    for sweep in range(ITERS):
        work_tiles = mask_now
        whole_tiles = lax.all_gather(work_tiles, "segment", axis=1, tiled=True)
        spectrum = spectrum_part(whole_tiles, forward_rows, forward_cols, freq_count)
        intensity = intensity_rows(spectrum, spectra, rows_inverse, inverse_cols, tile_edge)
        intensity = intensity * weight[:, None, None]
        from_left = passed_along(intensity[:, :, tile_edge - RB :], "tile", 1)
        from_right = passed_along(intensity[:, :, :RB], "tile", -1)
        left_band = pick_bands(from_left, side_source[:, 0])
        right_band = pick_bands(from_right, side_source[:, 1])
        padded = jnp.concatenate([left_band, intensity, right_band], 2)
        horiz_blur = weights[0] * padded[:, :, 0:tile_edge]
        for shift_by in range(1, 2 * RB + 1):
            horiz_blur = (
                horiz_blur + weights[shift_by] * padded[:, :, shift_by : shift_by + tile_edge]
            )
        extended = with_halo(horiz_blur.astype(jnp.bfloat16), (("segment", 1),), RB).astype(
            horiz_blur.dtype
        )
        upper_rim = extended[:, :RB]
        lower_rim = extended[:, row_count + RB :]
        upper_next = jnp.concatenate([zero_rim, upper_rim[:-1]], 0) * up_weight
        lower_next = jnp.concatenate([lower_rim[1:], zero_rim], 0) * down_weight
        upper_rim = jnp.where(segment_index == 0, upper_next, upper_rim)
        lower_rim = jnp.where(segment_index == last_segment, lower_next, lower_rim)
        vert_padded = jnp.concatenate([upper_rim, horiz_blur, lower_rim], 1)
        vert_blur = weights[0] * vert_padded[:, 0:row_count, :]
        for shift_by in range(1, 2 * RB + 1):
            vert_blur = (
                vert_blur + weights[shift_by] * vert_padded[:, shift_by : shift_by + row_count, :]
            )
        resist = jax.nn.sigmoid(STEEPNESS * (vert_blur - THRESHOLD))
        mask_now = (
            mask_now.astype(jnp.float32)
            + STEP_GAIN * (tile_target_images.astype(jnp.float32) - resist)
        ).astype(jnp.bfloat16)
    return (mask_now, resist)


def solution(mesh):
    in_specs = (
        P("tile", "segment", None),
        P("tile", "segment", None),
        P(),
        P("tile"),
        P("tile"),
        P("tile", None),
    )
    out_specs = (P("tile", "segment", None), P("tile", "segment", None))
    return jax.shard_map(body, mesh=mesh, in_specs=in_specs, out_specs=out_specs, check_vma=False)
```

profile of v0, /device:TPU:198, one launch (start us, length us, event | category | flops | bytes accessed | tf_op | source)
XLA Modules:
  0.0 219.6 jit_solution(1284356911872364960)
XLA Ops:
  7.2 0.7 all-gather.3.cloned.1.call-update
  8.3 0.7 copy.204
  9.0 1.4 fusion.317
  10.5 0.6 fusion.306
  11.1 0.7 broadcast_divide_fusion
  11.7 0.6 compare_and_fusion.1
  12.3 0.6 pad_clamp_fusion.1
  12.9 0.7 fusion.322
  14.1 0.6 maximum_maximum_fusion
  14.7 0.5 compare_select_fusion.2
  15.2 0.7 fusion.314
  15.9 0.6 fusion.304
  16.5 38.0 %all-gather.3.cloned.1.call-done = bf16[16,256,256]{2,1,0:T(8,128)(2,1)} async-done(((bf16[16,16,256]{2,1,0:T(8,128)(2,1)}), bf16[16,256,256]{2,1,0:T(8,128)(2,1)}) %all-gather.3.cloned.1.call-update) | async-done | bytes 2097168 | tf_op jit(solution)/shard_map/all_gather | solution.py:145
  54.5 2.5 %fusion.67 = f32[16,62,62]{1,2,0:T(8,128)S(1)} fusion(bf16[16,256,256]{2,1,0:T(8,128)(2,1)} %all-gather.3.cloned.1.call-done, bf16[256,31]{0,1:T(8,128)(2,1)S(1)} %get-tuple-element.236, bf16[256,31]{0,1:T(8,128)(2,1)S(1)} %get-tuple-element.234, bf16[256,31]{0,1:T(8,128)(2,1)S(1)} %get-tuple-element.235), kind=kOutput, calls=%fused_computation.64 | convolution fusion | flops 161894400 | bytes 2390784 | tf_op jit(solution)/shard_map/ra,nrb->nab/dot_general | solution.py:76
  57.5 0.2 copy.202
  57.7 0.7 broadcast.123.clone
  58.5 8.2 %while.20 = (s32[]{:T(128)}, f32[2,8,16,256]{3,2,1,0:T(8,128)}, f32[12,1,31,31]{3,2,0,1:T(8,128)S(1)}, f32[2,8,2,31,31]{4,1,3,2,0:T(8,128)S(1)}, f32[12,1,31,31]...) while((s32[]{:T(128)}, f32[2,8,16,256]{3,2,1,0:T(8,128)}, ...), condition=%wide.region_3.4_spmd, body=%wide.region_1.3_spmd.sunk | while | flops 115241184 | bytes 2505049 | solution.py:116
  58.6 0.4 add_convert_fusion.5
  59.0 0.3 fusion.337
  59.3 2.6 %multiply_reduce_fusion.4 = f32[8,16,512]{2,1,0:T(8,128)S(1)} fusion(bf16[8,12,31,31]{3,2,1,0:T(8,128)(2,1)S(1)} %get-tuple-element.326, bf16[8,12,31,31]{3,2,1,0:T(8,128)(2,1)S(1)} %fusion.337, bf16[8,12,31,31]{3,2,1,0:T(8,128)(2,1)S(1)} %get-tuple-element.327, bf16[62,512]{1,0:T(8,128)(2,1)} %get-tuple-element.361, ...), kind=kOutput, calls=%fused_computation.4.clone.1 | convolution fusion | flops 113976320 | bytes 881152 | tf_op jit(solution)/shard_map/while/body/eval_jaxpr/nkrb,by->nkry/dot_general | solution.py:107
  61.9 0.7 fusion.338
  62.7 0.4 add_convert_fusion.5
  63.1 0.3 fusion.337
  63.4 2.6 %multiply_reduce_fusion.4 = f32[8,16,512]{2,1,0:T(8,128)S(1)} fusion(bf16[8,12,31,31]{3,2,1,0:T(8,128)(2,1)S(1)} %get-tuple-element.326, bf16[8,12,31,31]{3,2,1,0:T(8,128)(2,1)S(1)} %fusion.337, bf16[8,12,31,31]{3,2,1,0:T(8,128)(2,1)S(1)} %get-tuple-element.327, bf16[62,512]{1,0:T(8,128)(2,1)} %get-tuple-element.361, ...), kind=kOutput, calls=%fused_computation.4.clone.1 | convolution fusion | flops 113976320 | bytes 881152 | tf_op jit(solution)/shard_map/while/body/eval_jaxpr/nkrb,by->nkry/dot_general | solution.py:107
  66.0 0.7 fusion.338
  66.7 1.0 bitcast_multiply_fusion.1
  67.8 4.7 %collective-permute-start = (f32[16,16,8]{2,1,0:T(8,128)S(1)}, f32[16,16,8]{2,1,0:T(8,128)S(1)}, u32[]{:S(2)}, u32[]{:S(2)}) collective-permute-start(f32[16,16,8]{2,1,0:T(8,128)S(1)} %get-tuple-element.203), channel_id=1, source_target_pairs={{0,1},{1,2},{2,3},{3,4},{4,5},{5,6},{6,7},{7,8},{8,9},{9,10},{10,1... | collective-permute-start | bytes 24584 | tf_op jit(solution)/shard_map/ppermute | solution.py:20
  72.6 0.6 pad_clamp_fusion
  73.2 0.8 slice.537
  74.0 2.1 collective-permute-start.1
  76.1 0.7 gather_fusion
  76.9 0.8 select_multiply_fusion.3
  77.7 6.8 %collective-permute-done.1 = f32[16,16,8]{2,1,0:T(8,128)S(1)} collective-permute-done((f32[16,16,8]{2,1,0:T(8,128)S(1)}, f32[16,16,8]{2,1,0:T(8,128)S(1)}, u32[]{:S(2)}, u32[]{:S(2)}) %collective-permute-start.1) | collective-permute-done | bytes 8224 | tf_op jit(solution)/shard_map/ppermute | solution.py:20
  84.5 0.6 gather_fusion.1
  85.2 12.2 %fusion.315 = (bf16[16,16,256]{2,1,0:T(8,128)(2,1)S(1)}, f32[16,16,256]{2,1,0:T(8,128)S(1)}) fusion(f32[16,16,8]{2,1,0:T(8,128)S(1)} %select_multiply_fusion.1, f32[16,16,256]{2,1,0:T(8,128)S(1)} %bitcast_multiply_fusion.1, f32[]{:T(128)} %bitcast.49, f32[]{:T(128)} %bitcast.48, f32[]{:T(128)} %bitcast.47, f32[]{:T(128)} %bitcast.46, f32[]{:T(128)} %bitcast.45, ...), kind=kLoop, calls=%fused_computation.474 | loop fusion | flops 3276800 | bytes 671812 | tf_op jit(solution)/shard_map/convert_element_type | solution.py:159
  97.5 2.9 %collective-permute-start.3 = (bf16[16,8,256]{2,1,0:T(8,128)(2,1)S(1)}, bf16[16,8,256]{2,1,0:T(8,128)(2,1)S(1)}, u32[]{:S(2)}, u32[]{:S(2)}) collective-permute-start(bf16[16,8,256]{2,1,0:T(8,128)(2,1)S(1)} %get-tuple-element.208), channel_id=1, source_target_pairs={{32,0},{64,32},{96,64},{128,96},{160,128},{192,160},{224,192},{256... | collective-permute-start | bytes 196616 | tf_op jit(solution)/shard_map/ppermute | solution.py:32
  100.5 1.9 collective-permute-done.2
  102.5 11.4 %fusion.76 = bf16[16,16,256]{2,1,0:T(8,128)(2,1)S(1)} fusion(bf16[16,16,256]{2,1,0:T(8,128)(2,1)S(1)} %copy-done.2, f32[16,16,256]{2,1,0:T(8,128)S(1)} %get-tuple-element.174, f32[16,8,256]{2,1,0:T(8,128)S(1)} %get-tuple-element.200, f32[16,8,256]{2,1,0:T(8,128)S(1)} %get-tuple-element.199, bf16[16,16,256]{2,1,0:T(8,128)(2,1)S(1)} %copy-done.4, ...), kind=kLoop, calls=%fused_computation.185 | loop fusion | flops 3932160 | bytes 917572 | tf_op jit(solution)/shard_map/convert_element_type | solution.py:178
  113.9 0.7 copy-done
  114.6 0.7 copy.207
  115.3 38.7 %all-gather.5.cloned.1.call-done = bf16[16,256,256]{2,0,1:T(8,128)(2,1)} async-done(((bf16[16,16,256]{2,0,1:T(8,128)(2,1)}), bf16[16,256,256]{2,0,1:T(8,128)(2,1)}) %all-gather.5.cloned.1.call-update) | async-done | bytes 2097168 | tf_op jit(solution)/shard_map/all_gather | solution.py:145
  154.0 2.5 %fusion.71 = f32[16,62,62]{1,2,0:T(8,128)S(1)} fusion(bf16[16,256,256]{2,0,1:T(8,128)(2,1)} %all-gather.5.cloned.1.call-done, bf16[256,31]{0,1:T(8,128)(2,1)S(1)} %get-tuple-element.236, bf16[256,31]{0,1:T(8,128)(2,1)S(1)} %get-tuple-element.234, bf16[256,31]{0,1:T(8,128)(2,1)S(1)} %copy-done.6), kind=kOutput, calls=%fused_computation.66 | convolution fusion | flops 161894400 | bytes 2390784 | tf_op jit(solution)/shard_map/ra,nrb->nab/dot_general | solution.py:76
  157.0 0.2 copy.210
  157.2 0.7 broadcast.123
  158.0 8.2 %while.21 = (s32[]{:T(128)}, f32[2,8,16,256]{3,2,1,0:T(8,128)}, f32[12,1,31,31]{3,2,0,1:T(8,128)S(1)}, f32[2,8,2,31,31]{4,1,3,2,0:T(8,128)S(1)}, f32[12,1,31,31]...) while((s32[]{:T(128)}, f32[2,8,16,256]{3,2,1,0:T(8,128)}, ...), condition=%wide.region_6.8_spmd, body=%wide.region_4.7_spmd.sunk | while | flops 115241184 | bytes 2505049 | solution.py:116
  158.1 0.4 add_convert_fusion.6
  158.5 0.3 fusion.342
  158.8 2.6 %multiply_reduce_fusion.5 = f32[8,16,512]{2,1,0:T(8,128)S(1)} fusion(bf16[8,12,31,31]{3,2,1,0:T(8,128)(2,1)S(1)} %get-tuple-element.337, bf16[8,12,31,31]{3,2,1,0:T(8,128)(2,1)S(1)} %fusion.342, bf16[8,12,31,31]{3,2,1,0:T(8,128)(2,1)S(1)} %get-tuple-element.338, bf16[62,512]{1,0:T(8,128)(2,1)} %get-tuple-element.385, ...), kind=kOutput, calls=%fused_computation.31.clone.1 | convolution fusion | flops 113976320 | bytes 881152 | tf_op jit(solution)/shard_map/while/body/eval_jaxpr/nkrb,by->nkry/dot_general | solution.py:107
  161.4 0.7 fusion.343
  162.2 0.4 add_convert_fusion.6
  162.6 0.3 fusion.342
  162.9 2.6 %multiply_reduce_fusion.5 = f32[8,16,512]{2,1,0:T(8,128)S(1)} fusion(bf16[8,12,31,31]{3,2,1,0:T(8,128)(2,1)S(1)} %get-tuple-element.337, bf16[8,12,31,31]{3,2,1,0:T(8,128)(2,1)S(1)} %fusion.342, bf16[8,12,31,31]{3,2,1,0:T(8,128)(2,1)S(1)} %get-tuple-element.338, bf16[62,512]{1,0:T(8,128)(2,1)} %get-tuple-element.385, ...), kind=kOutput, calls=%fused_computation.31.clone.1 | convolution fusion | flops 113976320 | bytes 881152 | tf_op jit(solution)/shard_map/while/body/eval_jaxpr/nkrb,by->nkry/dot_general | solution.py:107
  165.5 0.7 fusion.343
  166.2 1.0 bitcast_multiply_fusion
  167.3 4.7 %collective-permute-start.4 = (f32[16,16,8]{2,1,0:T(8,128)S(1)}, f32[16,16,8]{2,1,0:T(8,128)S(1)}, u32[]{:S(2)}, u32[]{:S(2)}) collective-permute-start(f32[16,16,8]{2,1,0:T(8,128)S(1)} %get-tuple-element.197), channel_id=1, source_target_pairs={{0,1},{1,2},{2,3},{3,4},{4,5},{5,6},{6,7},{7,8},{8,9},{9,10},{10,1... | collective-permute-start | bytes 24584 | tf_op jit(solution)/shard_map/ppermute | solution.py:20
  172.1 1.9 collective-permute-start.5
  174.0 1.2 collective-permute-done.4
  175.3 0.7 gather_fusion.2
  176.3 6.4 %collective-permute-done.5 = f32[16,16,8]{2,1,0:T(8,128)S(1)} collective-permute-done((f32[16,16,8]{2,1,0:T(8,128)S(1)}, f32[16,16,8]{2,1,0:T(8,128)S(1)}, u32[]{:S(2)}, u32[]{:S(2)}) %collective-permute-start.5) | collective-permute-done | bytes 8224 | tf_op jit(solution)/shard_map/ppermute | solution.py:20
  182.7 0.6 gather_fusion.3
  183.4 12.2 %fusion.312 = (bf16[16,16,256]{2,1,0:T(8,128)(2,1)S(1)}, f32[16,16,256]{2,1,0:T(8,128)S(1)}) fusion(f32[16,16,8]{2,1,0:T(8,128)S(1)} %select_multiply_fusion, f32[16,16,256]{2,1,0:T(8,128)S(1)} %bitcast_multiply_fusion, f32[]{:T(128)} %bitcast.49, f32[]{:T(128)} %bitcast.48, f32[]{:T(128)} %bitcast.47, f32[]{:T(128)} %bitcast.46, f32[]{:T(128)} %bitcast.45, ...), kind=kLoop, calls=%fused_computation.472 | loop fusion | flops 3276800 | bytes 671812 | tf_op jit(solution)/shard_map/convert_element_type | solution.py:159
  195.6 2.9 %collective-permute-start.7 = (bf16[16,8,256]{2,1,0:T(8,128)(2,1)S(1)}, bf16[16,8,256]{2,1,0:T(8,128)(2,1)S(1)}, u32[]{:S(2)}, u32[]{:S(2)}) collective-permute-start(bf16[16,8,256]{2,1,0:T(8,128)(2,1)S(1)} %get-tuple-element.206), channel_id=1, source_target_pairs={{32,0},{64,32},{96,64},{128,96},{160,128},{192,160},{224,192},{256... | collective-permute-start | bytes 196616 | tf_op jit(solution)/shard_map/ppermute | solution.py:32
  198.6 1.9 collective-permute-done.6
  200.7 12.1 %fusion.79 = (bf16[16,16,256]{2,1,0:T(8,128)(2,1)}, f32[16,16,256]{2,1,0:T(8,128)}) fusion(bf16[16,16,256]{2,1,0:T(8,128)(2,1)S(1)} %copy-done.3, bf16[16,16,256]{2,1,0:T(8,128)(2,1)S(1)} %copy-done.1, f32[16,8,256]{2,1,0:T(8,128)S(1)} %get-tuple-element.194, f32[16,16,256]{2,1,0:T(8,128)S(1)} %get-tuple-element.170, f32[]{:T(128)} %bitcast.49, ...), kind=kLoop, calls=%fused_computation.188 | loop fusion | flops 3932160 | bytes 1179716 | tf_op jit(solution)/shard_map/convert_element_type | solution.py:178
  (90 shorter events, 3.4 us)
Async XLA Ops:
  7.2 4.6 %copy-start.13 = (s32[16,2]{0,1:T(2,128)S(1)}, s32[16,2]{0,1:T(2,128)}, u32[]{:S(2)}) copy-start(s32[16,2]{0,1:T(2,128)} %param.17) | copy-start | bytes 388
  7.2 7.5 %copy-start.18 = (f32[16]{0:T(128)S(1)}, f32[16]{0:T(128)}, u32[]{:S(2)}) copy-start(f32[16]{0:T(128)} %param.15) | copy-start | bytes 196
  7.2 7.5 %copy-start.17 = (s32[16]{0:T(128)S(1)}, s32[16]{0:T(128)}, u32[]{:S(2)}) copy-start(s32[16]{0:T(128)} %param.16) | copy-start | bytes 196
  7.2 47.4 %all-gather.3.cloned.1.call-start = ((), (), s32[]{:S(2)}) async-start(), calls=%async_computation | async-start | bytes 2228224 | tf_op jit(solution)/shard_map/all_gather | solution.py:145
  7.9 146.1 %all-gather.5.cloned.1.call-start = ((), (), s32[]{:S(2)}) async-start(), calls=%async_computation.1 | async-start | bytes 2228224 | tf_op jit(solution)/shard_map/all_gather | solution.py:145
  8.2 46.3 %copy-start.5 = (bf16[256,31]{0,1:T(8,128)(2,1)}, bf16[256,31]{0,1:T(8,128)(2,1)S(1)}, u32[]{:S(2)}) copy-start(bf16[256,31]{0,1:T(8,128)(2,1)S(1)} %get-tuple-element.235) | copy-start | bytes 47620
  66.7 18.4 %copy-start.8 = (pred[16]{0:T(512)(128)(4,1)S(1)}, pred[16]{0:T(512)(128)(4,1)}, u32[]{:S(2)}) copy-start(pred[16]{0:T(512)(128)(4,1)} %get-tuple-element.211) | copy-start | bytes 52
  66.7 18.4 %copy-start.10 = (f32[16]{0:T(128)S(1)}, f32[16]{0:T(128)}, u32[]{:S(2)}) copy-start(f32[16]{0:T(128)} %get-tuple-element.210) | copy-start | bytes 196
  67.8 34.6 %copy-start.7 = (f32[16]{0:T(128)S(1)}, f32[16]{0:T(128)}, u32[]{:S(2)}) copy-start(f32[16]{0:T(128)} %get-tuple-element.171) | copy-start | bytes 196
  67.8 8.2 %collective-permute-start = (f32[16,16,8]{2,1,0:T(8,128)S(1)}, f32[16,16,8]{2,1,0:T(8,128)S(1)}, u32[]{:S(2)}, u32[]{:S(2)}) collective-permute-start(f32[16,16,8]{2,1,0:T(8,128)S(1)} %get-tuple-element.203), channel_id=1, source_target_pairs={{0,1},{1,2},{2,3},{3,4},{4,5},{5,6},{6,7},{7,8},{8,9},{9,10},{10,1... | collective-permute-start | bytes 24584 | tf_op jit(solution)/shard_map/ppermute | solution.py:20
  74.0 10.6 %collective-permute-start.1 = (f32[16,16,8]{2,1,0:T(8,128)S(1)}, f32[16,16,8]{2,1,0:T(8,128)S(1)}, u32[]{:S(2)}, u32[]{:S(2)}) collective-permute-start(f32[16,16,8]{2,1,0:T(8,128)S(1)} %get-tuple-element.204), channel_id=1, source_target_pairs={{1,0},{2,1},{3,2},{4,3},{5,4},{6,5},{7,6},{8,7},{9,8},{10,9},{11,1... | collective-permute-start | bytes 24584 | tf_op jit(solution)/shard_map/ppermute | solution.py:20
  77.7 24.8 %copy-start.2 = (bf16[16,16,256]{2,1,0:T(8,128)(2,1)S(1)}, bf16[16,16,256]{2,1,0:T(8,128)(2,1)}, u32[]{:S(2)}) copy-start(bf16[16,16,256]{2,1,0:T(8,128)(2,1)} %param.13) | copy-start | bytes 393220
  77.7 24.8 %copy-start.4 = (bf16[16,16,256]{2,1,0:T(8,128)(2,1)S(1)}, bf16[16,16,256]{2,1,0:T(8,128)(2,1)}, u32[]{:S(2)}) copy-start(bf16[16,16,256]{2,1,0:T(8,128)(2,1)} %param.12) | copy-start | bytes 393220
  97.4 56.6 %copy-start.6 = (bf16[256,31]{0,1:T(8,128)(2,1)S(1)}, bf16[256,31]{0,1:T(8,128)(2,1)}, u32[]{:S(2)}) copy-start(bf16[256,31]{0,1:T(8,128)(2,1)} %copy-done.5) | copy-start | bytes 47620
  97.5 4.9 %collective-permute-start.2 = (bf16[16,8,256]{2,1,0:T(8,128)(2,1)S(1)}, bf16[16,8,256]{2,1,0:T(8,128)(2,1)S(1)}, u32[]{:S(2)}, u32[]{:S(2)}) collective-permute-start(bf16[16,8,256]{2,1,0:T(8,128)(2,1)S(1)} %get-tuple-element.207), channel_id=1, source_target_pairs={{0,32},{32,64},{64,96},{96,128},{128,160},{160,192},{192,224},{224... | collective-permute-start | bytes 196616 | tf_op jit(solution)/shard_map/ppermute | solution.py:30
  97.5 4.9 %collective-permute-start.3 = (bf16[16,8,256]{2,1,0:T(8,128)(2,1)S(1)}, bf16[16,8,256]{2,1,0:T(8,128)(2,1)S(1)}, u32[]{:S(2)}, u32[]{:S(2)}) collective-permute-start(bf16[16,8,256]{2,1,0:T(8,128)(2,1)S(1)} %get-tuple-element.208), channel_id=1, source_target_pairs={{32,0},{64,32},{96,64},{128,96},{160,128},{192,160},{224,192},{256... | collective-permute-start | bytes 196616 | tf_op jit(solution)/shard_map/ppermute | solution.py:32
  100.5 56.0 %copy-start.15 = (f32[16]{0:T(128)}, f32[16]{0:T(128)S(1)}, u32[]{:S(2)}) copy-start(f32[16]{0:T(128)S(1)} %add_convert_fusion.2) | copy-start | bytes 196
  113.9 0.7 copy-start
  156.5 1.4 copy-start.12
  158.0 8.2 %copy-start.14 = (f32[16]{0:T(128)S(1)}, f32[16]{0:T(128)}, u32[]{:S(2)}) copy-start(f32[16]{0:T(128)} %compare_select_fusion.2) | copy-start | bytes 196
  158.0 18.1 %copy-start.9 = (pred[16]{0:T(512)(128)(4,1)S(1)}, pred[16]{0:T(512)(128)(4,1)}, u32[]{:S(2)}) copy-start(pred[16]{0:T(512)(128)(4,1)} %get-tuple-element.175) | copy-start | bytes 52
  158.0 18.1 %copy-start.11 = (f32[16]{0:T(128)S(1)}, f32[16]{0:T(128)}, u32[]{:S(2)}) copy-start(f32[16]{0:T(128)} %get-tuple-element.209) | copy-start | bytes 196
  167.3 33.2 %copy-start.16 = (f32[16]{0:T(128)S(1)}, f32[16]{0:T(128)}, u32[]{:S(2)}) copy-start(f32[16]{0:T(128)} %copy-done.15) | copy-start | bytes 196
  167.3 7.9 %collective-permute-start.4 = (f32[16,16,8]{2,1,0:T(8,128)S(1)}, f32[16,16,8]{2,1,0:T(8,128)S(1)}, u32[]{:S(2)}, u32[]{:S(2)}) collective-permute-start(f32[16,16,8]{2,1,0:T(8,128)S(1)} %get-tuple-element.197), channel_id=1, source_target_pairs={{0,1},{1,2},{2,3},{3,4},{4,5},{5,6},{6,7},{7,8},{8,9},{9,10},{10,1... | collective-permute-start | bytes 24584 | tf_op jit(solution)/shard_map/ppermute | solution.py:20
  172.1 10.6 %collective-permute-start.5 = (f32[16,16,8]{2,1,0:T(8,128)S(1)}, f32[16,16,8]{2,1,0:T(8,128)S(1)}, u32[]{:S(2)}, u32[]{:S(2)}) collective-permute-start(f32[16,16,8]{2,1,0:T(8,128)S(1)} %get-tuple-element.198), channel_id=1, source_target_pairs={{1,0},{2,1},{3,2},{4,3},{5,4},{6,5},{7,6},{8,7},{9,8},{10,9},{11,1... | collective-permute-start | bytes 24584 | tf_op jit(solution)/shard_map/ppermute | solution.py:20
  176.2 24.5 %copy-start.1 = (bf16[16,16,256]{2,1,0:T(8,128)(2,1)S(1)}, bf16[16,16,256]{2,1,0:T(8,128)(2,1)}, u32[]{:S(2)}) copy-start(bf16[16,16,256]{2,1,0:T(8,128)(2,1)} %copy-done) | copy-start | bytes 393220
  176.2 24.5 %copy-start.3 = (bf16[16,16,256]{2,1,0:T(8,128)(2,1)S(1)}, bf16[16,16,256]{2,1,0:T(8,128)(2,1)}, u32[]{:S(2)}) copy-start(bf16[16,16,256]{2,1,0:T(8,128)(2,1)} %param.13) | copy-start | bytes 393220
  195.6 4.9 %collective-permute-start.6 = (bf16[16,8,256]{2,1,0:T(8,128)(2,1)S(1)}, bf16[16,8,256]{2,1,0:T(8,128)(2,1)S(1)}, u32[]{:S(2)}, u32[]{:S(2)}) collective-permute-start(bf16[16,8,256]{2,1,0:T(8,128)(2,1)S(1)} %get-tuple-element.205), channel_id=1, source_target_pairs={{0,32},{32,64},{64,96},{96,128},{128,160},{160,192},{192,224},{224... | collective-permute-start | bytes 196616 | tf_op jit(solution)/shard_map/ppermute | solution.py:30
  195.6 4.9 %collective-permute-start.7 = (bf16[16,8,256]{2,1,0:T(8,128)(2,1)S(1)}, bf16[16,8,256]{2,1,0:T(8,128)(2,1)S(1)}, u32[]{:S(2)}, u32[]{:S(2)}) collective-permute-start(bf16[16,8,256]{2,1,0:T(8,128)(2,1)S(1)} %get-tuple-element.206), channel_id=1, source_target_pairs={{32,0},{64,32},{96,64},{128,96},{160,128},{192,160},{224,192},{256... | collective-permute-start | bytes 196616 | tf_op jit(solution)/shard_map/ppermute | solution.py:32
Sparse Core Ops, SparseCore 0:
  10.2 44.3 all-gather.2
  115.4 38.5 all-gather.4
where the time goes:
time: 221 us; the launch traced here: 220 us
  waiting for transfers between devices  95.7 us (43%)
  other arithmetic  63.5 us (29%)
  starting transfers between devices  19.5 us (9%)
  matrix products  15.4 us (7%)
  between operations  14.6 us (7%)
  local copies, waits for them, and re-layouts  10.8 us (5%)
    all_gather x2, waiting for transfers between devices, body(): whole_tiles = lax.all_gather(work_tiles, 'segment', axis=1, tiled=True)  76.7 us
    convert_element_type x2, other arithmetic, body(): horiz_blur.astype(jnp.bfloat16)  24.4 us
    convert_element_type x2, other arithmetic, body(): mask_now = (mask_now.astype(jnp.float32) + STEP_GAIN * (tile_target_image...  23.5 us
    ppermute x4, waiting for transfers between devices, passed_along(): return lax.ppermute(block, axis, route)  14.4 us
    ppermute x4, starting transfers between devices, passed_along(): return lax.ppermute(block, axis, route)  13.5 us
    dot_general x4, matrix products, one_block(): jnp.einsum('nkrb,by->nkry', field_a, inverse_cols, preferred_element_type...  10.4 us
    ppermute x2, starting transfers between devices, with_halo(): lax.ppermute(head, axis, [((i + 1) % count, i) for i in range(count)])  5.89 us
    dot_general x2, matrix products, spectrum_part(): jnp.einsum('ra,nrb->nab', rows_table, y_part, preferred_element_type=jnp....  5.01 us
  transfers between devices with their start and end apart: 10, of which 7 were waited for; matrix products, arithmetic and copies ran while one was open for 6% of the time, Pallas kernels for 0%

commit v1 on v0

v1 whole, which is shorter than its diff:
```python
import functools
import math

import jax
import jax.numpy as jnp
import ml_dtypes
import numpy as np
from jax import lax
from jax.experimental import pallas as pl
from jax.experimental.pallas import tpu as pltpu
from jax.sharding import PartitionSpec as P

EDGE = 256
KF = 31
NK = 12
RB = 8
ITERS = 2
SLOTS = 16
USED = 12
GROUPS = USED // 4
ROWS = 16
EXT = ROWS + 2 * RB
COARSE = 64
STEEPNESS = 1.5
THRESHOLD = 2.0
STEP_GAIN = 0.5
BF = jnp.bfloat16
F32 = jnp.float32


def bf16(x):
    return np.asarray(x, np.float32).astype(ml_dtypes.bfloat16)


def high_low(x):
    high = bf16(x)
    return high, bf16(np.asarray(x, np.float32) - high.astype(np.float32))


@functools.cache
def tables():
    freq = np.arange(32) - KF // 2
    live = (np.arange(32) < KF).astype(np.float64)

    def waves(position):
        angle = 2.0 * np.pi * ((np.asarray(position)[:, None] * freq[None, :]) % EDGE) / EDGE
        return np.cos(angle) * live, np.sin(angle) * live

    cos, sin = waves(np.arange(EDGE))
    t = {}
    t["cols"] = bf16(np.concatenate([np.tile(cos, (1, 4)), np.tile(-sin, (1, 4))], 1) / 16.0)
    t["rows"] = bf16(np.concatenate([cos, sin], 1).T / 16.0)
    ext_cos, ext_sin = waves((np.arange(EDGE + 2 * RB) - RB) % EDGE)
    t["ext"] = bf16(np.concatenate([ext_cos, ext_sin], 1))
    c_cos, c_sin = waves(np.arange(COARSE) * (EDGE // COARSE))
    inv = np.zeros((256, 512))
    for i in range(4):
        r, c = slice(32 * i, 32 * i + 32), 128 * i
        inv[r, c : c + 64] = c_cos.T
        inv[r, c + 64 : c + 128] = c_sin.T
        r = slice(128 + 32 * i, 128 + 32 * i + 32)
        inv[r, c : c + 64] = -c_sin.T
        inv[r, c + 64 : c + 128] = c_cos.T
    t["inv"] = bf16(inv)
    d = np.arange(EDGE)[None, :] - (EDGE // COARSE) * np.arange(COARSE)[:, None]
    interp = np.ones((COARSE, EDGE))
    for m in range(1, 32):
        interp += 2.0 * np.cos(2.0 * np.pi * m * d / EDGE)
    interp /= COARSE
    taps = np.exp(-(np.arange(-RB, RB + 1.0) ** 2) / (2.0 * (RB / 2.0) ** 2))
    taps /= taps.sum()
    blur = np.zeros((EDGE, EDGE))
    for a in range(EDGE):
        for b in range(max(0, a - RB), min(EDGE, a + RB + 1)):
            blur[a, b] = taps[a - b + RB]
    across = interp @ blur
    high, low = high_low(np.concatenate([across, across], 0))
    t["across"] = np.concatenate([high, low], 0)
    down = np.zeros((ROWS, EXT))
    for r in range(ROWS):
        down[r, r : r + 2 * RB + 1] = taps
    t["down"] = np.concatenate(high_low(down), 0)
    left = np.tile(np.concatenate([interp[:, :RB]] * 2, 0), (1, 16))
    right = np.tile(np.concatenate([interp[:, -RB:]] * 2, 0), (1, 16))
    t["band"] = bf16(np.concatenate([left, right], 1))
    w_left, w_right = np.zeros((RB, RB)), np.zeros((RB, RB))
    for c in range(RB):
        for q in range(RB):
            if c >= q:
                w_left[c, q] = taps[c - q]
            if c <= q:
                w_right[c, q] = taps[2 * RB + c - q]
    t["reach"] = np.concatenate([np.tile(w_left, (16, 16)), np.tile(w_right, (16, 16))], 1).astype(
        np.float32
    )
    return t


def dot(a, b):
    return jnp.dot(a, b, preferred_element_type=F32)


def lane_block(width, size):
    return lax.broadcasted_iota(jnp.int32, (1, width), 1) // size


def put_column_transform(mask, cols_ref, y_ref):
    both = dot(mask.reshape(USED * ROWS, EDGE), cols_ref[...])
    place = lane_block(256, 32) % 4
    for j in range(GROUPS):
        total = jnp.zeros((ROWS, 256), F32)
        for i in range(4):
            first = (4 * j + i) * ROWS
            total = jnp.where(place == i, both[first : first + ROWS], total)
        total = total.astype(BF)
        y_ref[:, 128 * j : 128 * (j + 1)] = total[:, :128]
        y_ref[:, 384 + 128 * j : 384 + 128 * (j + 1)] = total[:, 128:]


def start_kernel(mask_ref, spectra_ref, cols_ref, reach_ref, dose_ref, row_ref, side_ref,
                 y_ref, kernels_ref, slot_ref, small_ref, pick_ref):
    put_column_transform(mask_ref[:USED], cols_ref, y_ref)
    kernels_ref[...] = jnp.zeros_like(kernels_ref)
    for k in range(NK):
        for part in range(2):
            kernels_ref[k, part, :KF, :KF] = spectra_ref[k, part]
    for k in range(NK):
        for part in range(2):
            one = kernels_ref[k, part]
            one = one + pltpu.roll(one, 32, 1)
            kernels_ref[k, part] = one + pltpu.roll(one, 64, 1)
    wide, narrow = lane_block(128 * USED, 128), lane_block(128, RB)
    weight = jnp.zeros((1, 128 * USED), F32)
    up_wide, down_wide = weight, weight
    up_narrow = jnp.zeros((1, 128), F32)
    down_narrow = up_narrow
    left = jnp.full((1, 128), -1, jnp.int32)
    right = left
    for g in range(USED):
        row = row_ref[g]
        scale = jnp.where(row >= 0, dose_ref[g], 0.0) * (1.0 / (NK * KF * KF))
        weight = jnp.where(wide == g, scale, weight)
        if g > 0:
            before = row_ref[g - 1]
            joined = jnp.where((before >= 0) & (row >= 0) & (before == row - 1), 1.0, 0.0)
            up_wide = jnp.where(wide == g, joined, up_wide)
            down_wide = jnp.where(wide == g - 1, joined, down_wide)
            up_narrow = jnp.where(narrow == g, joined, up_narrow)
            down_narrow = jnp.where(narrow == g - 1, joined, down_narrow)
        left = jnp.where(narrow == g, side_ref[g, 0], left)
        right = jnp.where(narrow == g, side_ref[g, 1], right)
    slot_ref[...] = jnp.concatenate([weight, up_wide, down_wide, jnp.zeros((5, 128 * USED), F32)], 0)
    small_ref[...] = jnp.concatenate([up_narrow, down_narrow, jnp.zeros((6, 128), F32)], 0)
    source = lax.broadcasted_iota(jnp.int32, (128, 1), 0) // RB
    wanted = jnp.concatenate([left, right], 1)
    pick_ref[...] = jnp.where(source == wanted, reach_ref[...], 0.0).astype(BF)


def field_kernel(all_ref, rows_ref, kernels_ref, ext_ref, inv_ref, band_ref, slot_ref,
                 coarse_ref, to_left_ref, to_right_ref, held):
    first = pl.multiple_of(lax.axis_index("segment") * ROWS, ROWS)
    ext = ext_ref[pl.ds(first, EXT), :]
    inner = dot(rows_ref[...], all_ref[...])
    half = 32 * USED
    real = inner[:32, :half] + inner[32:, half:]
    imag = inner[:32, half:] - inner[32:, :half]
    place = lane_block(256, RB) % 16
    bands = jnp.zeros((EXT, 256), F32)
    for j in range(GROUPS):
        re, im = real[:, 128 * j : 128 * (j + 1)], imag[:, 128 * j : 128 * (j + 1)]
        for k in range(NK):
            k_re, k_im = kernels_ref[k, 0], kernels_ref[k, 1]
            p_re = k_re * re - k_im * im
            p_im = k_re * im + k_im * re
            block = jnp.concatenate(
                [jnp.concatenate([p_re, p_im], 1), jnp.concatenate([-p_im, p_re], 1)], 0
            ).astype(BF)
            held[j, k * EXT : (k + 1) * EXT, :] = dot(ext, block).astype(BF)
        field = dot(held[j], inv_ref[...])
        squares = jnp.sum((field * field).reshape(NK, EXT, 512), axis=0)
        squares = squares * slot_ref[0:1, 512 * j : 512 * (j + 1)]
        coarse_ref[:, 512 * j : 512 * (j + 1)] = squares
        low = squares.astype(BF)
        stack = jnp.concatenate([low[:, 128 * i : 128 * (i + 1)] for i in range(4)], 0)
        edges = dot(stack, band_ref[...])
        for i in range(4):
            bands = jnp.where(place == 4 * j + i, edges[EXT * i : EXT * (i + 1)], bands)
    to_left_ref[...] = bands[:, :128].astype(BF)
    to_right_ref[...] = bands[:, 128:].astype(BF)


def joined_rows(cells, up, down, step):
    segment = lax.axis_index("segment")
    top, middle, bottom = cells[:RB], cells[RB : RB + ROWS], cells[RB + ROWS :]
    top = jnp.where(segment == 0, pltpu.roll(top, step, 1) * up, top)
    width = cells.shape[1]
    bottom = jnp.where(
        segment == lax.axis_size("segment") - 1, pltpu.roll(bottom, width - step, 1) * down, bottom
    )
    return jnp.concatenate([top, middle, bottom], 0)


def blur_down(cells, down_ref):
    both = dot(down_ref[...], cells.astype(BF))
    return both[:ROWS] + both[ROWS:]


def blur_kernel(coarse_ref, slot_ref, down_ref, across_ref, inner_ref):
    cells = joined_rows(coarse_ref[...], slot_ref[1:2, :], slot_ref[2:3, :], 128)
    low = blur_down(cells, down_ref).astype(BF)
    stack = jnp.concatenate([low[:, 128 * g : 128 * (g + 1)] for g in range(USED)], 0)
    inner_ref[...] = dot(jnp.concatenate([stack, stack], 1), across_ref[...])


def update_kernel(last, inner_ref, from_left_ref, from_right_ref, pick_ref, small_ref, down_ref, cols_ref,
                  mask_ref, target_ref, new_ref, out_ref):
    up, down = small_ref[0:1, :], small_ref[1:2, :]
    lane = lax.broadcasted_iota(jnp.int32, (1, 128), 1)
    left = dot(from_left_ref[...], pick_ref[:, :128])
    right = dot(from_right_ref[...], pick_ref[:, 128:])
    left = blur_down(joined_rows(left, up, down, RB), down_ref)
    right = blur_down(joined_rows(right, up, down, RB), down_ref)
    for g in range(SLOTS):
        if g < USED:
            blurred = inner_ref[ROWS * g : ROWS * (g + 1), :]
            add_left = jnp.where(lane < RB, pltpu.roll(left, (128 - RB * g) % 128, 1), 0.0)
            add_right = jnp.where(lane >= 128 - RB, pltpu.roll(right, 128 - RB - RB * g, 1), 0.0)
            blurred = blurred + jnp.concatenate([add_left, add_right], 1)
        else:
            blurred = jnp.zeros((ROWS, EDGE), F32)
        resist = jax.nn.sigmoid(STEEPNESS * (blurred - THRESHOLD))
        if last:
            out_ref[g] = resist
        step = STEP_GAIN * (target_ref[g].astype(F32) - resist)
        new_ref[g] = (mask_ref[g].astype(F32) + step).astype(BF)
    if not last:
        put_column_transform(new_ref[:USED], cols_ref, out_ref)


VMEM = pl.BlockSpec(memory_space=pltpu.VMEM)
SMEM = pl.BlockSpec(memory_space=pltpu.SMEM)


def call(kernel, ins, outs, flops, scratch=(), name=None):
    size = sum(math.prod(o.shape) * o.dtype.itemsize for o in outs)
    return pl.pallas_call(
        kernel,
        out_shape=tuple(outs),
        in_specs=list(ins),
        out_specs=tuple(VMEM for _ in outs),
        scratch_shapes=list(scratch),
        compiler_params=pltpu.CompilerParams(vmem_limit_bytes=32 * 2**20),
        cost_estimate=pl.CostEstimate(flops=flops, bytes_accessed=2 * size, transcendentals=0),
        name=name,
    )


def passed_along(block, distance):
    devices = range(lax.axis_size("tile"))
    route = [(i - distance, i) for i in devices if i - distance in devices]
    return lax.ppermute(block, "tile", route)


def body(mask, target, spectra, dose, slot_row, side_source):
    t = {name: jnp.asarray(value) for name, value in tables().items()}
    shape = jax.ShapeDtypeStruct
    y_shape = shape((ROWS, 64 * USED), BF)
    y, kernels, slot, small, pick = call(
        start_kernel,
        [VMEM, VMEM, VMEM, VMEM, SMEM, SMEM, SMEM],
        [y_shape, shape((NK, 2, 32, 128), F32), shape((8, 128 * USED), F32), shape((8, 128), F32), shape((128, 256), BF)],
        10**8,
        name="start",
    )(mask, spectra, t["cols"], t["reach"], dose, slot_row, side_source)
    for sweep in range(ITERS):
        last = sweep == ITERS - 1
        rows_all = lax.all_gather(y, "segment", axis=0, tiled=True)
        coarse, to_left, to_right = call(
            field_kernel,
            [VMEM] * 7,
            [shape((EXT, 128 * USED), F32), shape((EXT, 128), BF), shape((EXT, 128), BF)],
            10**9,
            [pltpu.VMEM((GROUPS, NK * EXT, 256), BF)],
            name="fields",
        )(rows_all, t["rows"], kernels, t["ext"], t["inv"], t["band"], slot)
        from_left = passed_along(to_right, 1)
        from_right = passed_along(to_left, -1)
        (inner,) = call(
            blur_kernel, [VMEM] * 4, [shape((USED * ROWS, EDGE), F32)], 10**9, name="blur"
        )(coarse, slot, t["down"], t["across"])
        out = shape((SLOTS, ROWS, EDGE), F32) if last else y_shape
        mask, result = call(
            functools.partial(update_kernel, last),
            [VMEM] * 9,
            [shape((SLOTS, ROWS, EDGE), BF), out],
            10**8,
            name="update",
        )(inner, from_left, from_right, pick, small, t["down"], t["cols"], mask, target)
        y = result
    return mask, result


def solution(mesh):
    in_specs = (
        P("tile", "segment", None),
        P("tile", "segment", None),
        P(),
        P("tile"),
        P("tile"),
        P("tile", None),
    )
    out_specs = (P("tile", "segment", None), P("tile", "segment", None))
    return jax.shard_map(body, mesh=mesh, in_specs=in_specs, out_specs=out_specs, check_vma=False)
```

time: 221 us -> 69 us (0.31)
  waiting for transfers between devices: 95.7 us -> 11.2 us
  other arithmetic: 63.5 us -> 0 us
  blocking collectives: 0 us -> 34.8 us
  matrix products: 15.4 us -> 0 us
  between operations: 14.6 us -> 0.84 us
  local copies, waits for them, and re-layouts: 10.8 us -> 1.91 us
  Pallas kernels: 0 us -> 6.8 us
  starting transfers between devices: 19.5 us -> 13.2 us
    all_gather x2 -> x0, waiting for transfers between devices: 76.7 us -> none  [body(): whole_tiles = lax.all_gather(work_tiles, 'segment', axis=1, tiled=True)]
    convert_element_type x12 -> x0, other arithmetic: 51.1 us -> none  [the longest x2 24.4 us: body(): horiz_blur.astype(jnp.bfloat16)]
    all_gather x0 -> x2, blocking collectives: none -> 34.8 us  [body(): rows_all = lax.all_gather(y, 'segment', axis=0, tiled=True)]
    dot_general x6 -> x0, matrix products: 15.4 us -> none  [the longest x4 10.4 us: one_block(): jnp.einsum('nkrb,by->nkry', field_a, inverse_cols, preferred_element_type...]
    ppermute x8 -> x4, waiting for transfers between devices: 18.2 us -> 11.2 us  [passed_along(): return lax.ppermute(block, 'tile', route)]
    pallas_call x0 -> x7, Pallas kernels: none -> 6.8 us  [the longest x2 2.88 us: body(): call(field_kernel, [VMEM] * 7, [shape((EXT, 128 * USED), F32), shape((EXT...]
    ppermute x8 -> x4, starting transfers between devices: 19.4 us -> 13.2 us  [passed_along(): return lax.ppermute(block, 'tile', route)]
    mul x7 -> x0, other arithmetic: 3.66 us -> none  [the longest x2 2.07 us: body(): intensity = intensity * weight[:, None, None]]
  transfers between devices with their start and end apart: 10 -> 4, of which waited for: 7 -> 2; matrix products, arithmetic and copies ran while one was open for 6% -> 0% of each run, Pallas kernels for 0% -> 1%
where the time goes in v1:
time: 69 us; the launch traced here: 68.8 us
  blocking collectives  34.8 us (50%)
  starting transfers between devices  13.2 us (19%)
  waiting for transfers between devices  11.2 us (16%)
  Pallas kernels  6.8 us (10%)
  local copies, waits for them, and re-layouts  1.91 us (3%)
  between operations  0.84 us (1%)
    all_gather x2, blocking collectives, body(): rows_all = lax.all_gather(y, 'segment', axis=0, tiled=True)  34.8 us
    ppermute x4, starting transfers between devices, passed_along(): return lax.ppermute(block, 'tile', route)  13.2 us
    ppermute x4, waiting for transfers between devices, passed_along(): return lax.ppermute(block, 'tile', route)  11.2 us
    pallas_call x2, Pallas kernels, body(): call(field_kernel, [VMEM] * 7, [shape((EXT, 128 * USED), F32), shape((EXT...  2.88 us
    unnamed x26, local copies, waits for them, and re-layouts  1.91 us
    pallas_call x2, Pallas kernels, body(): call(functools.partial(update_kernel, last), [VMEM] * 9, [shape((SLOTS, R...  1.8 us
    pallas_call x1, Pallas kernels, body(): call(start_kernel, [VMEM, VMEM, VMEM, VMEM, SMEM, SMEM, SMEM], [y_shape,...  1.51 us
  transfers between devices with their start and end apart: 4, of which 2 were waited for; matrix products, arithmetic and copies ran while one was open for 0% of the time, Pallas kernels for 1%

profile of v1, /device:TPU:198, one launch (start us, length us, event | category | flops | bytes accessed | tf_op | source)
XLA Modules:
  0.0 68.8 jit_solution(6793605336427065456)
XLA Ops:
  0.6 0.8 %copy.17.side_ref = s32[16,2]{1,0:T(8,128)S(1)} copy(s32[16,2]{0,1:T(2,128)} %param.19) | data formatting | bytes 256 | tf_op args[5]
  1.4 0.0 copy-start
  1.4 0.0 copy-start.1
  1.4 0.0 copy-start.3
  1.4 0.0 copy-start.5
  1.4 0.0 copy-start.6
  1.4 1.1 %copy.16.spectra_ref = f32[12,2,31,31]{3,2,1,0:T(8,128)S(1)} copy(f32[12,2,31,31]{3,1,2,0:T(2,128)} %param.16) | data formatting | bytes 184512 | tf_op args[2]
  2.5 0.0 copy-done
  2.5 0.0 copy-done.1
  2.5 0.0 copy-done.3
  2.5 0.0 copy-done.5
  2.5 0.0 copy-done.6
  2.6 0.0 copy-start.11
  2.6 1.5 %start.1 = (bf16[16,768]{1,0:T(8,128)(2,1)S(1)}, f32[12,2,32,128]{3,2,1,0:T(8,128)S(1)}, f32[8,1536]{1,0:T(8,128)S(1)}, f32[8,128]{1,0:T(8,128)S(1)}, bf16[128,256]{1,0:T(8,128)(2,1)S(1)}) custom-call(bf16[16,16,256]{2,1,0:T(8,128)(2,1)S(1)} %copy-done.1, f32[12,2,31,31]{3,2,1,0:T(8,128)S(1)} %copy.16.spectra_ref, bf16[256,256]{1,0:T(8,128)(2,1)S(1)} %copy-done, ...), custom_call_target="tpu_custom_call" | custom-call | flops 100000000 | bytes 1073152 | tf_op jit(solution)/shard_map/start/pallas_call | solution.py:268
  4.1 0.0 copy-start.7
  4.1 0.0 copy-start.9
  4.1 0.0 copy-start.10
  4.1 18.8 %all_gather.6.all_ref = bf16[256,768]{1,0:T(8,128)(2,1)S(1)} all-gather(bf16[16,768]{1,0:T(8,128)(2,1)S(1)} %get-tuple-element.15), channel_id=1, replica_groups=mesh['segment'=16,'tile'=32] {'segment'}, dimensions={0}, use_global_device_ids=true | all-gather | bytes 417792 | tf_op jit(solution)/shard_map/all_gather | solution.py:277
  22.9 0.0 copy-done.11
  22.9 0.0 copy-done.7
  22.9 0.0 copy-done.9
  22.9 0.0 copy-done.10
  22.9 0.0 copy-start.4
  22.9 0.0 copy-start.8
  23.0 1.4 %fields.2 = (f32[32,1536]{1,0:T(8,128)S(1)}, bf16[32,128]{1,0:T(8,128)(2,1)S(1)}, bf16[32,128]{1,0:T(8,128)(2,1)S(1)}) custom-call(bf16[256,768]{1,0:T(8,128)(2,1)S(1)} %all_gather.6.all_ref, bf16[64,256]{1,0:T(8,128)(2,1)S(1)} %copy-done.11, f32[12,2,32,128]{3,2,1,0:T(8,128)S(1)} %get-tuple-element.16.kernels_ref, bf16[272,64]{1,0:T(8,128)(2,1)S(1)} %copy-done.9, ...), custom_call_target="tpu_custom_call" | custom-call | flops 1000000000 | bytes 425984 | tf_op jit(solution)/shard_map/fields/pallas_call | solution.py:278
  24.4 5.4 %collective-permute-start = (bf16[32,128]{1,0:T(8,128)(2,1)S(1)}, bf16[32,128]{1,0:T(8,128)(2,1)S(1)}, u32[]{:S(2)}, u32[]{:S(2)}) collective-permute-start(bf16[32,128]{1,0:T(8,128)(2,1)S(1)} %get-tuple-element.19), channel_id=1, source_target_pairs={{0,1},{1,2},{2,3},{3,4},{4,5},{5,6},{6,7},{7,8},{8,9},{9,10},{10,1... | collective-permute-start | bytes 24584 | tf_op jit(solution)/shard_map/ppermute | solution.py:261
  29.8 1.9 %collective-permute-start.1 = (bf16[32,128]{1,0:T(8,128)(2,1)S(1)}, bf16[32,128]{1,0:T(8,128)(2,1)S(1)}, u32[]{:S(2)}, u32[]{:S(2)}) collective-permute-start(bf16[32,128]{1,0:T(8,128)(2,1)S(1)} %get-tuple-element.20), channel_id=1, source_target_pairs={{1,0},{2,1},{3,2},{4,3},{5,4},{6,5},{7,6},{8,7},{9,8},{10,9},{11,1... | collective-permute-start | bytes 24584 | tf_op jit(solution)/shard_map/ppermute | solution.py:261
  31.7 0.0 copy-done.4
  31.8 0.0 copy-done.8
  31.8 0.0 copy-start.2
  31.8 0.3 blur.2.inner_ref
  32.1 0.0 collective-permute-done.from_left_ref
  32.1 6.6 %collective-permute-done.1.from_right_ref = bf16[32,128]{1,0:T(8,128)(2,1)S(1)} collective-permute-done((bf16[32,128]{1,0:T(8,128)(2,1)S(1)}, bf16[32,128]{1,0:T(8,128)(2,1)S(1)}, u32[]{:S(2)}, u32[]{:S(2)}) %collective-permute-start.1) | collective-permute-done | bytes 8224 | tf_op jit(solution)/shard_map/ppermute | solution.py:261
  38.7 0.0 copy-done.2
  38.7 0.6 update.2
  39.3 16.0 %all_gather.7.all_ref = bf16[256,768]{1,0:T(8,128)(2,1)S(1)} all-gather(bf16[16,768]{1,0:T(8,128)(2,1)S(1)} %get-tuple-element.23), channel_id=1, replica_groups=mesh['segment'=16,'tile'=32] {'segment'}, dimensions={0}, use_global_device_ids=true | all-gather | bytes 417792 | tf_op jit(solution)/shard_map/all_gather | solution.py:277
  55.3 1.4 %fields.3 = (f32[32,1536]{1,0:T(8,128)S(1)}, bf16[32,128]{1,0:T(8,128)(2,1)S(1)}, bf16[32,128]{1,0:T(8,128)(2,1)S(1)}) custom-call(bf16[256,768]{1,0:T(8,128)(2,1)S(1)} %all_gather.7.all_ref, bf16[64,256]{1,0:T(8,128)(2,1)S(1)} %copy-done.11, f32[12,2,32,128]{3,2,1,0:T(8,128)S(1)} %get-tuple-element.16.kernels_ref, bf16[272,64]{1,0:T(8,128)(2,1)S(1)} %copy-done.9, ...), custom_call_target="tpu_custom_call" | custom-call | flops 1000000000 | bytes 425984 | tf_op jit(solution)/shard_map/fields/pallas_call | solution.py:278
  56.7 1.9 %collective-permute-start.2 = (bf16[32,128]{1,0:T(8,128)(2,1)S(1)}, bf16[32,128]{1,0:T(8,128)(2,1)S(1)}, u32[]{:S(2)}, u32[]{:S(2)}) collective-permute-start(bf16[32,128]{1,0:T(8,128)(2,1)S(1)} %get-tuple-element.25), channel_id=1, source_target_pairs={{0,1},{1,2},{2,3},{3,4},{4,5},{5,6},{6,7},{7,8},{8,9},{9,10},{10,1... | collective-permute-start | bytes 24584 | tf_op jit(solution)/shard_map/ppermute | solution.py:261
  58.7 3.9 %collective-permute-start.3 = (bf16[32,128]{1,0:T(8,128)(2,1)S(1)}, bf16[32,128]{1,0:T(8,128)(2,1)S(1)}, u32[]{:S(2)}, u32[]{:S(2)}) collective-permute-start(bf16[32,128]{1,0:T(8,128)(2,1)S(1)} %get-tuple-element.26), channel_id=1, source_target_pairs={{1,0},{2,1},{3,2},{4,3},{5,4},{6,5},{7,6},{8,7},{9,8},{10,9},{11,1... | collective-permute-start | bytes 24584 | tf_op jit(solution)/shard_map/ppermute | solution.py:261
  62.6 0.3 blur.3.inner_ref
  62.9 0.0 collective-permute-done.2.from_left_ref
  62.9 4.6 %collective-permute-done.3.from_right_ref = bf16[32,128]{1,0:T(8,128)(2,1)S(1)} collective-permute-done((bf16[32,128]{1,0:T(8,128)(2,1)S(1)}, bf16[32,128]{1,0:T(8,128)(2,1)S(1)}, u32[]{:S(2)}, u32[]{:S(2)}) %collective-permute-start.3) | collective-permute-done | bytes 8224 | tf_op jit(solution)/shard_map/ppermute | solution.py:261
  67.5 1.2 %update.3 = (bf16[16,16,256]{2,1,0:T(8,128)(2,1)}, f32[16,16,256]{2,1,0:T(8,128)}) custom-call(f32[192,256]{1,0:T(8,128)S(1)} %blur.3.inner_ref, bf16[32,128]{1,0:T(8,128)(2,1)S(1)} %collective-permute-done.2.from_left_ref, bf16[32,128]{1,0:T(8,128)(2,1)S(1)} %collective-permute-done.3.from_right_ref, bf16[128,256]{1,0:T(8,128)(2,1)S(1)} %get-tuple-element.21.pick_ref, ...), custom_call_target="tpu_custom_call" | custom-call | flops 100000000 | bytes 786432 | tf_op jit(solution)/shard_map/update/pallas_call | solution.py:292
Async XLA Ops:
  1.4 1.1 %copy-start = (bf16[256,256]{1,0:T(8,128)(2,1)S(1)}, bf16[256,256]{1,0:T(8,128)(2,1)}, u32[]{:S(2)}) copy-start(bf16[256,256]{1,0:T(8,128)(2,1)} %constant.16.clone.cols_ref) | copy-start | bytes 393220
  1.4 1.1 %copy-start.1 = (bf16[16,16,256]{2,1,0:T(8,128)(2,1)S(1)}, bf16[16,16,256]{2,1,0:T(8,128)(2,1)}, u32[]{:S(2)}) copy-start(bf16[16,16,256]{2,1,0:T(8,128)(2,1)} %mask_ref.3) | copy-start | bytes 393220
  1.4 1.1 %copy-start.3 = (f32[128,256]{1,0:T(8,128)S(1)}, f32[128,256]{1,0:T(8,128)}, u32[]{:S(2)}) copy-start(f32[128,256]{1,0:T(8,128)} %constant.23.clone.reach_ref) | copy-start | bytes 393220
  1.4 1.1 %copy-start.5 = (f32[16]{0:T(128)S(1)}, f32[16]{0:T(128)}, u32[]{:S(2)}) copy-start(f32[16]{0:T(128)} %dose_ref.1) | copy-start | bytes 196
  1.4 1.1 %copy-start.6 = (s32[16]{0:T(128)S(1)}, s32[16]{0:T(128)}, u32[]{:S(2)}) copy-start(s32[16]{0:T(128)} %row_ref.1) | copy-start | bytes 196
  2.6 20.4 %copy-start.11 = (bf16[64,256]{1,0:T(8,128)(2,1)S(1)}, bf16[64,256]{1,0:T(8,128)(2,1)}, u32[]{:S(2)}) copy-start(bf16[64,256]{1,0:T(8,128)(2,1)} %constant.17.clone.rows_ref) | copy-start | bytes 98308
  4.1 18.8 %copy-start.7 = (bf16[256,512]{1,0:T(8,128)(2,1)S(1)}, bf16[256,512]{1,0:T(8,128)(2,1)}, u32[]{:S(2)}) copy-start(bf16[256,512]{1,0:T(8,128)(2,1)} %constant.19.clone.inv_ref) | copy-start | bytes 786436
  4.1 18.8 %copy-start.9 = (bf16[272,64]{1,0:T(8,128)(2,1)S(1)}, bf16[272,64]{1,0:T(8,128)(2,1)}, u32[]{:S(2)}) copy-start(bf16[272,64]{1,0:T(8,128)(2,1)} %constant.18.clone.ext_ref) | copy-start | bytes 104452
  4.1 18.8 %copy-start.10 = (bf16[128,256]{1,0:T(8,128)(2,1)S(1)}, bf16[128,256]{1,0:T(8,128)(2,1)}, u32[]{:S(2)}) copy-start(bf16[128,256]{1,0:T(8,128)(2,1)} %constant.22.clone.band_ref) | copy-start | bytes 196612
  22.9 8.8 %copy-start.4 = (bf16[32,32]{1,0:T(8,128)(2,1)S(1)}, bf16[32,32]{1,0:T(8,128)(2,1)}, u32[]{:S(2)}) copy-start(bf16[32,32]{1,0:T(8,128)(2,1)} %constant.21.clone.down_ref) | copy-start | bytes 6148
  22.9 8.8 %copy-start.8 = (bf16[256,256]{1,0:T(8,128)(2,1)S(1)}, bf16[256,256]{1,0:T(8,128)(2,1)}, u32[]{:S(2)}) copy-start(bf16[256,256]{1,0:T(8,128)(2,1)} %constant.20.clone.across_ref) | copy-start | bytes 393220
  24.4 7.7 %collective-permute-start = (bf16[32,128]{1,0:T(8,128)(2,1)S(1)}, bf16[32,128]{1,0:T(8,128)(2,1)S(1)}, u32[]{:S(2)}, u32[]{:S(2)}) collective-permute-start(bf16[32,128]{1,0:T(8,128)(2,1)S(1)} %get-tuple-element.19), channel_id=1, source_target_pairs={{0,1},{1,2},{2,3},{3,4},{4,5},{5,6},{6,7},{7,8},{8,9},{9,10},{10,1... | collective-permute-start | bytes 24584 | tf_op jit(solution)/shard_map/ppermute | solution.py:261
  29.8 8.9 %collective-permute-start.1 = (bf16[32,128]{1,0:T(8,128)(2,1)S(1)}, bf16[32,128]{1,0:T(8,128)(2,1)S(1)}, u32[]{:S(2)}, u32[]{:S(2)}) collective-permute-start(bf16[32,128]{1,0:T(8,128)(2,1)S(1)} %get-tuple-element.20), channel_id=1, source_target_pairs={{1,0},{2,1},{3,2},{4,3},{5,4},{6,5},{7,6},{8,7},{9,8},{10,9},{11,1... | collective-permute-start | bytes 24584 | tf_op jit(solution)/shard_map/ppermute | solution.py:261
  31.8 6.9 %copy-start.2 = (bf16[16,16,256]{2,1,0:T(8,128)(2,1)S(1)}, bf16[16,16,256]{2,1,0:T(8,128)(2,1)}, u32[]{:S(2)}) copy-start(bf16[16,16,256]{2,1,0:T(8,128)(2,1)} %target_ref.3) | copy-start | bytes 393220
  56.7 6.2 %collective-permute-start.2 = (bf16[32,128]{1,0:T(8,128)(2,1)S(1)}, bf16[32,128]{1,0:T(8,128)(2,1)S(1)}, u32[]{:S(2)}, u32[]{:S(2)}) collective-permute-start(bf16[32,128]{1,0:T(8,128)(2,1)S(1)} %get-tuple-element.25), channel_id=1, source_target_pairs={{0,1},{1,2},{2,3},{3,4},{4,5},{5,6},{6,7},{7,8},{8,9},{9,10},{10,1... | collective-permute-start | bytes 24584 | tf_op jit(solution)/shard_map/ppermute | solution.py:261
  58.7 8.9 %collective-permute-start.3 = (bf16[32,128]{1,0:T(8,128)(2,1)S(1)}, bf16[32,128]{1,0:T(8,128)(2,1)S(1)}, u32[]{:S(2)}, u32[]{:S(2)}) collective-permute-start(bf16[32,128]{1,0:T(8,128)(2,1)S(1)} %get-tuple-element.26), channel_id=1, source_target_pairs={{1,0},{2,1},{3,2},{4,3},{5,4},{6,5},{7,6},{8,7},{9,8},{10,9},{11,1... | collective-permute-start | bytes 24584 | tf_op jit(solution)/shard_map/ppermute | solution.py:261

commit v2 on v1

v2 whole, which is shorter than its diff:
```python
import functools
import math

import jax
import jax.numpy as jnp
import ml_dtypes
import numpy as np
from jax import lax
from jax.experimental import pallas as pl
from jax.experimental.pallas import tpu as pltpu
from jax.sharding import PartitionSpec as P

EDGE = 256
KF = 31
NK = 12
RB = 8
SLOTS = 16
USED = 12
GROUPS = USED // 4
ROWS = 16
EXT = ROWS + 2 * RB
COARSE = 64
STEEPNESS = 1.5
THRESHOLD = 2.0
STEP_GAIN = 0.5
BF = jnp.bfloat16
F32 = jnp.float32


def bf16(x):
    return np.asarray(x, np.float32).astype(ml_dtypes.bfloat16)


def high_low(x):
    high = bf16(x)
    return high, bf16(np.asarray(x, np.float32) - high.astype(np.float32))


@functools.cache
def tables():
    freq = np.arange(32) - KF // 2
    live = (np.arange(32) < KF).astype(np.float64)

    def waves(position):
        angle = 2.0 * np.pi * ((np.asarray(position)[:, None] * freq[None, :]) % EDGE) / EDGE
        return np.cos(angle) * live, np.sin(angle) * live

    cos, sin = waves(np.arange(EDGE))
    t = {}
    t["cols"] = bf16(np.concatenate([np.tile(cos, (1, 4)), np.tile(-sin, (1, 4))], 1) / 16.0)
    t["rows"] = bf16(np.concatenate([cos, sin], 1).T / 16.0)
    ext_cos, ext_sin = waves((np.arange(EDGE + 2 * RB) - RB) % EDGE)
    t["ext"] = bf16(np.concatenate([ext_cos, ext_sin], 1))
    c_cos, c_sin = waves(np.arange(COARSE) * (EDGE // COARSE))
    t["grid"] = bf16(np.concatenate([c_cos, c_sin], 1))
    inv = np.zeros((256, 512))
    for i in range(4):
        r, c = slice(32 * i, 32 * i + 32), 128 * i
        inv[r, c : c + 64] = c_cos.T
        inv[r, c + 64 : c + 128] = c_sin.T
        r = slice(128 + 32 * i, 128 + 32 * i + 32)
        inv[r, c : c + 64] = -c_sin.T
        inv[r, c + 64 : c + 128] = c_cos.T
    t["inv"] = bf16(inv)
    d = np.arange(EDGE)[None, :] - (EDGE // COARSE) * np.arange(COARSE)[:, None]
    interp = np.ones((COARSE, EDGE))
    for m in range(1, 32):
        interp += 2.0 * np.cos(2.0 * np.pi * m * d / EDGE)
    interp /= COARSE
    taps = np.exp(-(np.arange(-RB, RB + 1.0) ** 2) / (2.0 * (RB / 2.0) ** 2))
    taps /= taps.sum()
    blur = np.zeros((EDGE, EDGE))
    above = np.zeros((EDGE, EDGE))
    below = np.zeros((EDGE, EDGE))
    for b in range(EDGE):
        for step in range(-RB, RB + 1):
            a = b + step
            (above if a < 0 else below if a >= EDGE else blur)[a % EDGE, b] += taps[step + RB]
    across = np.zeros((128, EDGE))
    across[:COARSE] = interp @ blur
    across[COARSE : COARSE + RB] = above[EDGE - RB :]
    across[COARSE + RB : COARSE + 2 * RB] = below[:RB]
    t["across"] = np.concatenate(high_low(across), 0)
    main_high, main_low = high_low((interp @ blur).T)
    t["tall"] = np.concatenate(
        [main_high, bf16((interp @ above).T), bf16((interp @ below).T), main_low], 1
    )
    down = np.zeros((ROWS, EXT))
    for r in range(ROWS):
        down[r, r : r + 2 * RB + 1] = taps
    t["down"] = np.concatenate(high_low(down), 0)
    band = np.zeros((128, 256))
    band[:COARSE, :128] = np.tile(interp[:, :RB], (1, 16))
    band[:COARSE, 128:] = np.tile(interp[:, -RB:], (1, 16))
    t["band"] = bf16(band)
    return t


def dot(a, b):
    return jnp.dot(a, b, preferred_element_type=F32)


def lane_block(width, size):
    return lax.broadcasted_iota(jnp.int32, (1, width), 1) // size


def four_slots(blocks, place):
    total = blocks[0]
    for i in range(1, 4):
        total = jnp.where(place == i, blocks[i], total)
    return total


def start_kernel(mask_ref, target_ref, spectra_ref, cols_ref, dose_ref, row_ref, side_ref,
                 y_ref, kernels_ref, slot_ref, pick_ref):
    of_mask = dot(mask_ref[:USED].reshape(USED * ROWS, EDGE), cols_ref[...])
    of_target = dot(target_ref[:USED].reshape(USED * ROWS, EDGE), cols_ref[...])
    place = lane_block(256, 32) % 4
    for n, both in enumerate((of_mask, of_mask + STEP_GAIN * of_target)):
        for j in range(GROUPS):
            firsts = [(4 * j + i) * ROWS for i in range(4)]
            total = four_slots([both[f : f + ROWS] for f in firsts], place).astype(BF)
            lane = 768 * n + 128 * j
            y_ref[:, lane : lane + 128] = total[:, :128]
            y_ref[:, lane + 384 : lane + 512] = total[:, 128:]
    kernels_ref[...] = jnp.zeros_like(kernels_ref)
    for k in range(NK):
        for part in range(2):
            kernels_ref[k, part, :KF, :KF] = spectra_ref[pl.ds(2 * KF * k + part, KF, stride=2), :]
    for k in range(NK):
        for part in range(2):
            one = kernels_ref[k, part]
            one = one + pltpu.roll(one, 32, 1)
            kernels_ref[k, part] = one + pltpu.roll(one, 64, 1)
    wide, narrow = lane_block(128 * USED, 128), lane_block(256, 2 * RB)
    weight = jnp.zeros((1, 128 * USED), F32)
    up, down = weight, weight
    wanted = jnp.full((1, 256), -1, jnp.int32)
    is_left = lane_block(256, RB) % 2 == 0
    for g in range(USED):
        row = row_ref[g]
        scale = jnp.where(row >= 0, dose_ref[g], 0.0) * (1.0 / (NK * KF * KF))
        weight = jnp.where(wide == g, scale, weight)
        if g > 0:
            before = row_ref[g - 1]
            joined = jnp.where((before >= 0) & (row >= 0) & (before == row - 1), 1.0, 0.0)
            up = jnp.where(wide == g, joined, up)
            down = jnp.where(wide == g - 1, joined, down)
        wanted = jnp.where(narrow == g, jnp.where(is_left, side_ref[0, g], side_ref[1, g]), wanted)
    slot_ref[...] = jnp.concatenate([weight, up, down, jnp.zeros((5, 128 * USED), F32)], 0)
    here = lax.broadcasted_iota(jnp.int32, (256, 1), 0)
    lane = lax.broadcasted_iota(jnp.int32, (1, 256), 1)
    match = ((here % 128) // RB == wanted) & (here % RB == lane % RB) & ((here < 128) == is_left)
    pick_ref[...] = jnp.where(match, 1.0, 0.0).astype(BF)


def intensities(inner, kernels_ref, points, inv_ref, band_ref, slot_ref, held, coarse_ref, to_left_ref, to_right_ref):
    count = points.shape[0]
    place = lane_block(256, RB) % 16
    bands = jnp.zeros((count, 256), F32)
    for j in range(GROUPS):
        total = inner(j)
        re = total[:32, :128] + total[32:, 128:]
        im = total[:32, 128:] - total[32:, :128]
        for k in range(NK):
            k_re, k_im = kernels_ref[k, 0], kernels_ref[k, 1]
            p_re = k_re * re - k_im * im
            p_im = k_re * im + k_im * re
            block = jnp.concatenate(
                [jnp.concatenate([p_re, p_im], 1), jnp.concatenate([-p_im, p_re], 1)], 0
            ).astype(BF)
            held[j, k * count : (k + 1) * count, :] = dot(points, block).astype(BF)
        field = dot(held[j], inv_ref[...])
        squares = jnp.sum((field * field).reshape(NK, count, 512), axis=0)
        squares = squares * slot_ref[0:1, 512 * j : 512 * (j + 1)]
        parts = [squares[:, 128 * i : 128 * (i + 1)] for i in range(4)]
        parts = [(part + pltpu.roll(part, COARSE, 1)).astype(BF) for part in parts]
        for i in range(4):
            first = 128 * (4 * j + i)
            coarse_ref[:, first : first + 128] = parts[i]
        edges = dot(jnp.concatenate(parts, 0), band_ref[...])
        for i in range(4):
            bands = jnp.where(place == 4 * j + i, edges[count * i : count * (i + 1)], bands)
    to_left_ref[...] = bands[:, :128].astype(BF)
    to_right_ref[...] = bands[:, 128:].astype(BF)


def field_kernel(all_ref, rows_ref, kernels_ref, grid_ref, inv_ref, band_ref, slot_ref,
                 coarse_ref, to_left_ref, to_right_ref, base_ref, held):
    inner = dot(rows_ref[...], all_ref[...])
    base_ref[...] = inner[:, 768:]
    half = 32 * USED

    def group(j):
        return jnp.concatenate(
            [inner[:, 128 * j : 128 * (j + 1)], inner[:, half + 128 * j : half + 128 * (j + 1)]], 1
        )

    intensities(group, kernels_ref, grid_ref[...], inv_ref, band_ref, slot_ref, held,
                coarse_ref, to_left_ref, to_right_ref)


def side_lanes(from_left_ref, from_right_ref, pick_ref):
    received = jnp.concatenate([from_left_ref[...], from_right_ref[...]], 1)
    picked = dot(received, pick_ref[...])
    lane = lax.broadcasted_iota(jnp.int32, (1, 128), 1)
    inside = (lane >= COARSE) & (lane < COARSE + 2 * RB)
    parts = []
    for g in range(USED):
        part = picked[:, 128 * (g // 8) : 128 * (g // 8) + 128]
        part = pltpu.roll(part, (COARSE - 2 * RB * (g % 8)) % 128, 1)
        parts.append(jnp.where(inside, part, 0.0))
    return jnp.concatenate(parts, 1)


def own_lanes(coarse):
    return jnp.where(lax.broadcasted_iota(jnp.int32, (1, 128 * USED), 1) % 128 < COARSE, coarse, 0.0)


def middle_kernel(coarse_ref, from_left_ref, from_right_ref, pick_ref, slot_ref, tall_ref, across_ref,
                  rows_ref, cols_ref, base_ref, kernels_ref, ext_ref, inv_ref, band_ref,
                  mine_ref, next_ref, to_left_ref, to_right_ref, blurred, turned, held):
    cells = own_lanes(coarse_ref[...].astype(F32)) + side_lanes(from_left_ref, from_right_ref, pick_ref)
    above = pltpu.roll(cells, 128, 1) * slot_ref[1:2, :]
    below = pltpu.roll(cells, 128 * (USED - 1), 1) * slot_ref[2:3, :]
    main = cells.astype(BF)
    blurred[...] = dot(tall_ref[...], jnp.concatenate([main, above.astype(BF), below.astype(BF), main], 0)).astype(BF)
    first = pl.multiple_of(lax.axis_index("segment") * ROWS, ROWS)
    mine_ref[...] = blurred[pl.ds(first, ROWS), :]
    for g in range(USED):
        one = blurred[:, 128 * g : 128 * (g + 1)]
        fine = dot(jnp.concatenate([one, one], 1), across_ref[...])
        resist = resist_of(fine).astype(BF)
        turned[64 * g : 64 * (g + 1), :] = dot(rows_ref[...], resist).astype(BF)
    both = dot(turned[...], cols_ref[...])
    place = lane_block(256, 32) % 4
    half = 32 * USED

    def group(j):
        total = four_slots([both[64 * (4 * j + i) : 64 * (4 * j + i + 1)] for i in range(4)], place)
        base = jnp.concatenate(
            [base_ref[:, 128 * j : 128 * (j + 1)], base_ref[:, half + 128 * j : half + 128 * (j + 1)]], 1
        )
        return base - STEP_GAIN * total

    ext = ext_ref[pl.ds(first, EXT), :]
    intensities(group, kernels_ref, ext, inv_ref, band_ref, slot_ref, held, next_ref, to_left_ref, to_right_ref)


def resist_of(blurred):
    return 0.5 * jnp.tanh((0.5 * STEEPNESS) * (blurred - THRESHOLD)) + 0.5


def stacked(low):
    stack = jnp.concatenate([low[:, 128 * g : 128 * (g + 1)] for g in range(USED)], 0)
    return jnp.concatenate([stack, stack], 1)


def blur_rows(cells, slot_ref, down_ref):
    segment = lax.axis_index("segment")
    top, center, bottom = cells[:RB], cells[RB : RB + ROWS], cells[RB + ROWS :]
    top = jnp.where(segment == 0, pltpu.roll(top, 128, 1) * slot_ref[1:2, :], top)
    bottom = jnp.where(
        segment == lax.axis_size("segment") - 1,
        pltpu.roll(bottom, 128 * (USED - 1), 1) * slot_ref[2:3, :],
        bottom,
    )
    both = dot(down_ref[...], jnp.concatenate([top, center, bottom], 0).astype(BF))
    return (both[:ROWS] + both[ROWS:]).astype(BF)


def local_kernel(mine_ref, coarse_ref, slot_ref, down_ref, across_ref, mask_ref, target_ref, inner_ref, once_ref):
    resist = resist_of(dot(stacked(mine_ref[...]), across_ref[...]))
    for g in range(SLOTS):
        part = resist[ROWS * g : ROWS * (g + 1)] if g < USED else resist_of(jnp.zeros((ROWS, EDGE), F32))
        once_ref[g] = (mask_ref[g].astype(F32) + STEP_GAIN * (target_ref[g].astype(F32) - part)).astype(BF)
    cells = own_lanes(coarse_ref[...].astype(F32))
    inner_ref[...] = dot(stacked(blur_rows(cells, slot_ref, down_ref)), across_ref[...])


def final_kernel(inner_ref, from_left_ref, from_right_ref, pick_ref, slot_ref, down_ref, across_ref,
                 once_ref, target_ref, mask_ref, resist_ref):
    sides = blur_rows(side_lanes(from_left_ref, from_right_ref, pick_ref), slot_ref, down_ref)
    blurred = inner_ref[...] + dot(stacked(sides), across_ref[...])
    for g in range(SLOTS):
        part = resist_of(blurred[ROWS * g : ROWS * (g + 1)] if g < USED else jnp.zeros((ROWS, EDGE), F32))
        resist_ref[g] = part
        mask_ref[g] = (once_ref[g].astype(F32) + STEP_GAIN * (target_ref[g].astype(F32) - part)).astype(BF)


VMEM = pl.BlockSpec(memory_space=pltpu.VMEM)
SMEM = pl.BlockSpec(memory_space=pltpu.SMEM)


def call(kernel, ins, outs, flops, scratch=(), name=None):
    size = sum(math.prod(o.shape) * o.dtype.itemsize for o in outs)
    return pl.pallas_call(
        kernel,
        out_shape=tuple(outs),
        in_specs=list(ins),
        out_specs=tuple(VMEM for _ in outs),
        scratch_shapes=list(scratch),
        compiler_params=pltpu.CompilerParams(vmem_limit_bytes=32 * 2**20),
        cost_estimate=pl.CostEstimate(flops=flops, bytes_accessed=2 * size, transcendentals=0),
        name=name,
    )


def passed_along(block, distance):
    devices = range(lax.axis_size("tile"))
    route = [(i - distance, i) for i in devices if i - distance in devices]
    return lax.ppermute(block, "tile", route)


def body(mask, target, spectra, dose, slot_row, side_source):
    t = {name: jnp.asarray(value) for name, value in tables().items()}
    shape = jax.ShapeDtypeStruct
    plane = spectra.transpose(0, 2, 1, 3).reshape(NK * KF * 2, KF)
    y, kernels, slot, pick = call(
        start_kernel,
        [VMEM] * 4 + [SMEM] * 3,
        [
            shape((ROWS, 128 * USED), BF),
            shape((NK, 2, 32, 128), F32),
            shape((8, 128 * USED), F32),
            shape((256, 256), BF),
        ],
        10**8,
        name="start",
    )(mask, target, plane, t["cols"], dose, slot_row, side_source.T)
    rows_all = lax.all_gather(y, "segment", axis=0, tiled=True)
    coarse, to_left, to_right, base = call(
        field_kernel,
        [VMEM] * 7,
        [
            shape((COARSE, 128 * USED), BF),
            shape((COARSE, 128), BF),
            shape((COARSE, 128), BF),
            shape((64, 64 * USED), F32),
        ],
        10**9,
        [pltpu.VMEM((GROUPS, NK * COARSE, 256), BF)],
        name="fields",
    )(rows_all, t["rows"], kernels, t["grid"], t["inv"], t["band"], slot)
    from_left = passed_along(to_right, 1)
    from_right = passed_along(to_left, -1)
    mine, coarse, to_left, to_right = call(
        middle_kernel,
        [VMEM] * 14,
        [
            shape((ROWS, 128 * USED), BF),
            shape((EXT, 128 * USED), BF),
            shape((EXT, 128), BF),
            shape((EXT, 128), BF),
        ],
        10**9,
        [
            pltpu.VMEM((EDGE, 128 * USED), BF),
            pltpu.VMEM((64 * USED, EDGE), BF),
            pltpu.VMEM((GROUPS, NK * EXT, 256), BF),
        ],
        name="middle",
    )(coarse, from_left, from_right, pick, slot, t["tall"], t["across"], t["rows"], t["cols"], base,
      kernels, t["ext"], t["inv"], t["band"])
    from_left = passed_along(to_right, 1)
    from_right = passed_along(to_left, -1)
    inner, once = call(
        local_kernel,
        [VMEM] * 7,
        [shape((USED * ROWS, EDGE), F32), shape((SLOTS, ROWS, EDGE), BF)],
        10**9,
        name="local",
    )(mine, coarse, slot, t["down"], t["across"], mask, target)
    return call(
        final_kernel,
        [VMEM] * 9,
        [shape((SLOTS, ROWS, EDGE), BF), shape((SLOTS, ROWS, EDGE), F32)],
        10**8,
        name="final",
    )(inner, from_left, from_right, pick, slot, t["down"], t["across"], once, target)


def solution(mesh):
    in_specs = (
        P("tile", "segment", None),
        P("tile", "segment", None),
        P(),
        P("tile"),
        P("tile"),
        P("tile", None),
    )
    out_specs = (P("tile", "segment", None), P("tile", "segment", None))
    return jax.shard_map(body, mesh=mesh, in_specs=in_specs, out_specs=out_specs, check_vma=False)
```

time: 69 us -> 60.3 us (0.87)
  blocking collectives: 34.8 us -> 19.9 us
  Pallas kernels: 6.8 us -> 9.99 us
  local copies, waits for them, and re-layouts: 1.91 us -> 4.45 us
    all_gather x2 -> x1, blocking collectives: 34.8 us -> 19.9 us  [body(): rows_all = lax.all_gather(y, 'segment', axis=0, tiled=True)]
    pallas_call x7 -> x5, Pallas kernels: 6.8 us -> 9.99 us  [the longest x1 4.88 us: body(): call(middle_kernel, [VMEM] * 14, [shape((ROWS, 128 * USED), BF), shape((E...]
    unnamed x26 -> x36, local copies, waits for them, and re-layouts: 1.91 us -> 4.45 us
where the time goes in v2:
time: 60.3 us; the launch traced here: 59.9 us
  blocking collectives  19.9 us (33%)
  starting transfers between devices  13.2 us (22%)
  waiting for transfers between devices  11.6 us (19%)
  Pallas kernels  9.99 us (17%)
  local copies, waits for them, and re-layouts  4.45 us (7%)
  between operations  0.86 us (1%)
    all_gather x1, blocking collectives, body(): rows_all = lax.all_gather(y, 'segment', axis=0, tiled=True)  19.9 us
    ppermute x4, starting transfers between devices, passed_along(): return lax.ppermute(block, 'tile', route)  13.2 us
    ppermute x4, waiting for transfers between devices, passed_along(): return lax.ppermute(block, 'tile', route)  11.6 us
    pallas_call x1, Pallas kernels, body(): call(middle_kernel, [VMEM] * 14, [shape((ROWS, 128 * USED), BF), shape((E...  4.88 us
    unnamed x36, local copies, waits for them, and re-layouts  4.45 us
    pallas_call x1, Pallas kernels, body(): call(field_kernel, [VMEM] * 7, [shape((COARSE, 128 * USED), BF), shape((C...  2.05 us
    pallas_call x1, Pallas kernels, body(): call(start_kernel, [VMEM] * 4 + [SMEM] * 3, [shape((ROWS, 128 * USED), BF...  1.43 us
    pallas_call x1, Pallas kernels, body(): call(final_kernel, [VMEM] * 9, [shape((SLOTS, ROWS, EDGE), BF), shape((SL...  1.3 us
  transfers between devices with their start and end apart: 4, of which 2 were waited for; matrix products, arithmetic and copies ran while one was open for 0% of the time, Pallas kernels for 1%

profile of v2, /device:TPU:198, one launch (start us, length us, event | category | flops | bytes accessed | tf_op | source)
XLA Modules:
  0.0 59.9 jit_solution(6727334647735495490)
XLA Ops:
  0.6 0.0 copy-start.11
  0.6 0.0 copy-start.9
  0.7 0.0 copy-start.10
  0.7 0.6 %copy-done.11 = s32[16]{0:T(128)S(1)} copy-done((s32[16]{0:T(128)S(1)}, s32[16]{0:T(128)}, u32[]{:S(2)}) %copy-start.11) | copy-done | bytes 88
  1.3 0.0 copy-done.9
  1.3 0.0 copy-done.10
  1.3 0.0 copy-start
  1.3 0.9 %copy-done = bf16[16,16,256]{2,1,0:T(8,128)(2,1)S(1)} copy-done((bf16[16,16,256]{2,1,0:T(8,128)(2,1)S(1)}, bf16[16,16,256]{2,1,0:T(8,128)(2,1)}, u32[]{:S(2)}) %copy-start) | copy-done | bytes 131096
  2.2 0.0 copy-start.2
  2.2 1.0 %copy-done.2 = f32[12,2,31,31]{3,1,2,0:T(2,128)S(1)} copy-done((f32[12,2,31,31]{3,1,2,0:T(2,128)S(1)}, f32[12,2,31,31]{3,1,2,0:T(2,128)}, u32[]{:S(2)}) %copy-start.2) | copy-done | bytes 92280
  3.2 0.0 copy-start.4
  3.2 0.9 %copy-done.4 = bf16[16,16,256]{2,1,0:T(8,128)(2,1)S(1)} copy-done((bf16[16,16,256]{2,1,0:T(8,128)(2,1)S(1)}, bf16[16,16,256]{2,1,0:T(8,128)(2,1)}, u32[]{:S(2)}) %copy-start.4) | copy-done | bytes 131096
  4.1 0.0 copy-start.6
  4.1 0.9 %copy-done.6 = bf16[256,256]{1,0:T(8,128)(2,1)S(1)} copy-done((bf16[256,256]{1,0:T(8,128)(2,1)S(1)}, bf16[256,256]{1,0:T(8,128)(2,1)}, u32[]{:S(2)}) %copy-start.6) | copy-done | bytes 131096
  5.0 1.4 %start.1 = (bf16[16,1536]{1,0:T(8,128)(2,1)S(1)}, f32[12,2,32,128]{3,2,1,0:T(8,128)S(1)}, f32[8,1536]{1,0:T(8,128)S(1)}, bf16[256,256]{1,0:T(8,128)(2,1)S(1)}) custom-call(bf16[16,16,256]{2,1,0:T(8,128)(2,1)S(1)} %copy-done.4, bf16[16,16,256]{2,1,0:T(8,128)(2,1)S(1)} %copy-done, f32[744,31]{1,0:T(8,128)S(1)} %bitcast.4, bf16[256,256]{1,0:T(8,128)(2,1)S(1)} %copy-done.6, ...), custom_call_target="tpu_custom_call" | custom-call | flops 100000000 | bytes 1245184 | tf_op jit(solution)/shard_map/start/pallas_call | solution.py:319
  6.5 0.0 copy-start.12
  6.5 0.0 copy-start.15
  6.5 0.0 copy-start.16
  6.5 0.0 copy-start.17
  6.5 19.9 %all_gather.3.all_ref = bf16[256,1536]{1,0:T(8,128)(2,1)S(1)} all-gather(bf16[16,1536]{1,0:T(8,128)(2,1)S(1)} %get-tuple-element.16), channel_id=1, replica_groups=mesh['segment'=16,'tile'=32] {'segment'}, dimensions={0}, use_global_device_ids=true | all-gather | bytes 835584 | tf_op jit(solution)/shard_map/all_gather | solution.py:331
  26.4 0.0 copy-done.12
  26.4 0.0 copy-done.15
  26.4 0.0 copy-done.16
  26.4 0.0 copy-done.17
  26.4 0.0 copy-start.3
  26.4 0.0 copy-start.7
  26.4 0.0 copy-start.13
  26.5 0.0 copy-start.14
  26.5 2.0 %fields.1 = (bf16[64,1536]{1,0:T(8,128)(2,1)S(1)}, bf16[64,128]{1,0:T(8,128)(2,1)S(1)}, bf16[64,128]{1,0:T(8,128)(2,1)S(1)}, f32[64,768]{1,0:T(8,128)S(1)}) custom-call(bf16[256,1536]{1,0:T(8,128)(2,1)S(1)} %all_gather.3.all_ref, bf16[64,256]{1,0:T(8,128)(2,1)S(1)} %copy-done.16, f32[12,2,32,128]{3,2,1,0:T(8,128)S(1)} %get-tuple-element.17.kernels_ref, ...), custom_call_target="tpu_custom_call" | custom-call | flops 1000000000 | bytes 851968 | tf_op jit(solution)/shard_map/fields/pallas_call | solution.py:332
  28.5 5.4 %collective-permute-start = (bf16[64,128]{1,0:T(8,128)(2,1)S(1)}, bf16[64,128]{1,0:T(8,128)(2,1)S(1)}, u32[]{:S(2)}, u32[]{:S(2)}) collective-permute-start(bf16[64,128]{1,0:T(8,128)(2,1)S(1)} %get-tuple-element.20), channel_id=1, source_target_pairs={{0,1},{1,2},{2,3},{3,4},{4,5},{5,6},{6,7},{7,8},{8,9},{9,10},{10,1... | collective-permute-start | bytes 49160 | tf_op jit(solution)/shard_map/ppermute | solution.py:312
  34.0 1.9 %collective-permute-start.1 = (bf16[64,128]{1,0:T(8,128)(2,1)S(1)}, bf16[64,128]{1,0:T(8,128)(2,1)S(1)}, u32[]{:S(2)}, u32[]{:S(2)}) collective-permute-start(bf16[64,128]{1,0:T(8,128)(2,1)S(1)} %get-tuple-element.21), channel_id=1, source_target_pairs={{1,0},{2,1},{3,2},{4,3},{5,4},{6,5},{7,6},{8,7},{9,8},{10,9},{11,1... | collective-permute-start | bytes 49160 | tf_op jit(solution)/shard_map/ppermute | solution.py:312
  35.9 0.0 collective-permute-done.from_left_ref
  35.9 7.0 %collective-permute-done.1.from_right_ref = bf16[64,128]{1,0:T(8,128)(2,1)S(1)} collective-permute-done((bf16[64,128]{1,0:T(8,128)(2,1)S(1)}, bf16[64,128]{1,0:T(8,128)(2,1)S(1)}, u32[]{:S(2)}, u32[]{:S(2)}) %collective-permute-start.1) | collective-permute-done | bytes 16416 | tf_op jit(solution)/shard_map/ppermute | solution.py:312
  42.9 0.0 copy-done.3
  42.9 0.0 copy-done.7
  42.9 0.0 copy-done.13
  42.9 0.0 copy-done.14
  42.9 0.0 copy-start.1
  42.9 0.0 copy-start.5
  43.0 0.0 copy-start.8
  43.0 4.9 %middle.1 = (bf16[16,1536]{1,0:T(8,128)(2,1)S(1)}, bf16[32,1536]{1,0:T(8,128)(2,1)S(1)}, bf16[32,128]{1,0:T(8,128)(2,1)S(1)}, bf16[32,128]{1,0:T(8,128)(2,1)S(1)}) custom-call(bf16[64,1536]{1,0:T(8,128)(2,1)S(1)} %get-tuple-element.19.coarse_ref, bf16[64,128]{1,0:T(8,128)(2,1)S(1)} %collective-permute-done.from_left_ref, ...), custom_call_target="tpu_custom_call" | custom-call | flops 1000000000 | bytes 327680 | tf_op jit(solution)/shard_map/middle/pallas_call | solution.py:347
  47.9 1.9 %collective-permute-start.2 = (bf16[32,128]{1,0:T(8,128)(2,1)S(1)}, bf16[32,128]{1,0:T(8,128)(2,1)S(1)}, u32[]{:S(2)}, u32[]{:S(2)}) collective-permute-start(bf16[32,128]{1,0:T(8,128)(2,1)S(1)} %get-tuple-element.27), channel_id=1, source_target_pairs={{0,1},{1,2},{2,3},{3,4},{4,5},{5,6},{6,7},{7,8},{8,9},{9,10},{10,1... | collective-permute-start | bytes 24584 | tf_op jit(solution)/shard_map/ppermute | solution.py:312
  49.8 3.9 %collective-permute-start.3 = (bf16[32,128]{1,0:T(8,128)(2,1)S(1)}, bf16[32,128]{1,0:T(8,128)(2,1)S(1)}, u32[]{:S(2)}, u32[]{:S(2)}) collective-permute-start(bf16[32,128]{1,0:T(8,128)(2,1)S(1)} %get-tuple-element.28), channel_id=1, source_target_pairs={{1,0},{2,1},{3,2},{4,3},{5,4},{6,5},{7,6},{8,7},{9,8},{10,9},{11,1... | collective-permute-start | bytes 24584 | tf_op jit(solution)/shard_map/ppermute | solution.py:312
  53.7 0.0 copy-done.1
  53.7 0.0 copy-done.5
  53.7 0.0 copy-done.8
  53.7 0.3 local.1
  54.1 0.0 collective-permute-done.2.from_left_ref
  54.1 4.6 %collective-permute-done.3.from_right_ref = bf16[32,128]{1,0:T(8,128)(2,1)S(1)} collective-permute-done((bf16[32,128]{1,0:T(8,128)(2,1)S(1)}, bf16[32,128]{1,0:T(8,128)(2,1)S(1)}, u32[]{:S(2)}, u32[]{:S(2)}) %collective-permute-start.3) | collective-permute-done | bytes 8224 | tf_op jit(solution)/shard_map/ppermute | solution.py:312
  58.6 1.3 %final.1 = (bf16[16,16,256]{2,1,0:T(8,128)(2,1)}, f32[16,16,256]{2,1,0:T(8,128)}) custom-call(f32[192,256]{1,0:T(8,128)S(1)} %get-tuple-element.26.inner_ref, bf16[32,128]{1,0:T(8,128)(2,1)S(1)} %collective-permute-done.2.from_left_ref, bf16[32,128]{1,0:T(8,128)(2,1)S(1)} %collective-permute-done.3.from_right_ref, ...), custom_call_target="tpu_custom_call" | custom-call | flops 100000000 | bytes 786432 | tf_op jit(solution)/shard_map/final/pallas_call | solution.py:374
Async XLA Ops:
  0.6 0.7 %copy-start.11 = (s32[16]{0:T(128)S(1)}, s32[16]{0:T(128)}, u32[]{:S(2)}) copy-start(s32[16]{0:T(128)} %row_ref.1) | copy-start | bytes 196
  0.6 0.7 %copy-start.9 = (s32[16,2]{0,1:T(2,128)S(1)}, s32[16,2]{0,1:T(2,128)}, u32[]{:S(2)}) copy-start(s32[16,2]{0,1:T(2,128)} %param.20) | copy-start | bytes 388
  0.7 0.7 %copy-start.10 = (f32[16]{0:T(128)S(1)}, f32[16]{0:T(128)}, u32[]{:S(2)}) copy-start(f32[16]{0:T(128)} %dose_ref.1) | copy-start | bytes 196
  1.3 0.9 %copy-start = (bf16[16,16,256]{2,1,0:T(8,128)(2,1)S(1)}, bf16[16,16,256]{2,1,0:T(8,128)(2,1)}, u32[]{:S(2)}) copy-start(bf16[16,16,256]{2,1,0:T(8,128)(2,1)} %target_ref.5) | copy-start | bytes 393220
  2.2 1.0 %copy-start.2 = (f32[12,2,31,31]{3,1,2,0:T(2,128)S(1)}, f32[12,2,31,31]{3,1,2,0:T(2,128)}, u32[]{:S(2)}) copy-start(f32[12,2,31,31]{3,1,2,0:T(2,128)} %param.17) | copy-start | bytes 276772
  3.2 0.9 %copy-start.4 = (bf16[16,16,256]{2,1,0:T(8,128)(2,1)S(1)}, bf16[16,16,256]{2,1,0:T(8,128)(2,1)}, u32[]{:S(2)}) copy-start(bf16[16,16,256]{2,1,0:T(8,128)(2,1)} %mask_ref.3) | copy-start | bytes 393220
  4.1 0.9 %copy-start.6 = (bf16[256,256]{1,0:T(8,128)(2,1)S(1)}, bf16[256,256]{1,0:T(8,128)(2,1)}, u32[]{:S(2)}) copy-start(bf16[256,256]{1,0:T(8,128)(2,1)} %constant.18.clone.cols_ref) | copy-start | bytes 393220
  6.5 19.9 %copy-start.12 = (bf16[256,512]{1,0:T(8,128)(2,1)S(1)}, bf16[256,512]{1,0:T(8,128)(2,1)}, u32[]{:S(2)}) copy-start(bf16[256,512]{1,0:T(8,128)(2,1)} %constant.22.clone.inv_ref) | copy-start | bytes 786436
  6.5 19.9 %copy-start.15 = (bf16[128,256]{1,0:T(8,128)(2,1)S(1)}, bf16[128,256]{1,0:T(8,128)(2,1)}, u32[]{:S(2)}) copy-start(bf16[128,256]{1,0:T(8,128)(2,1)} %constant.26.clone.band_ref) | copy-start | bytes 196612
  6.5 19.9 %copy-start.16 = (bf16[64,256]{1,0:T(8,128)(2,1)S(1)}, bf16[64,256]{1,0:T(8,128)(2,1)}, u32[]{:S(2)}) copy-start(bf16[64,256]{1,0:T(8,128)(2,1)} %constant.19.clone.rows_ref) | copy-start | bytes 98308
  6.5 19.9 %copy-start.17 = (bf16[64,64]{1,0:T(8,128)(2,1)S(1)}, bf16[64,64]{1,0:T(8,128)(2,1)}, u32[]{:S(2)}) copy-start(bf16[64,64]{1,0:T(8,128)(2,1)} %constant.21.clone.grid_ref) | copy-start | bytes 24580
  26.4 16.5 %copy-start.3 = (bf16[256,256]{1,0:T(8,128)(2,1)S(1)}, bf16[256,256]{1,0:T(8,128)(2,1)}, u32[]{:S(2)}) copy-start(bf16[256,256]{1,0:T(8,128)(2,1)} %constant.23.clone.across_ref) | copy-start | bytes 393220
  26.4 16.5 %copy-start.7 = (bf16[256,256]{1,0:T(8,128)(2,1)S(1)}, bf16[256,256]{1,0:T(8,128)(2,1)}, u32[]{:S(2)}) copy-start(bf16[256,256]{1,0:T(8,128)(2,1)} %constant.18.clone.cols_ref) | copy-start | bytes 393220
  26.4 16.5 %copy-start.13 = (bf16[256,256]{1,0:T(8,128)(2,1)S(1)}, bf16[256,256]{1,0:T(8,128)(2,1)}, u32[]{:S(2)}) copy-start(bf16[256,256]{1,0:T(8,128)(2,1)} %constant.24.clone.tall_ref) | copy-start | bytes 393220
  26.5 16.5 %copy-start.14 = (bf16[272,64]{1,0:T(8,128)(2,1)S(1)}, bf16[272,64]{1,0:T(8,128)(2,1)}, u32[]{:S(2)}) copy-start(bf16[272,64]{1,0:T(8,128)(2,1)} %constant.20.clone.ext_ref) | copy-start | bytes 104452
  28.5 7.4 %collective-permute-start = (bf16[64,128]{1,0:T(8,128)(2,1)S(1)}, bf16[64,128]{1,0:T(8,128)(2,1)S(1)}, u32[]{:S(2)}, u32[]{:S(2)}) collective-permute-start(bf16[64,128]{1,0:T(8,128)(2,1)S(1)} %get-tuple-element.20), channel_id=1, source_target_pairs={{0,1},{1,2},{2,3},{3,4},{4,5},{5,6},{6,7},{7,8},{8,9},{9,10},{10,1... | collective-permute-start | bytes 49160 | tf_op jit(solution)/shard_map/ppermute | solution.py:312
  34.0 9.0 %collective-permute-start.1 = (bf16[64,128]{1,0:T(8,128)(2,1)S(1)}, bf16[64,128]{1,0:T(8,128)(2,1)S(1)}, u32[]{:S(2)}, u32[]{:S(2)}) collective-permute-start(bf16[64,128]{1,0:T(8,128)(2,1)S(1)} %get-tuple-element.21), channel_id=1, source_target_pairs={{1,0},{2,1},{3,2},{4,3},{5,4},{6,5},{7,6},{8,7},{9,8},{10,9},{11,1... | collective-permute-start | bytes 49160 | tf_op jit(solution)/shard_map/ppermute | solution.py:312
  42.9 10.8 %copy-start.1 = (bf16[16,16,256]{2,1,0:T(8,128)(2,1)S(1)}, bf16[16,16,256]{2,1,0:T(8,128)(2,1)}, u32[]{:S(2)}) copy-start(bf16[16,16,256]{2,1,0:T(8,128)(2,1)} %target_ref.5) | copy-start | bytes 393220
  42.9 10.8 %copy-start.5 = (bf16[16,16,256]{2,1,0:T(8,128)(2,1)S(1)}, bf16[16,16,256]{2,1,0:T(8,128)(2,1)}, u32[]{:S(2)}) copy-start(bf16[16,16,256]{2,1,0:T(8,128)(2,1)} %mask_ref.3) | copy-start | bytes 393220
  43.0 10.8 %copy-start.8 = (bf16[32,32]{1,0:T(8,128)(2,1)S(1)}, bf16[32,32]{1,0:T(8,128)(2,1)}, u32[]{:S(2)}) copy-start(bf16[32,32]{1,0:T(8,128)(2,1)} %constant.25.clone.down_ref) | copy-start | bytes 6148
  47.9 6.2 %collective-permute-start.2 = (bf16[32,128]{1,0:T(8,128)(2,1)S(1)}, bf16[32,128]{1,0:T(8,128)(2,1)S(1)}, u32[]{:S(2)}, u32[]{:S(2)}) collective-permute-start(bf16[32,128]{1,0:T(8,128)(2,1)S(1)} %get-tuple-element.27), channel_id=1, source_target_pairs={{0,1},{1,2},{2,3},{3,4},{4,5},{5,6},{6,7},{7,8},{8,9},{9,10},{10,1... | collective-permute-start | bytes 24584 | tf_op jit(solution)/shard_map/ppermute | solution.py:312
  49.8 8.9 %collective-permute-start.3 = (bf16[32,128]{1,0:T(8,128)(2,1)S(1)}, bf16[32,128]{1,0:T(8,128)(2,1)S(1)}, u32[]{:S(2)}, u32[]{:S(2)}) collective-permute-start(bf16[32,128]{1,0:T(8,128)(2,1)S(1)} %get-tuple-element.28), channel_id=1, source_target_pairs={{1,0},{2,1},{3,2},{4,3},{5,4},{6,5},{7,6},{8,7},{9,8},{10,9},{11,1... | collective-permute-start | bytes 24584 | tf_op jit(solution)/shard_map/ppermute | solution.py:312

commit v3 on v2

v3 whole, which is shorter than its diff:
```python
import functools
import math

import jax
import jax.numpy as jnp
import ml_dtypes
import numpy as np
from jax import lax
from jax.experimental import pallas as pl
from jax.experimental.pallas import tpu as pltpu
from jax.sharding import PartitionSpec as P

EDGE = 256
KF = 31
NK = 12
RB = 8
SLOTS = 16
USED = 12
GROUPS = USED // 4
ROWS = 16
EXT = ROWS + 2 * RB
COARSE = 64
STEEPNESS = 1.5
THRESHOLD = 2.0
STEP_GAIN = 0.5
BF = jnp.bfloat16
F32 = jnp.float32


def bf16(x):
    return np.asarray(x, np.float32).astype(ml_dtypes.bfloat16)


def high_low(x):
    high = bf16(x)
    return high, bf16(np.asarray(x, np.float32) - high.astype(np.float32))


@functools.cache
def tables():
    freq = np.arange(32) - KF // 2
    live = (np.arange(32) < KF).astype(np.float64)

    def waves(position):
        angle = 2.0 * np.pi * ((np.asarray(position)[:, None] * freq[None, :]) % EDGE) / EDGE
        return np.cos(angle) * live, np.sin(angle) * live

    cos, sin = waves(np.arange(EDGE))
    t = {}
    t["cols"] = bf16(np.concatenate([np.tile(cos, (1, 4)), np.tile(-sin, (1, 4))], 1) / 16.0)
    t["rows"] = bf16(np.concatenate([cos, sin], 1).T / 16.0)
    ext_cos, ext_sin = waves((np.arange(EDGE + 2 * RB) - RB) % EDGE)
    t["ext"] = bf16(np.concatenate([ext_cos, ext_sin], 1))
    c_cos, c_sin = waves(np.arange(COARSE) * (EDGE // COARSE))
    t["grid"] = bf16(np.concatenate([c_cos, c_sin], 1))
    inv = np.zeros((256, 512))
    for i in range(4):
        r, c = slice(32 * i, 32 * i + 32), 128 * i
        inv[r, c : c + 64] = c_cos.T
        inv[r, c + 64 : c + 128] = c_sin.T
        r = slice(128 + 32 * i, 128 + 32 * i + 32)
        inv[r, c : c + 64] = -c_sin.T
        inv[r, c + 64 : c + 128] = c_cos.T
    t["inv"] = bf16(inv)
    d = np.arange(EDGE)[None, :] - (EDGE // COARSE) * np.arange(COARSE)[:, None]
    interp = np.ones((COARSE, EDGE))
    for m in range(1, 32):
        interp += 2.0 * np.cos(2.0 * np.pi * m * d / EDGE)
    interp /= COARSE
    taps = np.exp(-(np.arange(-RB, RB + 1.0) ** 2) / (2.0 * (RB / 2.0) ** 2))
    taps /= taps.sum()
    blur = np.zeros((EDGE, EDGE))
    above = np.zeros((EDGE, EDGE))
    below = np.zeros((EDGE, EDGE))
    for b in range(EDGE):
        for step in range(-RB, RB + 1):
            a = b + step
            (above if a < 0 else below if a >= EDGE else blur)[a % EDGE, b] += taps[step + RB]
    wide = np.concatenate([interp @ blur] * 2, 0)
    t["across"] = np.concatenate(high_low(wide), 0)
    side = np.concatenate([np.arange(RB), np.arange(EDGE - RB, EDGE)])
    own = np.zeros((128 * USED, 256))
    for g in range(USED):
        own[128 * g : 128 * (g + 1), 16 * g : 16 * (g + 1)] = wide[:, side]
    t["own"] = bf16(own)
    full = np.concatenate([np.tile(cos, (1, 4)), np.tile(-sin, (1, 4))], 1) / 16.0
    inside = full.copy()
    inside[side] = 0.0
    t["inside"] = bf16(inside)
    rim = np.zeros((256, 768))
    for g in range(USED):
        rim[16 * g : 16 * (g + 1), 32 * g : 32 * g + 32] = cos[side] / 16.0
        rim[16 * g : 16 * (g + 1), 384 + 32 * g : 384 + 32 * g + 32] = -sin[side] / 16.0
    t["rim"] = bf16(rim)
    e_cos, e_sin = waves(side)
    inv_side = np.zeros((256, 128))
    for i in range(4):
        r, c = slice(32 * i, 32 * i + 32), 32 * i
        inv_side[r, c : c + 16] = e_cos.T
        inv_side[r, c + 16 : c + 32] = e_sin.T
        r = slice(128 + 32 * i, 128 + 32 * i + 32)
        inv_side[r, c : c + 16] = -e_sin.T
        inv_side[r, c + 16 : c + 32] = e_cos.T
    t["inv_side"] = bf16(inv_side)
    reach = np.zeros((512, 256))
    for n in range(512):
        q = n % 16
        if n % 256 >= 128 + 128 or (n % 256 >= 128 and (n // 16) % 2):
            continue
        for p in range(16):
            if n < 256 and q >= 8 and p < 8:
                reach[n, p::16] = above[EDGE - RB + q - 8, p]
            if n >= 256 and q < 8 and p >= 8:
                reach[n, p::16] = below[q, EDGE - RB + p - 8]
    t["reach"] = bf16(reach)
    main_high, main_low = high_low((interp @ blur).T)
    t["tall"] = np.concatenate(
        [main_high, bf16((interp @ above).T), bf16((interp @ below).T), main_low], 1
    )
    down = np.zeros((ROWS, EXT))
    for r in range(ROWS):
        down[r, r : r + 2 * RB + 1] = taps
    t["down"] = np.concatenate(high_low(down), 0)
    return t


def dot(a, b):
    return jnp.dot(a, b, preferred_element_type=F32)


def lane_block(width, size):
    return lax.broadcasted_iota(jnp.int32, (1, width), 1) // size


def four_slots(blocks, place):
    total = blocks[0]
    for i in range(1, 4):
        total = jnp.where(place == i, blocks[i], total)
    return total


def start_kernel(mask_hbm, target_hbm, cols_hbm, y_ref, mask_ref, target_ref, cols_ref, sems):
    copies = [
        pltpu.make_async_copy(mask_hbm.at[pl.ds(0, USED)], mask_ref, sems.at[0]),
        pltpu.make_async_copy(cols_hbm, cols_ref, sems.at[1]),
        pltpu.make_async_copy(target_hbm.at[pl.ds(0, USED)], target_ref, sems.at[2]),
    ]
    for copy in copies:
        copy.start()
    for copy in copies:
        copy.wait()
    of_mask = dot(mask_ref[...].reshape(USED * ROWS, EDGE), cols_ref[...])
    of_target = dot(target_ref[...].reshape(USED * ROWS, EDGE), cols_ref[...])
    place = lane_block(256, 32) % 4
    for n, both in enumerate((of_mask, of_mask + STEP_GAIN * of_target)):
        for j in range(GROUPS):
            firsts = [(4 * j + i) * ROWS for i in range(4)]
            total = four_slots([both[f : f + ROWS] for f in firsts], place).astype(BF)
            lane = 768 * n + 128 * j
            y_ref[:, lane : lane + 128] = total[:, :128]
            y_ref[:, lane + 384 : lane + 512] = total[:, 128:]


def lay_kernels(plane_ref, kernels_ref):
    kernels_ref[...] = jnp.zeros_like(kernels_ref)
    for k in range(NK):
        for part in range(2):
            kernels_ref[k, part, :KF, :KF] = plane_ref[pl.ds(2 * KF * k + part, KF, stride=2), :]
    for k in range(NK):
        for part in range(2):
            one = kernels_ref[k, part]
            one = one + pltpu.roll(one, 32, 1)
            kernels_ref[k, part] = one + pltpu.roll(one, 64, 1)


def lay_slots(dose_ref, row_ref, slot_ref, narrow_ref):
    wide, narrow, quarter = lane_block(128 * USED, 128), lane_block(256, 2 * RB), lane_block(128 * GROUPS, 32)
    weight, up, down = (jnp.zeros((1, 128 * USED), F32) for _ in range(3))
    up_narrow, down_narrow = (jnp.zeros((1, 256), F32) for _ in range(2))
    weight_quarter = jnp.zeros((1, 128 * GROUPS), F32)
    for g in range(USED):
        row = row_ref[g]
        scale = jnp.where(row >= 0, dose_ref[g], 0.0) * (1.0 / (NK * KF * KF))
        weight = jnp.where(wide == g, scale, weight)
        weight_quarter = jnp.where(quarter == g, scale, weight_quarter)
        if g > 0:
            before = row_ref[g - 1]
            joined = jnp.where((before >= 0) & (row >= 0) & (before == row - 1), 1.0, 0.0)
            up = jnp.where(wide == g, joined, up)
            down = jnp.where(wide == g - 1, joined, down)
            up_narrow = jnp.where(narrow == g, joined, up_narrow)
            down_narrow = jnp.where(narrow == g - 1, joined, down_narrow)
    slot_ref[...] = jnp.concatenate([weight, up, down, jnp.zeros((5, 128 * USED), F32)], 0)
    narrow_ref[...] = jnp.concatenate(
        [
            jnp.concatenate([up_narrow, jnp.zeros((1, 128), F32)], 1),
            jnp.concatenate([down_narrow, jnp.zeros((1, 128), F32)], 1),
            weight_quarter,
            jnp.zeros((5, 128 * GROUPS), F32),
        ],
        0,
    )


def lay_pick(side_ref, reach_ref, pick_ref):
    narrow = lane_block(256, 2 * RB)
    row = lax.broadcasted_iota(jnp.int32, (256, 1), 0)
    source = jnp.where(row < 128, row // 32 + 4 * ((row // 16) % 2), 8 + (row - 128) // 32)
    for n in range(2):
        wanted = jnp.full((1, 256), -1, jnp.int32)
        for g in range(USED):
            wanted = jnp.where(narrow == g, side_ref[n, g], wanted)
        rows = slice(256 * n, 256 * (n + 1))
        pick_ref[rows, :] = jnp.where(source == wanted, reach_ref[rows, :].astype(F32), 0.0).astype(BF)


def side_columns(inner, kernels_ref, points, inv_side_ref, narrow_ref, held, bands_ref):
    count = points.shape[0]
    half = 32 * USED
    sides = []
    for j in range(GROUPS):
        lanes, more = slice(128 * j, 128 * (j + 1)), slice(half + 128 * j, half + 128 * (j + 1))
        re = inner[:32, lanes] + inner[32:, more]
        im = inner[:32, more] - inner[32:, lanes]
        for k in range(NK):
            k_re, k_im = kernels_ref[k, 0], kernels_ref[k, 1]
            p_re = k_re * re - k_im * im
            p_im = k_re * im + k_im * re
            block = jnp.concatenate(
                [jnp.concatenate([p_re, p_im], 1), jnp.concatenate([-p_im, p_re], 1)], 0
            ).astype(BF)
            held[j, k * count : (k + 1) * count, :] = dot(points, block).astype(BF)
        field = dot(held[j], inv_side_ref[...])
        squares = jnp.sum((field * field).reshape(NK, count, 128), axis=0)
        sides.append((squares + pltpu.roll(squares, 112, 1)) * narrow_ref[2:3, lanes])
    even = lane_block(128, 16) % 2 == 0
    bands_ref[:, :128] = jnp.where(even, sides[0], pltpu.roll(sides[1], 16, 1)).astype(BF)
    bands_ref[:, 128:] = jnp.where(even, sides[2], 0.0).astype(BF)


def coarse_group(held, j, count, inv_ref, slot_ref):
    field = dot(held[j], inv_ref[...])
    squares = jnp.sum((field * field).reshape(NK, count, 512), axis=0)
    return squares * slot_ref[0:1, 512 * j : 512 * (j + 1)]


def first_kernel(all_ref, rows_ref, plane_ref, grid_ref, inv_side_ref, dose_ref, row_ref,
                 held_ref, bands_ref, base_ref, kernels_ref, slot_ref, narrow_ref):
    lay_kernels(plane_ref, kernels_ref)
    lay_slots(dose_ref, row_ref, slot_ref, narrow_ref)
    inner = dot(rows_ref[...], all_ref[...])
    base_ref[...] = inner[:, 768:]
    side_columns(inner[:, :768], kernels_ref, grid_ref[...], inv_side_ref, narrow_ref, held_ref, bands_ref)


def inside_kernel(held_ref, inv_ref, slot_ref, tall_ref, across_ref, rows_ref, inside_ref, base_ref, own_ref,
                  reach_ref, side_ref, part_ref, edge_ref, mine_ref, pick_ref, cells_ref, blurred, turned):
    lay_pick(side_ref, reach_ref, pick_ref)
    for j in range(GROUPS):
        cells_ref[:, 512 * j : 512 * (j + 1)] = coarse_group(held_ref, j, COARSE, inv_ref, slot_ref)
    cells = cells_ref[...]
    above = pltpu.roll(cells, 128, 1) * slot_ref[1:2, :]
    below = pltpu.roll(cells, 128 * (USED - 1), 1) * slot_ref[2:3, :]
    main = cells.astype(BF)
    edge_ref[...] = dot(main, own_ref[...])
    blurred[...] = dot(tall_ref[...], jnp.concatenate([main, above.astype(BF), below.astype(BF), main], 0)).astype(BF)
    first = pl.multiple_of(lax.axis_index("segment") * ROWS, ROWS)
    mine_ref[...] = blurred[pl.ds(first, ROWS), :]
    for g in range(USED):
        one = blurred[:, 128 * g : 128 * (g + 1)]
        fine = dot(jnp.concatenate([one, one], 1), across_ref[...])
        turned[64 * g : 64 * (g + 1), :] = dot(rows_ref[...], resist_of(fine).astype(BF)).astype(BF)
    both = dot(turned[...], inside_ref[...])
    place = lane_block(256, 32) % 4
    half = 32 * USED
    for j in range(GROUPS):
        total = four_slots([both[64 * (4 * j + i) : 64 * (4 * j + i + 1)] for i in range(4)], place)
        for n, first_lane in enumerate((128 * j, half + 128 * j)):
            lanes = slice(first_lane, first_lane + 128)
            part_ref[:, lanes] = base_ref[:, lanes] - STEP_GAIN * total[:, 128 * n : 128 * (n + 1)]


def lent(from_left_ref, from_right_ref, pick_ref):
    return dot(jnp.concatenate([from_left_ref[...], from_right_ref[...]], 1), pick_ref[...])


def second_kernel(from_left_ref, from_right_ref, pick_ref, edge_ref, narrow_ref, tall_ref, rows_ref, rim_ref, part_ref,
                  kernels_ref, ext_ref, inv_side_ref, held_ref, bands_ref, mine_side_ref, blurred):
    cells = edge_ref[...] + lent(from_left_ref, from_right_ref, pick_ref)
    above = pltpu.roll(cells, 2 * RB, 1) * narrow_ref[0:1, :256]
    below = pltpu.roll(cells, 256 - 2 * RB, 1) * narrow_ref[1:2, :256]
    main = cells.astype(BF)
    fine = dot(tall_ref[...], jnp.concatenate([main, above.astype(BF), below.astype(BF), main], 0))
    blurred[...] = fine
    first = pl.multiple_of(lax.axis_index("segment") * ROWS, ROWS)
    mine_side_ref[...] = blurred[pl.ds(first, ROWS), :]
    turned = dot(rows_ref[...], resist_of(fine).astype(BF)).astype(BF)
    inner = part_ref[...] - STEP_GAIN * dot(turned, rim_ref[...])
    side_columns(inner, kernels_ref, ext_ref[pl.ds(first, EXT), :], inv_side_ref, narrow_ref, held_ref, bands_ref)


def resist_of(blurred):
    return 0.5 * jnp.tanh((0.5 * STEEPNESS) * (blurred - THRESHOLD)) + 0.5


def stacked(low):
    stack = jnp.concatenate([low[:, 128 * g : 128 * (g + 1)] for g in range(USED)], 0)
    return jnp.concatenate([stack, stack], 1)


def blur_rows(cells, up, down, step, down_ref):
    segment = lax.axis_index("segment")
    width = cells.shape[1]
    top, center, bottom = cells[:RB], cells[RB : RB + ROWS], cells[RB + ROWS :]
    top = jnp.where(segment == 0, pltpu.roll(top, step, 1) * up, top)
    bottom = jnp.where(
        segment == lax.axis_size("segment") - 1, pltpu.roll(bottom, width - step, 1) * down, bottom
    )
    both = dot(down_ref[...], jnp.concatenate([top, center, bottom], 0).astype(BF))
    return both[:ROWS] + both[ROWS:]


def at_sides(narrow, g):
    part = narrow[:, 128 * (g // 8) : 128 * (g // 8) + 128]
    first = 2 * RB * (g % 8)
    return pltpu.roll(part, (128 - first) % 128, 1), pltpu.roll(part, (112 - first) % 128, 1)


def local_kernel(mine_ref, mine_side_ref, held_ref, inv_ref, slot_ref, down_ref, across_ref, mask_ref, target_ref,
                 inner_ref, once_ref, cells_ref):
    fine = dot(stacked(mine_ref[...]), across_ref[...])
    lane = lax.broadcasted_iota(jnp.int32, (1, 128), 1)
    mine_side = mine_side_ref[...]
    for g in range(SLOTS):
        if g < USED:
            left, right = at_sides(mine_side, g)
            part = fine[ROWS * g : ROWS * (g + 1)]
            left = jnp.where(lane < RB, left, part[:, :128])
            right = jnp.where(lane >= 128 - RB, right, part[:, 128:])
            part = jnp.concatenate([left, right], 1)
        else:
            part = jnp.zeros((ROWS, EDGE), F32)
        step = STEP_GAIN * (target_ref[g].astype(F32) - resist_of(part))
        once_ref[g] = (mask_ref[g].astype(F32) + step).astype(BF)
    for j in range(GROUPS):
        cells_ref[:, 512 * j : 512 * (j + 1)] = coarse_group(held_ref, j, EXT, inv_ref, slot_ref)
    low = blur_rows(cells_ref[...], slot_ref[1:2, :], slot_ref[2:3, :], 128, down_ref)
    inner_ref[...] = dot(stacked(low.astype(BF)), across_ref[...])


def final_kernel(inner_ref, from_left_ref, from_right_ref, pick_ref, narrow_ref, down_ref, once_ref, target_ref,
                 mask_hbm, resist_hbm, mask_ref, resist_ref, sems):
    def sent(n):
        four = pl.ds(4 * n, 4)
        return [
            pltpu.make_async_copy(resist_ref.at[four], resist_hbm.at[four], sems.at[n]),
            pltpu.make_async_copy(mask_ref.at[four], mask_hbm.at[four], sems.at[4 + n]),
        ]

    lane = lax.broadcasted_iota(jnp.int32, (1, 128), 1)
    for n in (3, 0, 1, 2):
        if n == 0:
            narrow = blur_rows(lent(from_left_ref, from_right_ref, pick_ref), narrow_ref[0:1, :256],
                               narrow_ref[1:2, :256], 2 * RB, down_ref)
        for g in range(4 * n, 4 * n + 4):
            if g < USED:
                left, right = at_sides(narrow, g)
                left = jnp.where(lane < RB, left, 0.0)
                right = jnp.where(lane >= 128 - RB, right, 0.0)
                part = inner_ref[ROWS * g : ROWS * (g + 1), :] + jnp.concatenate([left, right], 1)
            else:
                part = jnp.zeros((ROWS, EDGE), F32)
            part = resist_of(part)
            resist_ref[g] = part
            mask_ref[g] = (once_ref[g].astype(F32) + STEP_GAIN * (target_ref[g].astype(F32) - part)).astype(BF)
        for copy in sent(n):
            copy.start()
    for n in range(4):
        for copy in sent(n):
            copy.wait()


VMEM = pl.BlockSpec(memory_space=pltpu.VMEM)
SMEM = pl.BlockSpec(memory_space=pltpu.SMEM)
HBM = pl.BlockSpec(memory_space=pltpu.HBM)


def call(kernel, ins, outs, flops, scratch=(), name=None, place=VMEM, grant=32 * 2**20):
    size = sum(math.prod(o.shape) * o.dtype.itemsize for o in outs)
    return pl.pallas_call(
        kernel,
        out_shape=tuple(outs),
        in_specs=list(ins),
        out_specs=tuple(place for _ in outs),
        scratch_shapes=list(scratch),
        compiler_params=pltpu.CompilerParams(vmem_limit_bytes=grant),
        cost_estimate=pl.CostEstimate(flops=flops, bytes_accessed=2 * size, transcendentals=0),
        name=name,
    )


def passed_along(block, distance):
    devices = range(lax.axis_size("tile"))
    route = [(i - distance, i) for i in devices if i - distance in devices]
    return lax.ppermute(block, "tile", route)


def body(mask, target, spectra, dose, slot_row, side_source):
    t = {name: jnp.asarray(value) for name, value in tables().items()}
    shape = jax.ShapeDtypeStruct
    tile_rows = pltpu.VMEM((USED, ROWS, EDGE), BF)
    plane = spectra.transpose(0, 2, 1, 3).reshape(NK * KF * 2, KF)
    (y,) = call(
        start_kernel,
        [HBM] * 3,
        [shape((ROWS, 128 * USED), BF)],
        10**8,
        [tile_rows, tile_rows, pltpu.VMEM((EDGE, 256), BF), pltpu.SemaphoreType.DMA((3,))],
        name="start",
        grant=62 * 2**20,
    )(mask, target, t["cols"])
    rows_all = lax.all_gather(y, "segment", axis=0, tiled=True)
    held, bands, base, kernels, slot, narrow = call(
        first_kernel,
        [VMEM] * 5 + [SMEM] * 2,
        [
            shape((GROUPS, NK * COARSE, 256), BF),
            shape((COARSE, 256), BF),
            shape((64, 64 * USED), F32),
            shape((NK, 2, 32, 128), F32),
            shape((8, 128 * USED), F32),
            shape((8, 128 * GROUPS), F32),
        ],
        10**9,
        name="first",
    )(rows_all, t["rows"], plane, t["grid"], t["inv_side"], dose, slot_row)
    from_left = passed_along(bands, 1)
    from_right = passed_along(bands, -1)
    part, edge, mine, pick = call(
        inside_kernel,
        [VMEM] * 10 + [SMEM],
        [
            shape((64, 64 * USED), F32),
            shape((COARSE, 256), F32),
            shape((ROWS, 128 * USED), BF),
            shape((512, 256), BF),
        ],
        10**9,
        [
            pltpu.VMEM((COARSE, 128 * USED), F32),
            pltpu.VMEM((EDGE, 128 * USED), BF),
            pltpu.VMEM((64 * USED, EDGE), BF),
        ],
        name="inside",
    )(held, t["inv"], slot, t["tall"], t["across"], t["rows"], t["inside"], base, t["own"], t["reach"], side_source.T)
    held, bands, mine_side = call(
        second_kernel,
        [VMEM] * 12,
        [shape((GROUPS, NK * EXT, 256), BF), shape((EXT, 256), BF), shape((ROWS, 256), F32)],
        10**9,
        [pltpu.VMEM((EDGE, 256), F32)],
        name="second",
    )(from_left, from_right, pick, edge, narrow, t["tall"], t["rows"], t["rim"], part, kernels, t["ext"], t["inv_side"])
    from_left = passed_along(bands, 1)
    from_right = passed_along(bands, -1)
    inner, once = call(
        local_kernel,
        [VMEM] * 9,
        [shape((USED * ROWS, EDGE), F32), shape((SLOTS, ROWS, EDGE), BF)],
        10**9,
        [pltpu.VMEM((EXT, 128 * USED), F32)],
        name="local",
    )(mine, mine_side, held, t["inv"], slot, t["down"], t["across"], mask, target)
    return call(
        final_kernel,
        [VMEM] * 8,
        [shape((SLOTS, ROWS, EDGE), BF), shape((SLOTS, ROWS, EDGE), F32)],
        10**8,
        [
            pltpu.VMEM((SLOTS, ROWS, EDGE), BF),
            pltpu.VMEM((SLOTS, ROWS, EDGE), F32),
            pltpu.SemaphoreType.DMA((8,)),
        ],
        name="final",
        place=HBM,
    )(inner, from_left, from_right, pick, narrow, t["down"], once, target)


def solution(mesh):
    in_specs = (
        P("tile", "segment", None),
        P("tile", "segment", None),
        P(),
        P("tile"),
        P("tile"),
        P("tile", None),
    )
    out_specs = (P("tile", "segment", None), P("tile", "segment", None))
    return jax.shard_map(body, mesh=mesh, in_specs=in_specs, out_specs=out_specs, check_vma=False)
```

time: 60.3 us -> 54.4 us (0.902)
  the two profiles are of different devices: /device:TPU:198 before, /device:TPU:256 now
where the time goes in v3:
time: 54.4 us; the launch traced here: 54.2 us
  blocking collectives  20 us (37%)
  starting transfers between devices  12.7 us (23%)
  Pallas kernels  12.1 us (22%)
  waiting for transfers between devices  8.31 us (15%)
  between operations  0.96 us (2%)
    all_gather x1, blocking collectives, body(): rows_all = lax.all_gather(y, 'segment', axis=0, tiled=True)  20 us
    ppermute x4, starting transfers between devices, passed_along(): return lax.ppermute(block, 'tile', route)  12.7 us
    ppermute x4, waiting for transfers between devices, passed_along(): return lax.ppermute(block, 'tile', route)  8.31 us
    pallas_call x1, Pallas kernels, body(): call(inside_kernel, [VMEM] * 10 + [SMEM], [shape((64, 64 * USED), F32), s...  4.77 us
    pallas_call x1, Pallas kernels, body(): call(start_kernel, [HBM] * 3, [shape((ROWS, 128 * USED), BF)], 10 ** 8, [...  1.91 us
    pallas_call x1, Pallas kernels, body(): call(first_kernel, [VMEM] * 5 + [SMEM] * 2, [shape((GROUPS, NK * COARSE,...  1.86 us
    pallas_call x1, Pallas kernels, body(): call(second_kernel, [VMEM] * 12, [shape((GROUPS, NK * EXT, 256), BF), sha...  1.49 us
    pallas_call x1, Pallas kernels, body(): call(final_kernel, [VMEM] * 8, [shape((SLOTS, ROWS, EDGE), BF), shape((SL...  1.21 us
  transfers between devices with their start and end apart: 4, of which 2 were waited for; matrix products, arithmetic and copies ran while one was open for 0% of the time, Pallas kernels for 10%

profile of v3, /device:TPU:256, one launch (start us, length us, event | category | flops | bytes accessed | tf_op | source)
XLA Modules:
  0.0 54.2 jit_solution(13507335917069739676)
XLA Ops:
  0.6 0.0 copy-start.16
  0.6 0.0 copy-start.15
  0.7 0.0 copy-start.17
  0.7 0.0 copy-start.6
  0.7 0.0 copy-start.5
  0.7 0.0 copy-start.3
  0.7 1.9 %start.1 = bf16[16,1536]{1,0:T(8,128)(2,1)} custom-call(bf16[16,16,256]{2,1,0:T(8,128)(2,1)} %mask_ref.1, bf16[16,16,256]{2,1,0:T(8,128)(2,1)} %target_ref.3, bf16[256,256]{1,0:T(8,128)(2,1)} %constant.26.clone.cols_hbm), custom_call_target="tpu_custom_call" | custom-call | flops 100000000 | bytes 98304 | tf_op jit(solution)/shard_map/start/pallas_call | solution.py:413
  2.6 20.0 %all_gather.3.all_ref = bf16[256,1536]{1,0:T(8,128)(2,1)S(1)} all-gather(bf16[16,1536]{1,0:T(8,128)(2,1)} %start.1), channel_id=1, replica_groups=mesh['segment'=16,'tile'=32] {'segment'}, dimensions={0}, use_global_device_ids=true | all-gather | bytes 835584 | tf_op jit(solution)/shard_map/all_gather | solution.py:422
  22.6 0.0 copy-done.16
  22.6 0.0 copy-done.15
  22.6 0.0 copy-done.17
  22.6 0.0 copy-done.6
  22.6 0.0 copy-done.5
  22.6 0.0 copy-done.3
  22.7 0.0 copy-start.4
  22.7 0.0 copy-start.7
  22.7 0.0 copy-start.9
  22.7 0.0 copy-start.10
  22.7 0.0 copy-start.11
  22.7 0.0 copy-start.12
  22.7 0.0 copy-start.13
  22.7 1.9 %first.1 = (bf16[3,768,256]{2,1,0:T(8,128)(2,1)S(1)}, bf16[64,256]{1,0:T(8,128)(2,1)S(1)}, f32[64,768]{1,0:T(8,128)S(1)}, f32[12,2,32,128]{3,2,1,0:T(8,128)S(1)}...) custom-call(bf16[256,1536]{1,0:T(8,128)(2,1)S(1)} %all_gather.3.all_ref, bf16[64,256]{1,0:T(8,128)(2,1)S(1)} %copy-done.16, ...), custom_call_target="tpu_custom_call" | custom-call | flops 1000000000 | bytes 3727360 | tf_op jit(solution)/shard_map/first/pallas_call | solution.py:423
  24.6 3.8 %collective-permute-start.1 = (bf16[64,256]{1,0:T(8,128)(2,1)S(1)}, bf16[64,256]{1,0:T(8,128)(2,1)S(1)}, u32[]{:S(2)}, u32[]{:S(2)}) collective-permute-start(bf16[64,256]{1,0:T(8,128)(2,1)S(1)} %get-tuple-element.21), channel_id=1, source_target_pairs={{1,0},{2,1},{3,2},{4,3},{5,4},{6,5},{7,6},{8,7},{9,8},{10,9},{11,1... | collective-permute-start | bytes 98312 | tf_op jit(solution)/shard_map/ppermute | solution.py:405
  28.4 2.1 %collective-permute-start = (bf16[64,256]{1,0:T(8,128)(2,1)S(1)}, bf16[64,256]{1,0:T(8,128)(2,1)S(1)}, u32[]{:S(2)}, u32[]{:S(2)}) collective-permute-start(bf16[64,256]{1,0:T(8,128)(2,1)S(1)} %get-tuple-element.21), channel_id=1, source_target_pairs={{0,1},{1,2},{2,3},{3,4},{4,5},{5,6},{6,7},{7,8},{8,9},{9,10},{10,1... | collective-permute-start | bytes 98312 | tf_op jit(solution)/shard_map/ppermute | solution.py:405
  30.5 0.0 copy-done.4
  30.5 0.0 copy-done.7
  30.5 0.0 copy-done.9
  30.5 0.0 copy-done.10
  30.5 0.0 copy-done.11
  30.5 0.0 copy-done.12
  30.5 0.0 copy-done.13
  30.5 0.0 copy-start.8
  30.6 0.0 copy-start.14
  30.6 4.8 %inside.1 = (f32[64,768]{1,0:T(8,128)S(1)}, f32[64,256]{1,0:T(8,128)S(1)}, bf16[16,1536]{1,0:T(8,128)(2,1)S(1)}, bf16[512,256]{1,0:T(8,128)(2,1)S(1)}) custom-call(bf16[3,768,256]{2,1,0:T(8,128)(2,1)S(1)} %get-tuple-element.17.held_ref, bf16[256,512]{1,0:T(8,128)(2,1)S(1)} %copy-done.9, f32[8,1536]{1,0:T(8,128)S(1)} %get-tuple-element.18.slot_ref, ...), custom_call_target="tpu_custom_call" | custom-call | flops 1000000000 | bytes 1146880 | tf_op jit(solution)/shard_map/inside/pallas_call | solution.py:439
  35.3 0.0 collective-permute-done.1.from_right_ref
  35.4 2.1 %collective-permute-done.from_left_ref = bf16[64,256]{1,0:T(8,128)(2,1)S(1)} collective-permute-done((bf16[64,256]{1,0:T(8,128)(2,1)S(1)}, bf16[64,256]{1,0:T(8,128)(2,1)S(1)}, u32[]{:S(2)}, u32[]{:S(2)}) %collective-permute-start) | collective-permute-done | bytes 32800 | tf_op jit(solution)/shard_map/ppermute | solution.py:405
  37.5 0.0 copy-done.8
  37.5 0.0 copy-done.14
  37.5 0.0 copy-start
  37.5 0.0 copy-start.1
  37.5 0.0 copy-start.2
  37.5 1.5 %second.1 = (bf16[3,384,256]{2,1,0:T(8,128)(2,1)S(1)}, bf16[32,256]{1,0:T(8,128)(2,1)S(1)}, f32[16,256]{1,0:T(8,128)S(1)}) custom-call(bf16[64,256]{1,0:T(8,128)(2,1)S(1)} %collective-permute-done.from_left_ref, bf16[64,256]{1,0:T(8,128)(2,1)S(1)} %collective-permute-done.1.from_right_ref, bf16[512,256]{1,0:T(8,128)(2,1)S(1)} %get-tuple-element.22.pick_ref, ...), custom_call_target="tpu_custom_call" | custom-call | flops 1000000000 | bytes 1245184 | tf_op jit(solution)/shard_map/second/pallas_call | solution.py:456
  39.0 5.0 %collective-permute-start.3 = (bf16[32,256]{1,0:T(8,128)(2,1)S(1)}, bf16[32,256]{1,0:T(8,128)(2,1)S(1)}, u32[]{:S(2)}, u32[]{:S(2)}) collective-permute-start(bf16[32,256]{1,0:T(8,128)(2,1)S(1)} %get-tuple-element.30), channel_id=1, source_target_pairs={{1,0},{2,1},{3,2},{4,3},{5,4},{6,5},{7,6},{8,7},{9,8},{10,9},{11,1... | collective-permute-start | bytes 49160 | tf_op jit(solution)/shard_map/ppermute | solution.py:405
  44.0 1.9 %collective-permute-start.2 = (bf16[32,256]{1,0:T(8,128)(2,1)S(1)}, bf16[32,256]{1,0:T(8,128)(2,1)S(1)}, u32[]{:S(2)}, u32[]{:S(2)}) collective-permute-start(bf16[32,256]{1,0:T(8,128)(2,1)S(1)} %get-tuple-element.30), channel_id=1, source_target_pairs={{0,1},{1,2},{2,3},{3,4},{4,5},{5,6},{6,7},{7,8},{8,9},{9,10},{10,1... | collective-permute-start | bytes 49160 | tf_op jit(solution)/shard_map/ppermute | solution.py:405
  45.9 0.0 copy-done
  45.9 0.0 copy-done.1
  45.9 0.0 copy-done.2
  46.0 0.8 %local.1 = (f32[192,256]{1,0:T(8,128)S(1)}, bf16[16,16,256]{2,1,0:T(8,128)(2,1)S(1)}) custom-call(bf16[16,1536]{1,0:T(8,128)(2,1)S(1)} %get-tuple-element.20.mine_ref, f32[16,256]{1,0:T(8,128)S(1)} %get-tuple-element.27.mine_side_ref, bf16[3,384,256]{2,1,0:T(8,128)(2,1)S(1)} %get-tuple-element.28.held_ref, bf16[256,512]{1,0:T(8,128)(2,1)S(1)} %copy-done.9, ...), custom_call_target="tpu_custom_call" | custom-call | flops 1000000000 | bytes 655360 | tf_op jit(solution)/shard_map/local/pallas_call | solution.py:466
  46.8 0.0 collective-permute-done.3.from_right_ref
  46.8 6.2 %collective-permute-done.2.from_left_ref = bf16[32,256]{1,0:T(8,128)(2,1)S(1)} collective-permute-done((bf16[32,256]{1,0:T(8,128)(2,1)S(1)}, bf16[32,256]{1,0:T(8,128)(2,1)S(1)}, u32[]{:S(2)}, u32[]{:S(2)}) %collective-permute-start.2) | collective-permute-done | bytes 16416 | tf_op jit(solution)/shard_map/ppermute | solution.py:405
  53.0 1.2 %final.1 = (bf16[16,16,256]{2,1,0:T(8,128)(2,1)}, f32[16,16,256]{2,1,0:T(8,128)}) custom-call(f32[192,256]{1,0:T(8,128)S(1)} %get-tuple-element.29.inner_ref, bf16[32,256]{1,0:T(8,128)(2,1)S(1)} %collective-permute-done.2.from_left_ref, bf16[32,256]{1,0:T(8,128)(2,1)S(1)} %collective-permute-done.3.from_right_ref, ...), custom_call_target="tpu_custom_call" | custom-call | flops 100000000 | bytes 786432 | tf_op jit(solution)/shard_map/final/pallas_call | solution.py:474
Async XLA Ops:
  0.6 22.0 %copy-start.16 = (bf16[64,256]{1,0:T(8,128)(2,1)S(1)}, bf16[64,256]{1,0:T(8,128)(2,1)}, u32[]{:S(2)}) copy-start(bf16[64,256]{1,0:T(8,128)(2,1)} %constant.27.clone.rows_ref) | copy-start | bytes 98308
  0.6 22.0 %copy-start.15 = (bf16[256,128]{1,0:T(8,128)(2,1)S(1)}, bf16[256,128]{1,0:T(8,128)(2,1)}, u32[]{:S(2)}) copy-start(bf16[256,128]{1,0:T(8,128)(2,1)} %constant.35.clone.inv_side_ref) | copy-start | bytes 196612
  0.7 22.0 %copy-start.17 = (bf16[64,64]{1,0:T(8,128)(2,1)S(1)}, bf16[64,64]{1,0:T(8,128)(2,1)}, u32[]{:S(2)}) copy-start(bf16[64,64]{1,0:T(8,128)(2,1)} %constant.29.clone.grid_ref) | copy-start | bytes 24580
  0.7 22.0 %copy-start.6 = (s32[16]{0:T(128)S(1)}, s32[16]{0:T(128)}, u32[]{:S(2)}) copy-start(s32[16]{0:T(128)} %row_ref.1) | copy-start | bytes 196
  0.7 22.0 %copy-start.5 = (f32[16]{0:T(128)S(1)}, f32[16]{0:T(128)}, u32[]{:S(2)}) copy-start(f32[16]{0:T(128)} %dose_ref.1) | copy-start | bytes 196
  0.7 22.0 %copy-start.3 = (f32[12,2,31,31]{3,1,2,0:T(2,128)S(1)}, f32[12,2,31,31]{3,1,2,0:T(2,128)}, u32[]{:S(2)}) copy-start(f32[12,2,31,31]{3,1,2,0:T(2,128)} %param.21) | copy-start | bytes 276772
  22.7 7.8 %copy-start.4 = (s32[16,2]{0,1:T(2,128)S(1)}, s32[16,2]{0,1:T(2,128)}, u32[]{:S(2)}) copy-start(s32[16,2]{0,1:T(2,128)} %param.24) | copy-start | bytes 388
  22.7 7.8 %copy-start.7 = (bf16[1536,256]{1,0:T(8,128)(2,1)S(1)}, bf16[1536,256]{1,0:T(8,128)(2,1)}, u32[]{:S(2)}) copy-start(bf16[1536,256]{1,0:T(8,128)(2,1)} %constant.32.clone.own_ref) | copy-start | bytes 2359300
  22.7 7.8 %copy-start.9 = (bf16[256,512]{1,0:T(8,128)(2,1)S(1)}, bf16[256,512]{1,0:T(8,128)(2,1)}, u32[]{:S(2)}) copy-start(bf16[256,512]{1,0:T(8,128)(2,1)} %constant.30.clone.inv_ref) | copy-start | bytes 786436
  22.7 7.8 %copy-start.10 = (bf16[512,256]{1,0:T(8,128)(2,1)S(1)}, bf16[512,256]{1,0:T(8,128)(2,1)}, u32[]{:S(2)}) copy-start(bf16[512,256]{1,0:T(8,128)(2,1)} %constant.36.clone.reach_ref) | copy-start | bytes 786436
  22.7 7.8 %copy-start.11 = (bf16[256,256]{1,0:T(8,128)(2,1)S(1)}, bf16[256,256]{1,0:T(8,128)(2,1)}, u32[]{:S(2)}) copy-start(bf16[256,256]{1,0:T(8,128)(2,1)} %constant.31.clone.across_ref) | copy-start | bytes 393220
  22.7 7.8 %copy-start.12 = (bf16[256,256]{1,0:T(8,128)(2,1)S(1)}, bf16[256,256]{1,0:T(8,128)(2,1)}, u32[]{:S(2)}) copy-start(bf16[256,256]{1,0:T(8,128)(2,1)} %constant.37.clone.tall_ref) | copy-start | bytes 393220
  22.7 7.8 %copy-start.13 = (bf16[256,256]{1,0:T(8,128)(2,1)S(1)}, bf16[256,256]{1,0:T(8,128)(2,1)}, u32[]{:S(2)}) copy-start(bf16[256,256]{1,0:T(8,128)(2,1)} %constant.33.clone.inside_ref) | copy-start | bytes 393220
  24.6 10.7 %collective-permute-start.1 = (bf16[64,256]{1,0:T(8,128)(2,1)S(1)}, bf16[64,256]{1,0:T(8,128)(2,1)S(1)}, u32[]{:S(2)}, u32[]{:S(2)}) collective-permute-start(bf16[64,256]{1,0:T(8,128)(2,1)S(1)} %get-tuple-element.21), channel_id=1, source_target_pairs={{1,0},{2,1},{3,2},{4,3},{5,4},{6,5},{7,6},{8,7},{9,8},{10,9},{11,1... | collective-permute-start | bytes 98312 | tf_op jit(solution)/shard_map/ppermute | solution.py:405
  28.4 9.1 %collective-permute-start = (bf16[64,256]{1,0:T(8,128)(2,1)S(1)}, bf16[64,256]{1,0:T(8,128)(2,1)S(1)}, u32[]{:S(2)}, u32[]{:S(2)}) collective-permute-start(bf16[64,256]{1,0:T(8,128)(2,1)S(1)} %get-tuple-element.21), channel_id=1, source_target_pairs={{0,1},{1,2},{2,3},{3,4},{4,5},{5,6},{6,7},{7,8},{8,9},{9,10},{10,1... | collective-permute-start | bytes 98312 | tf_op jit(solution)/shard_map/ppermute | solution.py:405
  30.5 7.0 %copy-start.8 = (bf16[256,768]{1,0:T(8,128)(2,1)S(1)}, bf16[256,768]{1,0:T(8,128)(2,1)}, u32[]{:S(2)}) copy-start(bf16[256,768]{1,0:T(8,128)(2,1)} %constant.34.clone.rim_ref) | copy-start | bytes 1179652
  30.6 7.0 %copy-start.14 = (bf16[272,64]{1,0:T(8,128)(2,1)S(1)}, bf16[272,64]{1,0:T(8,128)(2,1)}, u32[]{:S(2)}) copy-start(bf16[272,64]{1,0:T(8,128)(2,1)} %constant.28.clone.ext_ref) | copy-start | bytes 104452
  37.5 8.4 %copy-start = (bf16[16,16,256]{2,1,0:T(8,128)(2,1)S(1)}, bf16[16,16,256]{2,1,0:T(8,128)(2,1)}, u32[]{:S(2)}) copy-start(bf16[16,16,256]{2,1,0:T(8,128)(2,1)} %target_ref.3) | copy-start | bytes 393220
  37.5 8.4 %copy-start.1 = (bf16[16,16,256]{2,1,0:T(8,128)(2,1)S(1)}, bf16[16,16,256]{2,1,0:T(8,128)(2,1)}, u32[]{:S(2)}) copy-start(bf16[16,16,256]{2,1,0:T(8,128)(2,1)} %mask_ref.1) | copy-start | bytes 393220
  37.5 8.4 %copy-start.2 = (bf16[32,32]{1,0:T(8,128)(2,1)S(1)}, bf16[32,32]{1,0:T(8,128)(2,1)}, u32[]{:S(2)}) copy-start(bf16[32,32]{1,0:T(8,128)(2,1)} %constant.38.clone.down_ref) | copy-start | bytes 6148
  39.0 7.8 %collective-permute-start.3 = (bf16[32,256]{1,0:T(8,128)(2,1)S(1)}, bf16[32,256]{1,0:T(8,128)(2,1)S(1)}, u32[]{:S(2)}, u32[]{:S(2)}) collective-permute-start(bf16[32,256]{1,0:T(8,128)(2,1)S(1)} %get-tuple-element.30), channel_id=1, source_target_pairs={{1,0},{2,1},{3,2},{4,3},{5,4},{6,5},{7,6},{8,7},{9,8},{10,9},{11,1... | collective-permute-start | bytes 49160 | tf_op jit(solution)/shard_map/ppermute | solution.py:405
  44.0 9.0 %collective-permute-start.2 = (bf16[32,256]{1,0:T(8,128)(2,1)S(1)}, bf16[32,256]{1,0:T(8,128)(2,1)S(1)}, u32[]{:S(2)}, u32[]{:S(2)}) collective-permute-start(bf16[32,256]{1,0:T(8,128)(2,1)S(1)} %get-tuple-element.30), channel_id=1, source_target_pairs={{0,1},{1,2},{2,3},{3,4},{4,5},{5,6},{6,7},{7,8},{8,9},{9,10},{10,1... | collective-permute-start | bytes 49160 | tf_op jit(solution)/shard_map/ppermute | solution.py:405

commit v4 on v3

--- a/solution.py
+++ b/solution.py
@@ -280,13 +280,16 @@
             part_ref[:, lanes] = base_ref[:, lanes] - STEP_GAIN * total[:, 128 * n : 128 * (n + 1)]
 
 
-def lent(from_left_ref, from_right_ref, pick_ref):
-    return dot(jnp.concatenate([from_left_ref[...], from_right_ref[...]], 1), pick_ref[...])
-
-
-def second_kernel(from_left_ref, from_right_ref, pick_ref, edge_ref, narrow_ref, tall_ref, rows_ref, rim_ref, part_ref,
+def lent(near_ref, far_ref, pick_ref):
+    odd = lax.axis_index("tile") % 2 == 1
+    far, near = far_ref[...].astype(F32), near_ref[...].astype(F32)
+    left, right = jnp.where(odd, near, far), jnp.where(odd, far, near)
+    return dot(jnp.concatenate([left, right], 1).astype(BF), pick_ref[...])
+
+
+def second_kernel(near_ref, far_ref, pick_ref, edge_ref, narrow_ref, tall_ref, rows_ref, rim_ref, part_ref,
                   kernels_ref, ext_ref, inv_side_ref, held_ref, bands_ref, mine_side_ref, blurred):
-    cells = edge_ref[...] + lent(from_left_ref, from_right_ref, pick_ref)
+    cells = edge_ref[...] + lent(near_ref, far_ref, pick_ref)
     above = pltpu.roll(cells, 2 * RB, 1) * narrow_ref[0:1, :256]
     below = pltpu.roll(cells, 256 - 2 * RB, 1) * narrow_ref[1:2, :256]
     main = cells.astype(BF)
@@ -348,7 +351,7 @@
     inner_ref[...] = dot(stacked(low.astype(BF)), across_ref[...])
 
 
-def final_kernel(inner_ref, from_left_ref, from_right_ref, pick_ref, narrow_ref, down_ref, once_ref, target_ref,
+def final_kernel(inner_ref, near_ref, far_ref, pick_ref, narrow_ref, down_ref, once_ref, target_ref,
                  mask_hbm, resist_hbm, mask_ref, resist_ref, sems):
     def sent(n):
         four = pl.ds(4 * n, 4)
@@ -360,7 +363,7 @@
     lane = lax.broadcasted_iota(jnp.int32, (1, 128), 1)
     for n in (3, 0, 1, 2):
         if n == 0:
-            narrow = blur_rows(lent(from_left_ref, from_right_ref, pick_ref), narrow_ref[0:1, :256],
+            narrow = blur_rows(lent(near_ref, far_ref, pick_ref), narrow_ref[0:1, :256],
                                narrow_ref[1:2, :256], 2 * RB, down_ref)
         for g in range(4 * n, 4 * n + 4):
             if g < USED:
@@ -399,10 +402,9 @@
     )
 
 
-def passed_along(block, distance):
-    devices = range(lax.axis_size("tile"))
-    route = [(i - distance, i) for i in devices if i - distance in devices]
-    return lax.ppermute(block, "tile", route)
+def swapped(block, first):
+    pairs = [(i, i + 1) for i in range(first, lax.axis_size("tile") - 1, 2)]
+    return lax.ppermute(block, "tile", pairs + [(j, i) for i, j in pairs])
 
 
 def body(mask, target, spectra, dose, slot_row, side_source):
@@ -434,8 +436,8 @@
         10**9,
         name="first",
     )(rows_all, t["rows"], plane, t["grid"], t["inv_side"], dose, slot_row)
-    from_left = passed_along(bands, 1)
-    from_right = passed_along(bands, -1)
+    from_near = swapped(bands, 0)
+    from_far = swapped(bands, 1)
     part, edge, mine, pick = call(
         inside_kernel,
         [VMEM] * 10 + [SMEM],
@@ -460,9 +462,9 @@
         10**9,
         [pltpu.VMEM((EDGE, 256), F32)],
         name="second",
-    )(from_left, from_right, pick, edge, narrow, t["tall"], t["rows"], t["rim"], part, kernels, t["ext"], t["inv_side"])
-    from_left = passed_along(bands, 1)
-    from_right = passed_along(bands, -1)
+    )(from_near, from_far, pick, edge, narrow, t["tall"], t["rows"], t["rim"], part, kernels, t["ext"], t["inv_side"])
+    from_near = swapped(bands, 0)
+    from_far = swapped(bands, 1)
     inner, once = call(
         local_kernel,
         [VMEM] * 9,
@@ -483,7 +485,7 @@
         ],
         name="final",
         place=HBM,
-    )(inner, from_left, from_right, pick, narrow, t["down"], once, target)
+    )(inner, from_near, from_far, pick, narrow, t["down"], once, target)
 
 
 def solution(mesh):

time: 54.4 us -> 50.3 us (0.925)
  the two profiles are of different devices: /device:TPU:256 before, /device:TPU:198 now
where the time goes in v4:
time: 50.3 us; the launch traced here: 50.1 us
  blocking collectives  20 us (40%)
  starting transfers between devices  14.1 us (28%)
  Pallas kernels  12.1 us (24%)
  waiting for transfers between devices  2.85 us (6%)
  between operations  0.98 us (2%)
    all_gather x1, blocking collectives, body(): rows_all = lax.all_gather(y, 'segment', axis=0, tiled=True)  20 us
    ppermute x4, starting transfers between devices, swapped(): return lax.ppermute(block, 'tile', pairs + [(j, i) for i, j in pairs])  14.1 us
    pallas_call x1, Pallas kernels, body(): call(inside_kernel, [VMEM] * 10 + [SMEM], [shape((64, 64 * USED), F32), s...  4.77 us
    ppermute x4, waiting for transfers between devices, swapped(): return lax.ppermute(block, 'tile', pairs + [(j, i) for i, j in pairs])  2.85 us
    pallas_call x1, Pallas kernels, body(): call(start_kernel, [HBM] * 3, [shape((ROWS, 128 * USED), BF)], 10 ** 8, [...  1.92 us
    pallas_call x1, Pallas kernels, body(): call(first_kernel, [VMEM] * 5 + [SMEM] * 2, [shape((GROUPS, NK * COARSE,...  1.86 us
    pallas_call x1, Pallas kernels, body(): call(second_kernel, [VMEM] * 12, [shape((GROUPS, NK * EXT, 256), BF), sha...  1.49 us
    pallas_call x1, Pallas kernels, body(): call(final_kernel, [VMEM] * 8, [shape((SLOTS, ROWS, EDGE), BF), shape((SL...  1.21 us
  transfers between devices with their start and end apart: 4, of which 2 were waited for; matrix products, arithmetic and copies ran while one was open for 0% of the time, Pallas kernels for 11%

profile of v4, /device:TPU:198, one launch (start us, length us, event | category | flops | bytes accessed | tf_op | source)
XLA Modules:
  0.0 50.1 jit_solution(4352982318810413317)
XLA Ops:
  0.6 0.0 copy-start.16
  0.6 0.0 copy-start.15
  0.7 0.0 copy-start.17
  0.7 0.0 copy-start.6
  0.7 0.0 copy-start.5
  0.7 0.0 copy-start.3
  0.7 1.9 %start.1 = bf16[16,1536]{1,0:T(8,128)(2,1)} custom-call(bf16[16,16,256]{2,1,0:T(8,128)(2,1)} %mask_ref.1, bf16[16,16,256]{2,1,0:T(8,128)(2,1)} %target_ref.3, bf16[256,256]{1,0:T(8,128)(2,1)} %constant.26.clone.cols_hbm), custom_call_target="tpu_custom_call" | custom-call | flops 100000000 | bytes 98304 | tf_op jit(solution)/shard_map/start/pallas_call | solution.py:415
  2.6 20.0 %all_gather.3.all_ref = bf16[256,1536]{1,0:T(8,128)(2,1)S(1)} all-gather(bf16[16,1536]{1,0:T(8,128)(2,1)} %start.1), channel_id=1, replica_groups=mesh['segment'=16,'tile'=32] {'segment'}, dimensions={0}, use_global_device_ids=true | all-gather | bytes 835584 | tf_op jit(solution)/shard_map/all_gather | solution.py:424
  22.6 0.0 copy-done.16
  22.6 0.0 copy-done.15
  22.6 0.0 copy-done.17
  22.6 0.0 copy-done.6
  22.6 0.0 copy-done.5
  22.6 0.0 copy-done.3
  22.7 0.0 copy-start.4
  22.7 0.0 copy-start.7
  22.7 0.0 copy-start.9
  22.7 0.0 copy-start.10
  22.7 0.0 copy-start.11
  22.7 0.0 copy-start.12
  22.7 0.0 copy-start.13
  22.7 1.9 %first.1 = (bf16[3,768,256]{2,1,0:T(8,128)(2,1)S(1)}, bf16[64,256]{1,0:T(8,128)(2,1)S(1)}, f32[64,768]{1,0:T(8,128)S(1)}, f32[12,2,32,128]{3,2,1,0:T(8,128)S(1)}...) custom-call(bf16[256,1536]{1,0:T(8,128)(2,1)S(1)} %all_gather.3.all_ref, bf16[64,256]{1,0:T(8,128)(2,1)S(1)} %copy-done.16, ...), custom_call_target="tpu_custom_call" | custom-call | flops 1000000000 | bytes 3727360 | tf_op jit(solution)/shard_map/first/pallas_call | solution.py:425
  24.6 5.4 %collective-permute-start.1 = (bf16[64,256]{1,0:T(8,128)(2,1)S(1)}, bf16[64,256]{1,0:T(8,128)(2,1)S(1)}, u32[]{:S(2)}, u32[]{:S(2)}) collective-permute-start(bf16[64,256]{1,0:T(8,128)(2,1)S(1)} %get-tuple-element.21), channel_id=1, source_target_pairs={{1,2},{3,4},{5,6},{7,8},{9,10},{11,12},{13,14},{15,16},{17,18},{19... | collective-permute-start | bytes 98312 | tf_op jit(solution)/shard_map/ppermute | solution.py:407
  30.0 1.9 %collective-permute-start = (bf16[64,256]{1,0:T(8,128)(2,1)S(1)}, bf16[64,256]{1,0:T(8,128)(2,1)S(1)}, u32[]{:S(2)}, u32[]{:S(2)}) collective-permute-start(bf16[64,256]{1,0:T(8,128)(2,1)S(1)} %get-tuple-element.21), channel_id=1, source_target_pairs={{0,1},{2,3},{4,5},{6,7},{8,9},{10,11},{12,13},{14,15},{16,17},{18,... | collective-permute-start | bytes 98312 | tf_op jit(solution)/shard_map/ppermute | solution.py:407
  32.0 0.0 copy-done.4
  32.0 0.0 copy-done.7
  32.0 0.0 copy-done.9
  32.0 0.0 copy-done.10
  32.0 0.0 copy-done.11
  32.0 0.0 copy-done.12
  32.0 0.0 copy-done.13
  32.0 0.0 copy-start.8
  32.0 0.0 copy-start.14
  32.0 4.8 %inside.1 = (f32[64,768]{1,0:T(8,128)S(1)}, f32[64,256]{1,0:T(8,128)S(1)}, bf16[16,1536]{1,0:T(8,128)(2,1)S(1)}, bf16[512,256]{1,0:T(8,128)(2,1)S(1)}) custom-call(bf16[3,768,256]{2,1,0:T(8,128)(2,1)S(1)} %get-tuple-element.17.held_ref, bf16[256,512]{1,0:T(8,128)(2,1)S(1)} %copy-done.9, f32[8,1536]{1,0:T(8,128)S(1)} %get-tuple-element.18.slot_ref, ...), custom_call_target="tpu_custom_call" | custom-call | flops 1000000000 | bytes 1146880 | tf_op jit(solution)/shard_map/inside/pallas_call | solution.py:441
  36.8 0.0 collective-permute-done.1.far_ref
  36.8 0.0 collective-permute-done.near_ref
  36.8 0.0 copy-done.8
  36.9 0.0 copy-done.14
  36.9 0.0 copy-start
  36.9 0.0 copy-start.1
  36.9 0.0 copy-start.2
  36.9 1.5 %second.1 = (bf16[3,384,256]{2,1,0:T(8,128)(2,1)S(1)}, bf16[32,256]{1,0:T(8,128)(2,1)S(1)}, f32[16,256]{1,0:T(8,128)S(1)}) custom-call(bf16[64,256]{1,0:T(8,128)(2,1)S(1)} %collective-permute-done.near_ref, bf16[64,256]{1,0:T(8,128)(2,1)S(1)} %collective-permute-done.1.far_ref, bf16[512,256]{1,0:T(8,128)(2,1)S(1)} %get-tuple-element.22.pick_ref, ...), custom_call_target="tpu_custom_call" | custom-call | flops 1000000000 | bytes 1245184 | tf_op jit(solution)/shard_map/second/pallas_call | solution.py:458
  38.4 4.9 %collective-permute-start.3 = (bf16[32,256]{1,0:T(8,128)(2,1)S(1)}, bf16[32,256]{1,0:T(8,128)(2,1)S(1)}, u32[]{:S(2)}, u32[]{:S(2)}) collective-permute-start(bf16[32,256]{1,0:T(8,128)(2,1)S(1)} %get-tuple-element.30), channel_id=1, source_target_pairs={{1,2},{3,4},{5,6},{7,8},{9,10},{11,12},{13,14},{15,16},{17,18},{19... | collective-permute-start | bytes 49160 | tf_op jit(solution)/shard_map/ppermute | solution.py:407
  43.3 1.9 %collective-permute-start.2 = (bf16[32,256]{1,0:T(8,128)(2,1)S(1)}, bf16[32,256]{1,0:T(8,128)(2,1)S(1)}, u32[]{:S(2)}, u32[]{:S(2)}) collective-permute-start(bf16[32,256]{1,0:T(8,128)(2,1)S(1)} %get-tuple-element.30), channel_id=1, source_target_pairs={{0,1},{2,3},{4,5},{6,7},{8,9},{10,11},{12,13},{14,15},{16,17},{18,... | collective-permute-start | bytes 49160 | tf_op jit(solution)/shard_map/ppermute | solution.py:407
  45.2 0.0 copy-done
  45.2 0.0 copy-done.1
  45.2 0.0 copy-done.2
  45.2 0.8 %local.1 = (f32[192,256]{1,0:T(8,128)S(1)}, bf16[16,16,256]{2,1,0:T(8,128)(2,1)S(1)}) custom-call(bf16[16,1536]{1,0:T(8,128)(2,1)S(1)} %get-tuple-element.20.mine_ref, f32[16,256]{1,0:T(8,128)S(1)} %get-tuple-element.27.mine_side_ref, bf16[3,384,256]{2,1,0:T(8,128)(2,1)S(1)} %get-tuple-element.28.held_ref, bf16[256,512]{1,0:T(8,128)(2,1)S(1)} %copy-done.9, ...), custom_call_target="tpu_custom_call" | custom-call | flops 1000000000 | bytes 655360 | tf_op jit(solution)/shard_map/local/pallas_call | solution.py:468
  46.1 1.3 %collective-permute-done.3.far_ref = bf16[32,256]{1,0:T(8,128)(2,1)S(1)} collective-permute-done((bf16[32,256]{1,0:T(8,128)(2,1)S(1)}, bf16[32,256]{1,0:T(8,128)(2,1)S(1)}, u32[]{:S(2)}, u32[]{:S(2)}) %collective-permute-start.3) | collective-permute-done | bytes 16416 | tf_op jit(solution)/shard_map/ppermute | solution.py:407
  47.4 1.6 %collective-permute-done.2.near_ref = bf16[32,256]{1,0:T(8,128)(2,1)S(1)} collective-permute-done((bf16[32,256]{1,0:T(8,128)(2,1)S(1)}, bf16[32,256]{1,0:T(8,128)(2,1)S(1)}, u32[]{:S(2)}, u32[]{:S(2)}) %collective-permute-start.2) | collective-permute-done | bytes 16416 | tf_op jit(solution)/shard_map/ppermute | solution.py:407
  48.9 1.2 %final.1 = (bf16[16,16,256]{2,1,0:T(8,128)(2,1)}, f32[16,16,256]{2,1,0:T(8,128)}) custom-call(f32[192,256]{1,0:T(8,128)S(1)} %get-tuple-element.29.inner_ref, bf16[32,256]{1,0:T(8,128)(2,1)S(1)} %collective-permute-done.2.near_ref, bf16[32,256]{1,0:T(8,128)(2,1)S(1)} %collective-permute-done.3.far_ref, bf16[512,256]{1,0:T(8,128)(2,1)S(1)} %get-tuple-element.22.pick_ref, ...), custom_call_target="tpu_custom_call" | custom-call | flops 100000000 | bytes 786432 | tf_op jit(solution)/shard_map/final/pallas_call | solution.py:476
Async XLA Ops:
  0.6 22.0 %copy-start.16 = (bf16[64,256]{1,0:T(8,128)(2,1)S(1)}, bf16[64,256]{1,0:T(8,128)(2,1)}, u32[]{:S(2)}) copy-start(bf16[64,256]{1,0:T(8,128)(2,1)} %constant.27.clone.rows_ref) | copy-start | bytes 98308
  0.6 22.0 %copy-start.15 = (bf16[256,128]{1,0:T(8,128)(2,1)S(1)}, bf16[256,128]{1,0:T(8,128)(2,1)}, u32[]{:S(2)}) copy-start(bf16[256,128]{1,0:T(8,128)(2,1)} %constant.35.clone.inv_side_ref) | copy-start | bytes 196612
  0.7 22.0 %copy-start.17 = (bf16[64,64]{1,0:T(8,128)(2,1)S(1)}, bf16[64,64]{1,0:T(8,128)(2,1)}, u32[]{:S(2)}) copy-start(bf16[64,64]{1,0:T(8,128)(2,1)} %constant.29.clone.grid_ref) | copy-start | bytes 24580
  0.7 22.0 %copy-start.6 = (s32[16]{0:T(128)S(1)}, s32[16]{0:T(128)}, u32[]{:S(2)}) copy-start(s32[16]{0:T(128)} %row_ref.1) | copy-start | bytes 196
  0.7 22.0 %copy-start.5 = (f32[16]{0:T(128)S(1)}, f32[16]{0:T(128)}, u32[]{:S(2)}) copy-start(f32[16]{0:T(128)} %dose_ref.1) | copy-start | bytes 196
  0.7 22.0 %copy-start.3 = (f32[12,2,31,31]{3,1,2,0:T(2,128)S(1)}, f32[12,2,31,31]{3,1,2,0:T(2,128)}, u32[]{:S(2)}) copy-start(f32[12,2,31,31]{3,1,2,0:T(2,128)} %param.21) | copy-start | bytes 276772
  22.7 9.3 %copy-start.4 = (s32[16,2]{0,1:T(2,128)S(1)}, s32[16,2]{0,1:T(2,128)}, u32[]{:S(2)}) copy-start(s32[16,2]{0,1:T(2,128)} %param.24) | copy-start | bytes 388
  22.7 9.3 %copy-start.7 = (bf16[1536,256]{1,0:T(8,128)(2,1)S(1)}, bf16[1536,256]{1,0:T(8,128)(2,1)}, u32[]{:S(2)}) copy-start(bf16[1536,256]{1,0:T(8,128)(2,1)} %constant.32.clone.own_ref) | copy-start | bytes 2359300
  22.7 9.3 %copy-start.9 = (bf16[256,512]{1,0:T(8,128)(2,1)S(1)}, bf16[256,512]{1,0:T(8,128)(2,1)}, u32[]{:S(2)}) copy-start(bf16[256,512]{1,0:T(8,128)(2,1)} %constant.30.clone.inv_ref) | copy-start | bytes 786436
  22.7 9.3 %copy-start.10 = (bf16[512,256]{1,0:T(8,128)(2,1)S(1)}, bf16[512,256]{1,0:T(8,128)(2,1)}, u32[]{:S(2)}) copy-start(bf16[512,256]{1,0:T(8,128)(2,1)} %constant.36.clone.reach_ref) | copy-start | bytes 786436
  22.7 9.3 %copy-start.11 = (bf16[256,256]{1,0:T(8,128)(2,1)S(1)}, bf16[256,256]{1,0:T(8,128)(2,1)}, u32[]{:S(2)}) copy-start(bf16[256,256]{1,0:T(8,128)(2,1)} %constant.31.clone.across_ref) | copy-start | bytes 393220
  22.7 9.3 %copy-start.12 = (bf16[256,256]{1,0:T(8,128)(2,1)S(1)}, bf16[256,256]{1,0:T(8,128)(2,1)}, u32[]{:S(2)}) copy-start(bf16[256,256]{1,0:T(8,128)(2,1)} %constant.37.clone.tall_ref) | copy-start | bytes 393220
  22.7 9.3 %copy-start.13 = (bf16[256,256]{1,0:T(8,128)(2,1)S(1)}, bf16[256,256]{1,0:T(8,128)(2,1)}, u32[]{:S(2)}) copy-start(bf16[256,256]{1,0:T(8,128)(2,1)} %constant.33.clone.inside_ref) | copy-start | bytes 393220
  24.6 12.2 %collective-permute-start.1 = (bf16[64,256]{1,0:T(8,128)(2,1)S(1)}, bf16[64,256]{1,0:T(8,128)(2,1)S(1)}, u32[]{:S(2)}, u32[]{:S(2)}) collective-permute-start(bf16[64,256]{1,0:T(8,128)(2,1)S(1)} %get-tuple-element.21), channel_id=1, source_target_pairs={{1,2},{3,4},{5,6},{7,8},{9,10},{11,12},{13,14},{15,16},{17,18},{19... | collective-permute-start | bytes 98312 | tf_op jit(solution)/shard_map/ppermute | solution.py:407
  30.0 6.8 %collective-permute-start = (bf16[64,256]{1,0:T(8,128)(2,1)S(1)}, bf16[64,256]{1,0:T(8,128)(2,1)S(1)}, u32[]{:S(2)}, u32[]{:S(2)}) collective-permute-start(bf16[64,256]{1,0:T(8,128)(2,1)S(1)} %get-tuple-element.21), channel_id=1, source_target_pairs={{0,1},{2,3},{4,5},{6,7},{8,9},{10,11},{12,13},{14,15},{16,17},{18,... | collective-permute-start | bytes 98312 | tf_op jit(solution)/shard_map/ppermute | solution.py:407
  32.0 4.8 %copy-start.8 = (bf16[256,768]{1,0:T(8,128)(2,1)S(1)}, bf16[256,768]{1,0:T(8,128)(2,1)}, u32[]{:S(2)}) copy-start(bf16[256,768]{1,0:T(8,128)(2,1)} %constant.34.clone.rim_ref) | copy-start | bytes 1179652
  32.0 4.8 %copy-start.14 = (bf16[272,64]{1,0:T(8,128)(2,1)S(1)}, bf16[272,64]{1,0:T(8,128)(2,1)}, u32[]{:S(2)}) copy-start(bf16[272,64]{1,0:T(8,128)(2,1)} %constant.28.clone.ext_ref) | copy-start | bytes 104452
  36.9 8.4 %copy-start = (bf16[16,16,256]{2,1,0:T(8,128)(2,1)S(1)}, bf16[16,16,256]{2,1,0:T(8,128)(2,1)}, u32[]{:S(2)}) copy-start(bf16[16,16,256]{2,1,0:T(8,128)(2,1)} %target_ref.3) | copy-start | bytes 393220
  36.9 8.4 %copy-start.1 = (bf16[16,16,256]{2,1,0:T(8,128)(2,1)S(1)}, bf16[16,16,256]{2,1,0:T(8,128)(2,1)}, u32[]{:S(2)}) copy-start(bf16[16,16,256]{2,1,0:T(8,128)(2,1)} %mask_ref.1) | copy-start | bytes 393220
  36.9 8.3 %copy-start.2 = (bf16[32,32]{1,0:T(8,128)(2,1)S(1)}, bf16[32,32]{1,0:T(8,128)(2,1)}, u32[]{:S(2)}) copy-start(bf16[32,32]{1,0:T(8,128)(2,1)} %constant.38.clone.down_ref) | copy-start | bytes 6148
  38.4 9.0 %collective-permute-start.3 = (bf16[32,256]{1,0:T(8,128)(2,1)S(1)}, bf16[32,256]{1,0:T(8,128)(2,1)S(1)}, u32[]{:S(2)}, u32[]{:S(2)}) collective-permute-start(bf16[32,256]{1,0:T(8,128)(2,1)S(1)} %get-tuple-element.30), channel_id=1, source_target_pairs={{1,2},{3,4},{5,6},{7,8},{9,10},{11,12},{13,14},{15,16},{17,18},{19... | collective-permute-start | bytes 49160 | tf_op jit(solution)/shard_map/ppermute | solution.py:407
  43.3 5.6 %collective-permute-start.2 = (bf16[32,256]{1,0:T(8,128)(2,1)S(1)}, bf16[32,256]{1,0:T(8,128)(2,1)S(1)}, u32[]{:S(2)}, u32[]{:S(2)}) collective-permute-start(bf16[32,256]{1,0:T(8,128)(2,1)S(1)} %get-tuple-element.30), channel_id=1, source_target_pairs={{0,1},{2,3},{4,5},{6,7},{8,9},{10,11},{12,13},{14,15},{16,17},{18,... | collective-permute-start | bytes 49160 | tf_op jit(solution)/shard_map/ppermute | solution.py:407

commit v5 on v4

--- a/solution.py
+++ b/solution.py
@@ -83,9 +83,12 @@
     for g in range(USED):
         own[128 * g : 128 * (g + 1), 16 * g : 16 * (g + 1)] = wide[:, side]
     t["own"] = bf16(own)
-    full = np.concatenate([np.tile(cos, (1, 4)), np.tile(-sin, (1, 4))], 1) / 16.0
-    inside = full.copy()
-    inside[side] = 0.0
+    inside = np.zeros((4 * EDGE, 256))
+    for i in range(4):
+        r, c = slice(EDGE * i, EDGE * (i + 1)), 32 * i
+        inside[r, c : c + 32] = cos / 16.0
+        inside[r, 128 + c : 128 + c + 32] = -sin / 16.0
+        inside[EDGE * i + side] = 0.0
     t["inside"] = bf16(inside)
     rim = np.zeros((256, 768))
     for g in range(USED):
@@ -245,22 +248,22 @@
 
 
 def first_kernel(all_ref, rows_ref, plane_ref, grid_ref, inv_side_ref, dose_ref, row_ref,
-                 held_ref, bands_ref, base_ref, kernels_ref, slot_ref, narrow_ref):
+                 held_ref, bands_ref, kernels_ref, slot_ref, narrow_ref):
     lay_kernels(plane_ref, kernels_ref)
     lay_slots(dose_ref, row_ref, slot_ref, narrow_ref)
-    inner = dot(rows_ref[...], all_ref[...])
-    base_ref[...] = inner[:, 768:]
-    side_columns(inner[:, :768], kernels_ref, grid_ref[...], inv_side_ref, narrow_ref, held_ref, bands_ref)
-
-
-def inside_kernel(held_ref, inv_ref, slot_ref, tall_ref, across_ref, rows_ref, inside_ref, base_ref, own_ref,
-                  reach_ref, side_ref, part_ref, edge_ref, mine_ref, pick_ref, cells_ref, blurred, turned):
+    inner = dot(rows_ref[...], all_ref[:, :768])
+    side_columns(inner, kernels_ref, grid_ref[...], inv_side_ref, narrow_ref, held_ref, bands_ref)
+
+
+def inside_kernel(held_ref, inv_ref, slot_ref, tall_ref, across_ref, rows_ref, inside_ref, all_ref, own_ref,
+                  reach_ref, side_ref, part_ref, edge_ref, mine_ref, pick_ref, cells_ref, blurred, resist_ref):
     lay_pick(side_ref, reach_ref, pick_ref)
     for j in range(GROUPS):
         cells_ref[:, 512 * j : 512 * (j + 1)] = coarse_group(held_ref, j, COARSE, inv_ref, slot_ref)
     cells = cells_ref[...]
-    above = pltpu.roll(cells, 128, 1) * slot_ref[1:2, :]
-    below = pltpu.roll(cells, 128 * (USED - 1), 1) * slot_ref[2:3, :]
+    lanes = 128 * USED
+    above = jnp.concatenate([cells[:, lanes - 128 :], cells[:, : lanes - 128]], 1) * slot_ref[1:2, :]
+    below = jnp.concatenate([cells[:, 128:], cells[:, :128]], 1) * slot_ref[2:3, :]
     main = cells.astype(BF)
     edge_ref[...] = dot(main, own_ref[...])
     blurred[...] = dot(tall_ref[...], jnp.concatenate([main, above.astype(BF), below.astype(BF), main], 0)).astype(BF)
@@ -269,15 +272,16 @@
     for g in range(USED):
         one = blurred[:, 128 * g : 128 * (g + 1)]
         fine = dot(jnp.concatenate([one, one], 1), across_ref[...])
-        turned[64 * g : 64 * (g + 1), :] = dot(rows_ref[...], resist_of(fine).astype(BF)).astype(BF)
-    both = dot(turned[...], inside_ref[...])
-    place = lane_block(256, 32) % 4
+        resist_ref[:, EDGE * g : EDGE * (g + 1)] = resist_of(fine).astype(BF)
     half = 32 * USED
     for j in range(GROUPS):
-        total = four_slots([both[64 * (4 * j + i) : 64 * (4 * j + i + 1)] for i in range(4)], place)
-        for n, first_lane in enumerate((128 * j, half + 128 * j)):
-            lanes = slice(first_lane, first_lane + 128)
-            part_ref[:, lanes] = base_ref[:, lanes] - STEP_GAIN * total[:, 128 * n : 128 * (n + 1)]
+        change = dot(resist_ref[:, 4 * EDGE * j : 4 * EDGE * (j + 1)], inside_ref[...])
+        firsts = (128 * j, half + 128 * j)
+        before = jnp.concatenate([all_ref[:, 768 + f : 896 + f] for f in firsts], 1)
+        y_part = (before.astype(F32) - STEP_GAIN * change).astype(BF)
+        total = dot(rows_ref[...], y_part)
+        for n, f in enumerate(firsts):
+            part_ref[:, f : f + 128] = total[:, 128 * n : 128 * (n + 1)]
 
 
 def lent(near_ref, far_ref, pick_ref):
@@ -422,13 +426,12 @@
         grant=62 * 2**20,
     )(mask, target, t["cols"])
     rows_all = lax.all_gather(y, "segment", axis=0, tiled=True)
-    held, bands, base, kernels, slot, narrow = call(
+    held, bands, kernels, slot, narrow = call(
         first_kernel,
         [VMEM] * 5 + [SMEM] * 2,
         [
             shape((GROUPS, NK * COARSE, 256), BF),
             shape((COARSE, 256), BF),
-            shape((64, 64 * USED), F32),
             shape((NK, 2, 32, 128), F32),
             shape((8, 128 * USED), F32),
             shape((8, 128 * GROUPS), F32),
@@ -451,10 +454,10 @@
         [
             pltpu.VMEM((COARSE, 128 * USED), F32),
             pltpu.VMEM((EDGE, 128 * USED), BF),
-            pltpu.VMEM((64 * USED, EDGE), BF),
+            pltpu.VMEM((EDGE, EDGE * USED), BF),
         ],
         name="inside",
-    )(held, t["inv"], slot, t["tall"], t["across"], t["rows"], t["inside"], base, t["own"], t["reach"], side_source.T)
+    )(held, t["inv"], slot, t["tall"], t["across"], t["rows"], t["inside"], rows_all, t["own"], t["reach"], side_source.T)
     held, bands, mine_side = call(
         second_kernel,
         [VMEM] * 12,

time: 50.3 us -> 49 us (0.974)
  Pallas kernels: 12.1 us -> 10.7 us
    pallas_call x1, Pallas kernels: 4.77 us -> 3.43 us  [body(): call(inside_kernel, [VMEM] * 10 + [SMEM], [shape((64, 64 * USED), F32), s...]
  transfers between devices with their start and end apart: 4 -> 4, of which waited for: 2 -> 3; matrix products, arithmetic and copies ran while one was open for 0% -> 0% of each run, Pallas kernels for 11% -> 9%
where the time goes in v5:
time: 49 us; the launch traced here: 48.8 us
  blocking collectives  20 us (41%)
  starting transfers between devices  13.8 us (28%)
  Pallas kernels  10.7 us (22%)
  waiting for transfers between devices  3.18 us (6%)
  between operations  0.95 us (2%)
    all_gather x1, blocking collectives, body(): rows_all = lax.all_gather(y, 'segment', axis=0, tiled=True)  20 us
    ppermute x4, starting transfers between devices, swapped(): return lax.ppermute(block, 'tile', pairs + [(j, i) for i, j in pairs])  13.8 us
    pallas_call x1, Pallas kernels, body(): call(inside_kernel, [VMEM] * 10 + [SMEM], [shape((64, 64 * USED), F32), s...  3.43 us
    ppermute x4, waiting for transfers between devices, swapped(): return lax.ppermute(block, 'tile', pairs + [(j, i) for i, j in pairs])  3.18 us
    pallas_call x1, Pallas kernels, body(): call(start_kernel, [HBM] * 3, [shape((ROWS, 128 * USED), BF)], 10 ** 8, [...  1.92 us
    pallas_call x1, Pallas kernels, body(): call(first_kernel, [VMEM] * 5 + [SMEM] * 2, [shape((GROUPS, NK * COARSE,...  1.86 us
    pallas_call x1, Pallas kernels, body(): call(second_kernel, [VMEM] * 12, [shape((GROUPS, NK * EXT, 256), BF), sha...  1.49 us
    pallas_call x1, Pallas kernels, body(): call(final_kernel, [VMEM] * 8, [shape((SLOTS, ROWS, EDGE), BF), shape((SL...  1.21 us
  transfers between devices with their start and end apart: 4, of which 3 were waited for; matrix products, arithmetic and copies ran while one was open for 0% of the time, Pallas kernels for 9%

profile of v5, /device:TPU:198, one launch (start us, length us, event | category | flops | bytes accessed | tf_op | source)
XLA Modules:
  0.0 48.8 jit_solution(14115262619685533187)
XLA Ops:
  0.6 0.0 copy-start.8
  0.6 0.0 copy-start.16
  0.7 0.0 copy-start.17
  0.7 0.0 copy-start.13
  0.7 0.0 copy-start.12
  0.7 0.0 copy-start.11
  0.7 1.9 %start.1 = bf16[16,1536]{1,0:T(8,128)(2,1)} custom-call(bf16[16,16,256]{2,1,0:T(8,128)(2,1)} %mask_ref.1, bf16[16,16,256]{2,1,0:T(8,128)(2,1)} %target_ref.3, bf16[256,256]{1,0:T(8,128)(2,1)} %constant.26.clone.cols_hbm), custom_call_target="tpu_custom_call" | custom-call | flops 100000000 | bytes 98304 | tf_op jit(solution)/shard_map/start/pallas_call | solution.py:419
  2.6 20.0 %all_gather.3.all_ref = bf16[256,1536]{1,0:T(8,128)(2,1)S(1)} all-gather(bf16[16,1536]{1,0:T(8,128)(2,1)} %start.1), channel_id=1, replica_groups=mesh['segment'=16,'tile'=32] {'segment'}, dimensions={0}, use_global_device_ids=true | all-gather | bytes 835584 | tf_op jit(solution)/shard_map/all_gather | solution.py:428
  22.6 0.0 copy-done.8
  22.6 0.0 copy-done.16
  22.6 0.0 copy-done.17
  22.6 0.0 copy-done.13
  22.6 0.0 copy-done.12
  22.6 0.0 copy-done.11
  22.7 0.0 copy-start
  22.7 0.0 copy-start.1
  22.7 0.0 copy-start.3
  22.7 0.0 copy-start.4
  22.7 0.0 copy-start.6
  22.7 0.0 copy-start.7
  22.7 0.0 copy-start.10
  22.7 1.9 %first.1 = (bf16[3,768,256]{2,1,0:T(8,128)(2,1)S(1)}, bf16[64,256]{1,0:T(8,128)(2,1)S(1)}, f32[12,2,32,128]{3,2,1,0:T(8,128)S(1)}, f32[8,1536]{1,0:T(8,128)S(1)}, f32[8,384]{1,0:T(8,128)S(1)}) custom-call(bf16[256,1536]{1,0:T(8,128)(2,1)S(1)} %all_gather.3.all_ref, bf16[64,256]{1,0:T(8,128)(2,1)S(1)} %copy-done.8, f32[744,31]{1,0:T(8,128)S(1)} %bitcast.5, ...), custom_call_target="tpu_custom_call" | custom-call | flops 1000000000 | bytes 3334144 | tf_op jit(solution)/shard_map/first/pallas_call | solution.py:429
  24.6 5.4 %collective-permute-start.1 = (bf16[64,256]{1,0:T(8,128)(2,1)S(1)}, bf16[64,256]{1,0:T(8,128)(2,1)S(1)}, u32[]{:S(2)}, u32[]{:S(2)}) collective-permute-start(bf16[64,256]{1,0:T(8,128)(2,1)S(1)} %get-tuple-element.19), channel_id=1, source_target_pairs={{1,2},{3,4},{5,6},{7,8},{9,10},{11,12},{13,14},{15,16},{17,18},{19... | collective-permute-start | bytes 98312 | tf_op jit(solution)/shard_map/ppermute | solution.py:411
  30.0 1.9 %collective-permute-start = (bf16[64,256]{1,0:T(8,128)(2,1)S(1)}, bf16[64,256]{1,0:T(8,128)(2,1)S(1)}, u32[]{:S(2)}, u32[]{:S(2)}) collective-permute-start(bf16[64,256]{1,0:T(8,128)(2,1)S(1)} %get-tuple-element.19), channel_id=1, source_target_pairs={{0,1},{2,3},{4,5},{6,7},{8,9},{10,11},{12,13},{14,15},{16,17},{18,... | collective-permute-start | bytes 98312 | tf_op jit(solution)/shard_map/ppermute | solution.py:411
  31.9 0.0 copy-done
  31.9 0.0 copy-done.1
  32.0 0.0 copy-done.3
  32.0 0.0 copy-done.4
  32.0 0.0 copy-done.6
  32.0 0.0 copy-done.7
  32.0 0.0 copy-done.10
  32.0 0.0 copy-start.14
  32.0 0.0 copy-start.15
  32.0 3.4 %inside.1 = (f32[64,768]{1,0:T(8,128)S(1)}, f32[64,256]{1,0:T(8,128)S(1)}, bf16[16,1536]{1,0:T(8,128)(2,1)S(1)}, bf16[512,256]{1,0:T(8,128)(2,1)S(1)}) custom-call(bf16[3,768,256]{2,1,0:T(8,128)(2,1)S(1)} %get-tuple-element.16.held_ref, bf16[256,512]{1,0:T(8,128)(2,1)S(1)} %copy-done.3, f32[8,1536]{1,0:T(8,128)S(1)} %get-tuple-element.17.slot_ref, ...), custom_call_target="tpu_custom_call" | custom-call | flops 1000000000 | bytes 1146880 | tf_op jit(solution)/shard_map/inside/pallas_call | solution.py:444
  35.5 0.0 collective-permute-done.1.far_ref
  35.5 0.3 collective-permute-done.near_ref
  35.8 0.0 copy-done.14
  35.8 0.0 copy-done.15
  35.8 0.0 copy-start.2
  35.8 0.0 copy-start.5
  35.8 0.0 copy-start.9
  35.8 1.5 %second.1 = (bf16[3,384,256]{2,1,0:T(8,128)(2,1)S(1)}, bf16[32,256]{1,0:T(8,128)(2,1)S(1)}, f32[16,256]{1,0:T(8,128)S(1)}) custom-call(bf16[64,256]{1,0:T(8,128)(2,1)S(1)} %collective-permute-done.near_ref, bf16[64,256]{1,0:T(8,128)(2,1)S(1)} %collective-permute-done.1.far_ref, bf16[512,256]{1,0:T(8,128)(2,1)S(1)} %get-tuple-element.20.pick_ref, ...), custom_call_target="tpu_custom_call" | custom-call | flops 1000000000 | bytes 1245184 | tf_op jit(solution)/shard_map/second/pallas_call | solution.py:461
  37.3 4.6 %collective-permute-start.3 = (bf16[32,256]{1,0:T(8,128)(2,1)S(1)}, bf16[32,256]{1,0:T(8,128)(2,1)S(1)}, u32[]{:S(2)}, u32[]{:S(2)}) collective-permute-start(bf16[32,256]{1,0:T(8,128)(2,1)S(1)} %get-tuple-element.28), channel_id=1, source_target_pairs={{1,2},{3,4},{5,6},{7,8},{9,10},{11,12},{13,14},{15,16},{17,18},{19... | collective-permute-start | bytes 49160 | tf_op jit(solution)/shard_map/ppermute | solution.py:411
  41.9 1.9 %collective-permute-start.2 = (bf16[32,256]{1,0:T(8,128)(2,1)S(1)}, bf16[32,256]{1,0:T(8,128)(2,1)S(1)}, u32[]{:S(2)}, u32[]{:S(2)}) collective-permute-start(bf16[32,256]{1,0:T(8,128)(2,1)S(1)} %get-tuple-element.28), channel_id=1, source_target_pairs={{0,1},{2,3},{4,5},{6,7},{8,9},{10,11},{12,13},{14,15},{16,17},{18,... | collective-permute-start | bytes 49160 | tf_op jit(solution)/shard_map/ppermute | solution.py:411
  43.9 0.0 copy-done.2
  43.9 0.0 copy-done.5
  43.9 0.0 copy-done.9
  43.9 0.8 %local.1 = (f32[192,256]{1,0:T(8,128)S(1)}, bf16[16,16,256]{2,1,0:T(8,128)(2,1)S(1)}) custom-call(bf16[16,1536]{1,0:T(8,128)(2,1)S(1)} %get-tuple-element.18.mine_ref, f32[16,256]{1,0:T(8,128)S(1)} %get-tuple-element.25.mine_side_ref, bf16[3,384,256]{2,1,0:T(8,128)(2,1)S(1)} %get-tuple-element.26.held_ref, bf16[256,512]{1,0:T(8,128)(2,1)S(1)} %copy-done.3, ...), custom_call_target="tpu_custom_call" | custom-call | flops 1000000000 | bytes 655360 | tf_op jit(solution)/shard_map/local/pallas_call | solution.py:471
  44.7 1.6 %collective-permute-done.3.far_ref = bf16[32,256]{1,0:T(8,128)(2,1)S(1)} collective-permute-done((bf16[32,256]{1,0:T(8,128)(2,1)S(1)}, bf16[32,256]{1,0:T(8,128)(2,1)S(1)}, u32[]{:S(2)}, u32[]{:S(2)}) %collective-permute-start.3) | collective-permute-done | bytes 16416 | tf_op jit(solution)/shard_map/ppermute | solution.py:411
  46.3 1.3 %collective-permute-done.2.near_ref = bf16[32,256]{1,0:T(8,128)(2,1)S(1)} collective-permute-done((bf16[32,256]{1,0:T(8,128)(2,1)S(1)}, bf16[32,256]{1,0:T(8,128)(2,1)S(1)}, u32[]{:S(2)}, u32[]{:S(2)}) %collective-permute-start.2) | collective-permute-done | bytes 16416 | tf_op jit(solution)/shard_map/ppermute | solution.py:411
  47.6 1.2 %final.1 = (bf16[16,16,256]{2,1,0:T(8,128)(2,1)}, f32[16,16,256]{2,1,0:T(8,128)}) custom-call(f32[192,256]{1,0:T(8,128)S(1)} %get-tuple-element.27.inner_ref, bf16[32,256]{1,0:T(8,128)(2,1)S(1)} %collective-permute-done.2.near_ref, bf16[32,256]{1,0:T(8,128)(2,1)S(1)} %collective-permute-done.3.far_ref, bf16[512,256]{1,0:T(8,128)(2,1)S(1)} %get-tuple-element.20.pick_ref, ...), custom_call_target="tpu_custom_call" | custom-call | flops 100000000 | bytes 786432 | tf_op jit(solution)/shard_map/final/pallas_call | solution.py:479
Async XLA Ops:
  0.6 22.0 %copy-start.8 = (bf16[64,256]{1,0:T(8,128)(2,1)S(1)}, bf16[64,256]{1,0:T(8,128)(2,1)}, u32[]{:S(2)}) copy-start(bf16[64,256]{1,0:T(8,128)(2,1)} %constant.27.clone.rows_ref) | copy-start | bytes 98308
  0.6 22.0 %copy-start.16 = (bf16[256,128]{1,0:T(8,128)(2,1)S(1)}, bf16[256,128]{1,0:T(8,128)(2,1)}, u32[]{:S(2)}) copy-start(bf16[256,128]{1,0:T(8,128)(2,1)} %constant.35.clone.inv_side_ref) | copy-start | bytes 196612
  0.7 22.0 %copy-start.17 = (bf16[64,64]{1,0:T(8,128)(2,1)S(1)}, bf16[64,64]{1,0:T(8,128)(2,1)}, u32[]{:S(2)}) copy-start(bf16[64,64]{1,0:T(8,128)(2,1)} %constant.29.clone.grid_ref) | copy-start | bytes 24580
  0.7 22.0 %copy-start.13 = (s32[16]{0:T(128)S(1)}, s32[16]{0:T(128)}, u32[]{:S(2)}) copy-start(s32[16]{0:T(128)} %row_ref.1) | copy-start | bytes 196
  0.7 22.0 %copy-start.12 = (f32[16]{0:T(128)S(1)}, f32[16]{0:T(128)}, u32[]{:S(2)}) copy-start(f32[16]{0:T(128)} %dose_ref.1) | copy-start | bytes 196
  0.7 22.0 %copy-start.11 = (f32[12,2,31,31]{3,1,2,0:T(2,128)S(1)}, f32[12,2,31,31]{3,1,2,0:T(2,128)}, u32[]{:S(2)}) copy-start(f32[12,2,31,31]{3,1,2,0:T(2,128)} %param.21) | copy-start | bytes 276772
  22.7 9.3 %copy-start = (bf16[1536,256]{1,0:T(8,128)(2,1)S(1)}, bf16[1536,256]{1,0:T(8,128)(2,1)}, u32[]{:S(2)}) copy-start(bf16[1536,256]{1,0:T(8,128)(2,1)} %constant.32.clone.own_ref) | copy-start | bytes 2359300
  22.7 9.3 %copy-start.1 = (bf16[1024,256]{1,0:T(8,128)(2,1)S(1)}, bf16[1024,256]{1,0:T(8,128)(2,1)}, u32[]{:S(2)}) copy-start(bf16[1024,256]{1,0:T(8,128)(2,1)} %constant.33.clone.inside_ref) | copy-start | bytes 1572868
  22.7 9.3 %copy-start.3 = (bf16[256,512]{1,0:T(8,128)(2,1)S(1)}, bf16[256,512]{1,0:T(8,128)(2,1)}, u32[]{:S(2)}) copy-start(bf16[256,512]{1,0:T(8,128)(2,1)} %constant.30.clone.inv_ref) | copy-start | bytes 786436
  22.7 9.3 %copy-start.4 = (bf16[512,256]{1,0:T(8,128)(2,1)S(1)}, bf16[512,256]{1,0:T(8,128)(2,1)}, u32[]{:S(2)}) copy-start(bf16[512,256]{1,0:T(8,128)(2,1)} %constant.36.clone.reach_ref) | copy-start | bytes 786436
  22.7 9.3 %copy-start.6 = (bf16[256,256]{1,0:T(8,128)(2,1)S(1)}, bf16[256,256]{1,0:T(8,128)(2,1)}, u32[]{:S(2)}) copy-start(bf16[256,256]{1,0:T(8,128)(2,1)} %constant.31.clone.across_ref) | copy-start | bytes 393220
  22.7 9.3 %copy-start.7 = (bf16[256,256]{1,0:T(8,128)(2,1)S(1)}, bf16[256,256]{1,0:T(8,128)(2,1)}, u32[]{:S(2)}) copy-start(bf16[256,256]{1,0:T(8,128)(2,1)} %constant.37.clone.tall_ref) | copy-start | bytes 393220
  22.7 9.3 %copy-start.10 = (s32[16,2]{0,1:T(2,128)S(1)}, s32[16,2]{0,1:T(2,128)}, u32[]{:S(2)}) copy-start(s32[16,2]{0,1:T(2,128)} %param.24) | copy-start | bytes 388
  24.6 10.9 %collective-permute-start.1 = (bf16[64,256]{1,0:T(8,128)(2,1)S(1)}, bf16[64,256]{1,0:T(8,128)(2,1)S(1)}, u32[]{:S(2)}, u32[]{:S(2)}) collective-permute-start(bf16[64,256]{1,0:T(8,128)(2,1)S(1)} %get-tuple-element.19), channel_id=1, source_target_pairs={{1,2},{3,4},{5,6},{7,8},{9,10},{11,12},{13,14},{15,16},{17,18},{19... | collective-permute-start | bytes 98312 | tf_op jit(solution)/shard_map/ppermute | solution.py:411
  30.0 5.8 %collective-permute-start = (bf16[64,256]{1,0:T(8,128)(2,1)S(1)}, bf16[64,256]{1,0:T(8,128)(2,1)S(1)}, u32[]{:S(2)}, u32[]{:S(2)}) collective-permute-start(bf16[64,256]{1,0:T(8,128)(2,1)S(1)} %get-tuple-element.19), channel_id=1, source_target_pairs={{0,1},{2,3},{4,5},{6,7},{8,9},{10,11},{12,13},{14,15},{16,17},{18,... | collective-permute-start | bytes 98312 | tf_op jit(solution)/shard_map/ppermute | solution.py:411
  32.0 3.8 %copy-start.14 = (bf16[256,768]{1,0:T(8,128)(2,1)S(1)}, bf16[256,768]{1,0:T(8,128)(2,1)}, u32[]{:S(2)}) copy-start(bf16[256,768]{1,0:T(8,128)(2,1)} %constant.34.clone.rim_ref) | copy-start | bytes 1179652
  32.0 3.8 %copy-start.15 = (bf16[272,64]{1,0:T(8,128)(2,1)S(1)}, bf16[272,64]{1,0:T(8,128)(2,1)}, u32[]{:S(2)}) copy-start(bf16[272,64]{1,0:T(8,128)(2,1)} %constant.28.clone.ext_ref) | copy-start | bytes 104452
  35.8 8.0 %copy-start.2 = (bf16[16,16,256]{2,1,0:T(8,128)(2,1)S(1)}, bf16[16,16,256]{2,1,0:T(8,128)(2,1)}, u32[]{:S(2)}) copy-start(bf16[16,16,256]{2,1,0:T(8,128)(2,1)} %target_ref.3) | copy-start | bytes 393220
  35.8 8.0 %copy-start.5 = (bf16[16,16,256]{2,1,0:T(8,128)(2,1)S(1)}, bf16[16,16,256]{2,1,0:T(8,128)(2,1)}, u32[]{:S(2)}) copy-start(bf16[16,16,256]{2,1,0:T(8,128)(2,1)} %mask_ref.1) | copy-start | bytes 393220
  35.8 8.0 %copy-start.9 = (bf16[32,32]{1,0:T(8,128)(2,1)S(1)}, bf16[32,32]{1,0:T(8,128)(2,1)}, u32[]{:S(2)}) copy-start(bf16[32,32]{1,0:T(8,128)(2,1)} %constant.38.clone.down_ref) | copy-start | bytes 6148
  37.3 9.0 %collective-permute-start.3 = (bf16[32,256]{1,0:T(8,128)(2,1)S(1)}, bf16[32,256]{1,0:T(8,128)(2,1)S(1)}, u32[]{:S(2)}, u32[]{:S(2)}) collective-permute-start(bf16[32,256]{1,0:T(8,128)(2,1)S(1)} %get-tuple-element.28), channel_id=1, source_target_pairs={{1,2},{3,4},{5,6},{7,8},{9,10},{11,12},{13,14},{15,16},{17,18},{19... | collective-permute-start | bytes 49160 | tf_op jit(solution)/shard_map/ppermute | solution.py:411
  41.9 5.6 %collective-permute-start.2 = (bf16[32,256]{1,0:T(8,128)(2,1)S(1)}, bf16[32,256]{1,0:T(8,128)(2,1)S(1)}, u32[]{:S(2)}, u32[]{:S(2)}) collective-permute-start(bf16[32,256]{1,0:T(8,128)(2,1)S(1)} %get-tuple-element.28), channel_id=1, source_target_pairs={{0,1},{2,3},{4,5},{6,7},{8,9},{10,11},{12,13},{14,15},{16,17},{18,... | collective-permute-start | bytes 49160 | tf_op jit(solution)/shard_map/ppermute | solution.py:411

commit v6 on v5

--- a/solution.py
+++ b/solution.py
@@ -50,9 +50,9 @@
     t["cols"] = bf16(np.concatenate([np.tile(cos, (1, 4)), np.tile(-sin, (1, 4))], 1) / 16.0)
     t["rows"] = bf16(np.concatenate([cos, sin], 1).T / 16.0)
     ext_cos, ext_sin = waves((np.arange(EDGE + 2 * RB) - RB) % EDGE)
-    t["ext"] = bf16(np.concatenate([ext_cos, ext_sin], 1))
+    t["ext"] = bf16(np.concatenate([ext_cos, -ext_sin, ext_sin, ext_cos], 1))
     c_cos, c_sin = waves(np.arange(COARSE) * (EDGE // COARSE))
-    t["grid"] = bf16(np.concatenate([c_cos, c_sin], 1))
+    t["grid"] = bf16(np.block([[c_cos, -c_sin], [c_sin, c_cos]]))
     inv = np.zeros((256, 512))
     for i in range(4):
         r, c = slice(32 * i, 32 * i + 32), 128 * i
@@ -150,9 +150,10 @@
     ]
     for copy in copies:
         copy.start()
-    for copy in copies:
-        copy.wait()
+    copies[0].wait()
+    copies[1].wait()
     of_mask = dot(mask_ref[...].reshape(USED * ROWS, EDGE), cols_ref[...])
+    copies[2].wait()
     of_target = dot(target_ref[...].reshape(USED * ROWS, EDGE), cols_ref[...])
     place = lane_block(256, 32) % 4
     for n, both in enumerate((of_mask, of_mask + STEP_GAIN * of_target)):
@@ -181,13 +182,14 @@
     weight, up, down = (jnp.zeros((1, 128 * USED), F32) for _ in range(3))
     up_narrow, down_narrow = (jnp.zeros((1, 256), F32) for _ in range(2))
     weight_quarter = jnp.zeros((1, 128 * GROUPS), F32)
+    rows, doses = row_ref[...], dose_ref[...]
     for g in range(USED):
-        row = row_ref[g]
-        scale = jnp.where(row >= 0, dose_ref[g], 0.0) * (1.0 / (NK * KF * KF))
+        row = rows[:, g : g + 1]
+        scale = jnp.where(row >= 0, doses[:, g : g + 1], 0.0) * (1.0 / (NK * KF * KF))
         weight = jnp.where(wide == g, scale, weight)
         weight_quarter = jnp.where(quarter == g, scale, weight_quarter)
         if g > 0:
-            before = row_ref[g - 1]
+            before = rows[:, g - 1 : g]
             joined = jnp.where((before >= 0) & (row >= 0) & (before == row - 1), 1.0, 0.0)
             up = jnp.where(wide == g, joined, up)
             down = jnp.where(wide == g - 1, joined, down)
@@ -209,30 +211,33 @@
     narrow = lane_block(256, 2 * RB)
     row = lax.broadcasted_iota(jnp.int32, (256, 1), 0)
     source = jnp.where(row < 128, row // 32 + 4 * ((row // 16) % 2), 8 + (row - 128) // 32)
+    sources = side_ref[...]
     for n in range(2):
         wanted = jnp.full((1, 256), -1, jnp.int32)
         for g in range(USED):
-            wanted = jnp.where(narrow == g, side_ref[n, g], wanted)
+            wanted = jnp.where(narrow == g, sources[n : n + 1, g : g + 1], wanted)
         rows = slice(256 * n, 256 * (n + 1))
         pick_ref[rows, :] = jnp.where(source == wanted, reach_ref[rows, :].astype(F32), 0.0).astype(BF)
 
 
 def side_columns(inner, kernels_ref, points, inv_side_ref, narrow_ref, held, bands_ref):
-    count = points.shape[0]
+    count = points.shape[0] // 2
     half = 32 * USED
     sides = []
     for j in range(GROUPS):
         lanes, more = slice(128 * j, 128 * (j + 1)), slice(half + 128 * j, half + 128 * (j + 1))
         re = inner[:32, lanes] + inner[32:, more]
         im = inner[:32, more] - inner[32:, lanes]
-        for k in range(NK):
-            k_re, k_im = kernels_ref[k, 0], kernels_ref[k, 1]
-            p_re = k_re * re - k_im * im
-            p_im = k_re * im + k_im * re
-            block = jnp.concatenate(
-                [jnp.concatenate([p_re, p_im], 1), jnp.concatenate([-p_im, p_re], 1)], 0
-            ).astype(BF)
-            held[j, k * count : (k + 1) * count, :] = dot(points, block).astype(BF)
+        for k in range(0, NK, 2):
+            pair = []
+            for n in (k, k + 1):
+                k_re, k_im = kernels_ref[n, 0], kernels_ref[n, 1]
+                pair.append(jnp.concatenate([k_re * re - k_im * im, k_re * im + k_im * re], 0).astype(BF))
+            both = dot(points, jnp.concatenate(pair, 1)).astype(BF)
+            for n in range(2):
+                rows, lane = slice((k + n) * count, (k + n + 1) * count), 128 * n
+                held[j, rows, :128] = both[:count, lane : lane + 128]
+                held[j, rows, 128:] = both[count:, lane : lane + 128]
         field = dot(held[j], inv_side_ref[...])
         squares = jnp.sum((field * field).reshape(NK, count, 128), axis=0)
         sides.append((squares + pltpu.roll(squares, 112, 1)) * narrow_ref[2:3, lanes])
@@ -303,7 +308,9 @@
     mine_side_ref[...] = blurred[pl.ds(first, ROWS), :]
     turned = dot(rows_ref[...], resist_of(fine).astype(BF)).astype(BF)
     inner = part_ref[...] - STEP_GAIN * dot(turned, rim_ref[...])
-    side_columns(inner, kernels_ref, ext_ref[pl.ds(first, EXT), :], inv_side_ref, narrow_ref, held_ref, bands_ref)
+    ext = ext_ref[pl.ds(first, EXT), :]
+    points = jnp.concatenate([ext[:, :64], ext[:, 64:]], 0)
+    side_columns(inner, kernels_ref, points, inv_side_ref, narrow_ref, held_ref, bands_ref)
 
 
 def resist_of(blurred):
@@ -388,7 +395,6 @@
 
 
 VMEM = pl.BlockSpec(memory_space=pltpu.VMEM)
-SMEM = pl.BlockSpec(memory_space=pltpu.SMEM)
 HBM = pl.BlockSpec(memory_space=pltpu.HBM)
 
 
@@ -428,7 +434,7 @@
     rows_all = lax.all_gather(y, "segment", axis=0, tiled=True)
     held, bands, kernels, slot, narrow = call(
         first_kernel,
-        [VMEM] * 5 + [SMEM] * 2,
+        [VMEM] * 7,
         [
             shape((GROUPS, NK * COARSE, 256), BF),
             shape((COARSE, 256), BF),
@@ -438,12 +444,12 @@
         ],
         10**9,
         name="first",
-    )(rows_all, t["rows"], plane, t["grid"], t["inv_side"], dose, slot_row)
+    )(rows_all, t["rows"], plane, t["grid"], t["inv_side"], dose.reshape(1, SLOTS), slot_row.reshape(1, SLOTS))
     from_near = swapped(bands, 0)
     from_far = swapped(bands, 1)
     part, edge, mine, pick = call(
         inside_kernel,
-        [VMEM] * 10 + [SMEM],
+        [VMEM] * 11,
         [
             shape((64, 64 * USED), F32),
             shape((COARSE, 256), F32),

time: 49 us -> 48.1 us (0.982)
  Pallas kernels: 10.7 us -> 9.81 us
  waiting for transfers between devices: 3.18 us -> 3.76 us
  starting transfers between devices: 13.8 us -> 13.3 us
    pallas_call x2, Pallas kernels: 5.29 us -> 4.15 us  [the longest x1 2.85 us: body(): call(inside_kernel, [VMEM] * 11, [shape((64, 64 * USED), F32), shape((COA...]
    ppermute x4, waiting for transfers between devices: 3.18 us -> 3.76 us  [swapped(): return lax.ppermute(block, 'tile', pairs + [(j, i) for i, j in pairs])]
    ppermute x4, starting transfers between devices: 13.8 us -> 13.3 us  [swapped(): return lax.ppermute(block, 'tile', pairs + [(j, i) for i, j in pairs])]
  transfers between devices with their start and end apart: 4 -> 4, of which waited for: 3 -> 3; matrix products, arithmetic and copies ran while one was open for 0% -> 0% of each run, Pallas kernels for 9% -> 8%
where the time goes in v6:
time: 48.1 us; the launch traced here: 47.9 us
  blocking collectives  20 us (42%)
  starting transfers between devices  13.3 us (28%)
  Pallas kernels  9.81 us (20%)
  waiting for transfers between devices  3.76 us (8%)
  between operations  0.95 us (2%)
    all_gather x1, blocking collectives, body(): rows_all = lax.all_gather(y, 'segment', axis=0, tiled=True)  20 us
    ppermute x4, starting transfers between devices, swapped(): return lax.ppermute(block, 'tile', pairs + [(j, i) for i, j in pairs])  13.3 us
    ppermute x4, waiting for transfers between devices, swapped(): return lax.ppermute(block, 'tile', pairs + [(j, i) for i, j in pairs])  3.76 us
    pallas_call x1, Pallas kernels, body(): call(inside_kernel, [VMEM] * 11, [shape((64, 64 * USED), F32), shape((COA...  2.85 us
    pallas_call x1, Pallas kernels, body(): call(start_kernel, [HBM] * 3, [shape((ROWS, 128 * USED), BF)], 10 ** 8, [...  2.05 us
    pallas_call x1, Pallas kernels, body(): call(second_kernel, [VMEM] * 12, [shape((GROUPS, NK * EXT, 256), BF), sha...  1.58 us
    pallas_call x1, Pallas kernels, body(): call(first_kernel, [VMEM] * 7, [shape((GROUPS, NK * COARSE, 256), BF), sh...  1.29 us
    pallas_call x1, Pallas kernels, body(): call(final_kernel, [VMEM] * 8, [shape((SLOTS, ROWS, EDGE), BF), shape((SL...  1.21 us
  transfers between devices with their start and end apart: 4, of which 3 were waited for; matrix products, arithmetic and copies ran while one was open for 0% of the time, Pallas kernels for 8%

profile of v6, /device:TPU:198, one launch (start us, length us, event | category | flops | bytes accessed | tf_op | source)
XLA Modules:
  0.0 47.9 jit_solution(9995779202360603539)
XLA Ops:
  0.6 0.0 copy-start.8
  0.6 0.0 copy-start.16
  0.7 0.0 copy-start.17
  0.7 0.0 copy-start.13
  0.7 0.0 copy-start.12
  0.7 0.0 copy-start.11
  0.7 2.1 %start.1 = bf16[16,1536]{1,0:T(8,128)(2,1)} custom-call(bf16[16,16,256]{2,1,0:T(8,128)(2,1)} %mask_ref.1, bf16[16,16,256]{2,1,0:T(8,128)(2,1)} %target_ref.3, bf16[256,256]{1,0:T(8,128)(2,1)} %constant.26.clone.cols_hbm), custom_call_target="tpu_custom_call" | custom-call | flops 100000000 | bytes 98304 | tf_op jit(solution)/shard_map/start/pallas_call | solution.py:425
  2.8 20.0 %all_gather.3.all_ref = bf16[256,1536]{1,0:T(8,128)(2,1)S(1)} all-gather(bf16[16,1536]{1,0:T(8,128)(2,1)} %start.1), channel_id=1, replica_groups=mesh['segment'=16,'tile'=32] {'segment'}, dimensions={0}, use_global_device_ids=true | all-gather | bytes 835584 | tf_op jit(solution)/shard_map/all_gather | solution.py:434
  22.7 0.0 copy-done.8
  22.8 0.0 copy-done.16
  22.8 0.0 copy-done.17
  22.8 0.0 copy-done.13
  22.8 0.0 copy-done.12
  22.8 0.0 copy-done.11
  22.8 0.0 copy-start
  22.8 0.0 copy-start.1
  22.8 0.0 copy-start.3
  22.8 0.0 copy-start.4
  22.8 0.0 copy-start.6
  22.9 0.0 copy-start.7
  22.9 0.0 copy-start.10
  22.9 1.3 %first.1 = (bf16[3,768,256]{2,1,0:T(8,128)(2,1)S(1)}, bf16[64,256]{1,0:T(8,128)(2,1)S(1)}, f32[12,2,32,128]{3,2,1,0:T(8,128)S(1)}, f32[8,1536]{1,0:T(8,128)S(1)}, f32[8,384]{1,0:T(8,128)S(1)}) custom-call(bf16[256,1536]{1,0:T(8,128)(2,1)S(1)} %all_gather.3.all_ref, bf16[64,256]{1,0:T(8,128)(2,1)S(1)} %copy-done.8, f32[744,31]{1,0:T(8,128)S(1)} %bitcast.7, ...), custom_call_target="tpu_custom_call" | custom-call | flops 1000000000 | bytes 3334144 | tf_op jit(solution)/shard_map/first/pallas_call | solution.py:435
  24.2 5.4 %collective-permute-start.1 = (bf16[64,256]{1,0:T(8,128)(2,1)S(1)}, bf16[64,256]{1,0:T(8,128)(2,1)S(1)}, u32[]{:S(2)}, u32[]{:S(2)}) collective-permute-start(bf16[64,256]{1,0:T(8,128)(2,1)S(1)} %get-tuple-element.19), channel_id=1, source_target_pairs={{1,2},{3,4},{5,6},{7,8},{9,10},{11,12},{13,14},{15,16},{17,18},{19... | collective-permute-start | bytes 98312 | tf_op jit(solution)/shard_map/ppermute | solution.py:417
  29.6 1.9 %collective-permute-start = (bf16[64,256]{1,0:T(8,128)(2,1)S(1)}, bf16[64,256]{1,0:T(8,128)(2,1)S(1)}, u32[]{:S(2)}, u32[]{:S(2)}) collective-permute-start(bf16[64,256]{1,0:T(8,128)(2,1)S(1)} %get-tuple-element.19), channel_id=1, source_target_pairs={{0,1},{2,3},{4,5},{6,7},{8,9},{10,11},{12,13},{14,15},{16,17},{18,... | collective-permute-start | bytes 98312 | tf_op jit(solution)/shard_map/ppermute | solution.py:417
  31.5 0.0 copy-done
  31.5 0.0 copy-done.1
  31.5 0.0 copy-done.3
  31.5 0.0 copy-done.4
  31.6 0.0 copy-done.6
  31.6 0.0 copy-done.7
  31.6 0.0 copy-done.10
  31.6 0.0 copy-start.14
  31.6 0.0 copy-start.15
  31.6 2.9 %inside.1 = (f32[64,768]{1,0:T(8,128)S(1)}, f32[64,256]{1,0:T(8,128)S(1)}, bf16[16,1536]{1,0:T(8,128)(2,1)S(1)}, bf16[512,256]{1,0:T(8,128)(2,1)S(1)}) custom-call(bf16[3,768,256]{2,1,0:T(8,128)(2,1)S(1)} %get-tuple-element.16.held_ref, bf16[256,512]{1,0:T(8,128)(2,1)S(1)} %copy-done.3, f32[8,1536]{1,0:T(8,128)S(1)} %get-tuple-element.17.slot_ref, ...), custom_call_target="tpu_custom_call" | custom-call | flops 1000000000 | bytes 1146880 | tf_op jit(solution)/shard_map/inside/pallas_call | solution.py:450
  34.5 0.0 collective-permute-done.1.far_ref
  34.5 0.9 %collective-permute-done.near_ref = bf16[64,256]{1,0:T(8,128)(2,1)S(1)} collective-permute-done((bf16[64,256]{1,0:T(8,128)(2,1)S(1)}, bf16[64,256]{1,0:T(8,128)(2,1)S(1)}, u32[]{:S(2)}, u32[]{:S(2)}) %collective-permute-start) | collective-permute-done | bytes 32800 | tf_op jit(solution)/shard_map/ppermute | solution.py:417
  35.4 0.0 copy-done.14
  35.4 0.0 copy-done.15
  35.4 0.0 copy-start.2
  35.4 0.0 copy-start.5
  35.4 0.0 copy-start.9
  35.4 1.6 %second.1 = (bf16[3,384,256]{2,1,0:T(8,128)(2,1)S(1)}, bf16[32,256]{1,0:T(8,128)(2,1)S(1)}, f32[16,256]{1,0:T(8,128)S(1)}) custom-call(bf16[64,256]{1,0:T(8,128)(2,1)S(1)} %collective-permute-done.near_ref, bf16[64,256]{1,0:T(8,128)(2,1)S(1)} %collective-permute-done.1.far_ref, bf16[512,256]{1,0:T(8,128)(2,1)S(1)} %get-tuple-element.20.pick_ref, ...), custom_call_target="tpu_custom_call" | custom-call | flops 1000000000 | bytes 1245184 | tf_op jit(solution)/shard_map/second/pallas_call | solution.py:467
  37.0 4.0 %collective-permute-start.3 = (bf16[32,256]{1,0:T(8,128)(2,1)S(1)}, bf16[32,256]{1,0:T(8,128)(2,1)S(1)}, u32[]{:S(2)}, u32[]{:S(2)}) collective-permute-start(bf16[32,256]{1,0:T(8,128)(2,1)S(1)} %get-tuple-element.28), channel_id=1, source_target_pairs={{1,2},{3,4},{5,6},{7,8},{9,10},{11,12},{13,14},{15,16},{17,18},{19... | collective-permute-start | bytes 49160 | tf_op jit(solution)/shard_map/ppermute | solution.py:417
  41.0 1.9 %collective-permute-start.2 = (bf16[32,256]{1,0:T(8,128)(2,1)S(1)}, bf16[32,256]{1,0:T(8,128)(2,1)S(1)}, u32[]{:S(2)}, u32[]{:S(2)}) collective-permute-start(bf16[32,256]{1,0:T(8,128)(2,1)S(1)} %get-tuple-element.28), channel_id=1, source_target_pairs={{0,1},{2,3},{4,5},{6,7},{8,9},{10,11},{12,13},{14,15},{16,17},{18,... | collective-permute-start | bytes 49160 | tf_op jit(solution)/shard_map/ppermute | solution.py:417
  43.0 0.0 copy-done.2
  43.0 0.0 copy-done.5
  43.0 0.0 copy-done.9
  43.0 0.8 %local.1 = (f32[192,256]{1,0:T(8,128)S(1)}, bf16[16,16,256]{2,1,0:T(8,128)(2,1)S(1)}) custom-call(bf16[16,1536]{1,0:T(8,128)(2,1)S(1)} %get-tuple-element.18.mine_ref, f32[16,256]{1,0:T(8,128)S(1)} %get-tuple-element.25.mine_side_ref, bf16[3,384,256]{2,1,0:T(8,128)(2,1)S(1)} %get-tuple-element.26.held_ref, bf16[256,512]{1,0:T(8,128)(2,1)S(1)} %copy-done.3, ...), custom_call_target="tpu_custom_call" | custom-call | flops 1000000000 | bytes 655360 | tf_op jit(solution)/shard_map/local/pallas_call | solution.py:477
  43.8 2.1 %collective-permute-done.3.far_ref = bf16[32,256]{1,0:T(8,128)(2,1)S(1)} collective-permute-done((bf16[32,256]{1,0:T(8,128)(2,1)S(1)}, bf16[32,256]{1,0:T(8,128)(2,1)S(1)}, u32[]{:S(2)}, u32[]{:S(2)}) %collective-permute-start.3) | collective-permute-done | bytes 16416 | tf_op jit(solution)/shard_map/ppermute | solution.py:417
  46.0 0.7 %collective-permute-done.2.near_ref = bf16[32,256]{1,0:T(8,128)(2,1)S(1)} collective-permute-done((bf16[32,256]{1,0:T(8,128)(2,1)S(1)}, bf16[32,256]{1,0:T(8,128)(2,1)S(1)}, u32[]{:S(2)}, u32[]{:S(2)}) %collective-permute-start.2) | collective-permute-done | bytes 16416 | tf_op jit(solution)/shard_map/ppermute | solution.py:417
  46.7 1.2 %final.1 = (bf16[16,16,256]{2,1,0:T(8,128)(2,1)}, f32[16,16,256]{2,1,0:T(8,128)}) custom-call(f32[192,256]{1,0:T(8,128)S(1)} %get-tuple-element.27.inner_ref, bf16[32,256]{1,0:T(8,128)(2,1)S(1)} %collective-permute-done.2.near_ref, bf16[32,256]{1,0:T(8,128)(2,1)S(1)} %collective-permute-done.3.far_ref, bf16[512,256]{1,0:T(8,128)(2,1)S(1)} %get-tuple-element.20.pick_ref, ...), custom_call_target="tpu_custom_call" | custom-call | flops 100000000 | bytes 786432 | tf_op jit(solution)/shard_map/final/pallas_call | solution.py:485
Async XLA Ops:
  0.6 22.1 %copy-start.8 = (bf16[64,256]{1,0:T(8,128)(2,1)S(1)}, bf16[64,256]{1,0:T(8,128)(2,1)}, u32[]{:S(2)}) copy-start(bf16[64,256]{1,0:T(8,128)(2,1)} %constant.27.clone.rows_ref) | copy-start | bytes 98308
  0.6 22.1 %copy-start.16 = (bf16[256,128]{1,0:T(8,128)(2,1)S(1)}, bf16[256,128]{1,0:T(8,128)(2,1)}, u32[]{:S(2)}) copy-start(bf16[256,128]{1,0:T(8,128)(2,1)} %constant.35.clone.inv_side_ref) | copy-start | bytes 196612
  0.7 22.1 %copy-start.17 = (bf16[128,64]{1,0:T(8,128)(2,1)S(1)}, bf16[128,64]{1,0:T(8,128)(2,1)}, u32[]{:S(2)}) copy-start(bf16[128,64]{1,0:T(8,128)(2,1)} %constant.29.clone.grid_ref) | copy-start | bytes 49156
  0.7 22.1 %copy-start.13 = (s32[16]{0:T(128)S(1)}, s32[16]{0:T(128)}, u32[]{:S(2)}) copy-start(s32[16]{0:T(128)} %param.23) | copy-start | bytes 196
  0.7 22.1 %copy-start.12 = (f32[16]{0:T(128)S(1)}, f32[16]{0:T(128)}, u32[]{:S(2)}) copy-start(f32[16]{0:T(128)} %param.22) | copy-start | bytes 196
  0.7 22.1 %copy-start.11 = (f32[12,2,31,31]{3,1,2,0:T(2,128)S(1)}, f32[12,2,31,31]{3,1,2,0:T(2,128)}, u32[]{:S(2)}) copy-start(f32[12,2,31,31]{3,1,2,0:T(2,128)} %param.21) | copy-start | bytes 276772
  22.8 8.7 %copy-start = (bf16[1536,256]{1,0:T(8,128)(2,1)S(1)}, bf16[1536,256]{1,0:T(8,128)(2,1)}, u32[]{:S(2)}) copy-start(bf16[1536,256]{1,0:T(8,128)(2,1)} %constant.32.clone.own_ref) | copy-start | bytes 2359300
  22.8 8.7 %copy-start.1 = (bf16[1024,256]{1,0:T(8,128)(2,1)S(1)}, bf16[1024,256]{1,0:T(8,128)(2,1)}, u32[]{:S(2)}) copy-start(bf16[1024,256]{1,0:T(8,128)(2,1)} %constant.33.clone.inside_ref) | copy-start | bytes 1572868
  22.8 8.7 %copy-start.3 = (bf16[256,512]{1,0:T(8,128)(2,1)S(1)}, bf16[256,512]{1,0:T(8,128)(2,1)}, u32[]{:S(2)}) copy-start(bf16[256,512]{1,0:T(8,128)(2,1)} %constant.30.clone.inv_ref) | copy-start | bytes 786436
  22.8 8.7 %copy-start.4 = (bf16[512,256]{1,0:T(8,128)(2,1)S(1)}, bf16[512,256]{1,0:T(8,128)(2,1)}, u32[]{:S(2)}) copy-start(bf16[512,256]{1,0:T(8,128)(2,1)} %constant.36.clone.reach_ref) | copy-start | bytes 786436
  22.8 8.7 %copy-start.6 = (bf16[256,256]{1,0:T(8,128)(2,1)S(1)}, bf16[256,256]{1,0:T(8,128)(2,1)}, u32[]{:S(2)}) copy-start(bf16[256,256]{1,0:T(8,128)(2,1)} %constant.31.clone.across_ref) | copy-start | bytes 393220
  22.9 8.7 %copy-start.7 = (bf16[256,256]{1,0:T(8,128)(2,1)S(1)}, bf16[256,256]{1,0:T(8,128)(2,1)}, u32[]{:S(2)}) copy-start(bf16[256,256]{1,0:T(8,128)(2,1)} %constant.37.clone.tall_ref) | copy-start | bytes 393220
  22.9 8.7 %copy-start.10 = (s32[16,2]{0,1:T(2,128)S(1)}, s32[16,2]{0,1:T(2,128)}, u32[]{:S(2)}) copy-start(s32[16,2]{0,1:T(2,128)} %param.24) | copy-start | bytes 388
  24.2 10.3 %collective-permute-start.1 = (bf16[64,256]{1,0:T(8,128)(2,1)S(1)}, bf16[64,256]{1,0:T(8,128)(2,1)S(1)}, u32[]{:S(2)}, u32[]{:S(2)}) collective-permute-start(bf16[64,256]{1,0:T(8,128)(2,1)S(1)} %get-tuple-element.19), channel_id=1, source_target_pairs={{1,2},{3,4},{5,6},{7,8},{9,10},{11,12},{13,14},{15,16},{17,18},{19... | collective-permute-start | bytes 98312 | tf_op jit(solution)/shard_map/ppermute | solution.py:417
  29.6 5.8 %collective-permute-start = (bf16[64,256]{1,0:T(8,128)(2,1)S(1)}, bf16[64,256]{1,0:T(8,128)(2,1)S(1)}, u32[]{:S(2)}, u32[]{:S(2)}) collective-permute-start(bf16[64,256]{1,0:T(8,128)(2,1)S(1)} %get-tuple-element.19), channel_id=1, source_target_pairs={{0,1},{2,3},{4,5},{6,7},{8,9},{10,11},{12,13},{14,15},{16,17},{18,... | collective-permute-start | bytes 98312 | tf_op jit(solution)/shard_map/ppermute | solution.py:417
  31.6 3.8 %copy-start.14 = (bf16[256,768]{1,0:T(8,128)(2,1)S(1)}, bf16[256,768]{1,0:T(8,128)(2,1)}, u32[]{:S(2)}) copy-start(bf16[256,768]{1,0:T(8,128)(2,1)} %constant.34.clone.rim_ref) | copy-start | bytes 1179652
  31.6 3.8 %copy-start.15 = (bf16[272,128]{1,0:T(8,128)(2,1)S(1)}, bf16[272,128]{1,0:T(8,128)(2,1)}, u32[]{:S(2)}) copy-start(bf16[272,128]{1,0:T(8,128)(2,1)} %constant.28.clone.ext_ref) | copy-start | bytes 208900
  35.4 7.6 %copy-start.2 = (bf16[16,16,256]{2,1,0:T(8,128)(2,1)S(1)}, bf16[16,16,256]{2,1,0:T(8,128)(2,1)}, u32[]{:S(2)}) copy-start(bf16[16,16,256]{2,1,0:T(8,128)(2,1)} %target_ref.3) | copy-start | bytes 393220
  35.4 7.6 %copy-start.5 = (bf16[16,16,256]{2,1,0:T(8,128)(2,1)S(1)}, bf16[16,16,256]{2,1,0:T(8,128)(2,1)}, u32[]{:S(2)}) copy-start(bf16[16,16,256]{2,1,0:T(8,128)(2,1)} %mask_ref.1) | copy-start | bytes 393220
  35.4 7.6 %copy-start.9 = (bf16[32,32]{1,0:T(8,128)(2,1)S(1)}, bf16[32,32]{1,0:T(8,128)(2,1)}, u32[]{:S(2)}) copy-start(bf16[32,32]{1,0:T(8,128)(2,1)} %constant.38.clone.down_ref) | copy-start | bytes 6148
  37.0 9.0 %collective-permute-start.3 = (bf16[32,256]{1,0:T(8,128)(2,1)S(1)}, bf16[32,256]{1,0:T(8,128)(2,1)S(1)}, u32[]{:S(2)}, u32[]{:S(2)}) collective-permute-start(bf16[32,256]{1,0:T(8,128)(2,1)S(1)} %get-tuple-element.28), channel_id=1, source_target_pairs={{1,2},{3,4},{5,6},{7,8},{9,10},{11,12},{13,14},{15,16},{17,18},{19... | collective-permute-start | bytes 49160 | tf_op jit(solution)/shard_map/ppermute | solution.py:417
  41.0 5.6 %collective-permute-start.2 = (bf16[32,256]{1,0:T(8,128)(2,1)S(1)}, bf16[32,256]{1,0:T(8,128)(2,1)S(1)}, u32[]{:S(2)}, u32[]{:S(2)}) collective-permute-start(bf16[32,256]{1,0:T(8,128)(2,1)S(1)} %get-tuple-element.28), channel_id=1, source_target_pairs={{0,1},{2,3},{4,5},{6,7},{8,9},{10,11},{12,13},{14,15},{16,17},{18,... | collective-permute-start | bytes 49160 | tf_op jit(solution)/shard_map/ppermute | solution.py:417

commit v7 on v6

--- a/solution.py
+++ b/solution.py
@@ -177,34 +177,34 @@
             kernels_ref[k, part] = one + pltpu.roll(one, 64, 1)
 
 
-def lay_slots(dose_ref, row_ref, slot_ref, narrow_ref):
-    wide, narrow, quarter = lane_block(128 * USED, 128), lane_block(256, 2 * RB), lane_block(128 * GROUPS, 32)
-    weight, up, down = (jnp.zeros((1, 128 * USED), F32) for _ in range(3))
-    up_narrow, down_narrow = (jnp.zeros((1, 256), F32) for _ in range(2))
-    weight_quarter = jnp.zeros((1, 128 * GROUPS), F32)
+def slot_lanes(dose_ref, row_ref, joined_block, weight_block):
+    up, down, weight = (jnp.zeros(block.shape, F32) for block in (joined_block, joined_block, weight_block))
     rows, doses = row_ref[...], dose_ref[...]
     for g in range(USED):
         row = rows[:, g : g + 1]
         scale = jnp.where(row >= 0, doses[:, g : g + 1], 0.0) * (1.0 / (NK * KF * KF))
-        weight = jnp.where(wide == g, scale, weight)
-        weight_quarter = jnp.where(quarter == g, scale, weight_quarter)
+        weight = jnp.where(weight_block == g, scale, weight)
         if g > 0:
             before = rows[:, g - 1 : g]
             joined = jnp.where((before >= 0) & (row >= 0) & (before == row - 1), 1.0, 0.0)
-            up = jnp.where(wide == g, joined, up)
-            down = jnp.where(wide == g - 1, joined, down)
-            up_narrow = jnp.where(narrow == g, joined, up_narrow)
-            down_narrow = jnp.where(narrow == g - 1, joined, down_narrow)
-    slot_ref[...] = jnp.concatenate([weight, up, down, jnp.zeros((5, 128 * USED), F32)], 0)
-    narrow_ref[...] = jnp.concatenate(
-        [
-            jnp.concatenate([up_narrow, jnp.zeros((1, 128), F32)], 1),
-            jnp.concatenate([down_narrow, jnp.zeros((1, 128), F32)], 1),
-            weight_quarter,
-            jnp.zeros((5, 128 * GROUPS), F32),
-        ],
-        0,
-    )
+            up = jnp.where(joined_block == g, joined, up)
+            down = jnp.where(joined_block == g - 1, joined, down)
+    return up, down, weight
+
+
+def lay_narrow(dose_ref, row_ref, narrow_ref):
+    up, down, weight = slot_lanes(dose_ref, row_ref, lane_block(256, 2 * RB), lane_block(128 * GROUPS, 32))
+    narrow_ref[0:1, :256] = up
+    narrow_ref[1:2, :256] = down
+    narrow_ref[2:3, :] = weight
+
+
+def lay_wide(dose_ref, row_ref, slot_ref):
+    wide = lane_block(128 * USED, 128)
+    up, down, weight = slot_lanes(dose_ref, row_ref, wide, wide)
+    slot_ref[0:1, :] = weight
+    slot_ref[1:2, :] = up
+    slot_ref[2:3, :] = down
 
 
 def lay_pick(side_ref, reach_ref, pick_ref):
@@ -253,15 +253,16 @@
 
 
 def first_kernel(all_ref, rows_ref, plane_ref, grid_ref, inv_side_ref, dose_ref, row_ref,
-                 held_ref, bands_ref, kernels_ref, slot_ref, narrow_ref):
+                 held_ref, bands_ref, kernels_ref, narrow_ref):
     lay_kernels(plane_ref, kernels_ref)
-    lay_slots(dose_ref, row_ref, slot_ref, narrow_ref)
+    lay_narrow(dose_ref, row_ref, narrow_ref)
     inner = dot(rows_ref[...], all_ref[:, :768])
     side_columns(inner, kernels_ref, grid_ref[...], inv_side_ref, narrow_ref, held_ref, bands_ref)
 
 
-def inside_kernel(held_ref, inv_ref, slot_ref, tall_ref, across_ref, rows_ref, inside_ref, all_ref, own_ref,
-                  reach_ref, side_ref, part_ref, edge_ref, mine_ref, pick_ref, cells_ref, blurred, resist_ref):
+def inside_kernel(held_ref, inv_ref, dose_ref, row_ref, tall_ref, across_ref, rows_ref, inside_ref, all_ref, own_ref,
+                  reach_ref, side_ref, part_ref, edge_ref, mine_ref, pick_ref, slot_ref, cells_ref, blurred, resist_ref):
+    lay_wide(dose_ref, row_ref, slot_ref)
     lay_pick(side_ref, reach_ref, pick_ref)
     for j in range(GROUPS):
         cells_ref[:, 512 * j : 512 * (j + 1)] = coarse_group(held_ref, j, COARSE, inv_ref, slot_ref)
@@ -432,29 +433,30 @@
         grant=62 * 2**20,
     )(mask, target, t["cols"])
     rows_all = lax.all_gather(y, "segment", axis=0, tiled=True)
-    held, bands, kernels, slot, narrow = call(
+    doses, rows = dose.reshape(1, SLOTS), slot_row.reshape(1, SLOTS)
+    held, bands, kernels, narrow = call(
         first_kernel,
         [VMEM] * 7,
         [
             shape((GROUPS, NK * COARSE, 256), BF),
             shape((COARSE, 256), BF),
             shape((NK, 2, 32, 128), F32),
-            shape((8, 128 * USED), F32),
             shape((8, 128 * GROUPS), F32),
         ],
         10**9,
         name="first",
-    )(rows_all, t["rows"], plane, t["grid"], t["inv_side"], dose.reshape(1, SLOTS), slot_row.reshape(1, SLOTS))
+    )(rows_all, t["rows"], plane, t["grid"], t["inv_side"], doses, rows)
     from_near = swapped(bands, 0)
     from_far = swapped(bands, 1)
-    part, edge, mine, pick = call(
+    part, edge, mine, pick, slot = call(
         inside_kernel,
-        [VMEM] * 11,
+        [VMEM] * 12,
         [
             shape((64, 64 * USED), F32),
             shape((COARSE, 256), F32),
             shape((ROWS, 128 * USED), BF),
             shape((512, 256), BF),
+            shape((8, 128 * USED), F32),
         ],
         10**9,
         [
@@ -463,7 +465,7 @@
             pltpu.VMEM((EDGE, EDGE * USED), BF),
         ],
         name="inside",
-    )(held, t["inv"], slot, t["tall"], t["across"], t["rows"], t["inside"], rows_all, t["own"], t["reach"], side_source.T)
+    )(held, t["inv"], doses, rows, t["tall"], t["across"], t["rows"], t["inside"], rows_all, t["own"], t["reach"], side_source.T)
     held, bands, mine_side = call(
         second_kernel,
         [VMEM] * 12,

time: 48.1 us -> 48.2 us (level)
  no operation moved by 1% of the time
where the time goes in v7:
time: 48.2 us; the launch traced here: 47.9 us
  blocking collectives  20 us (41%)
  starting transfers between devices  13.3 us (28%)
  Pallas kernels  9.89 us (21%)
  waiting for transfers between devices  3.71 us (8%)
  between operations  0.95 us (2%)
    all_gather x1, blocking collectives, body(): rows_all = lax.all_gather(y, 'segment', axis=0, tiled=True)  20 us
    ppermute x4, starting transfers between devices, swapped(): return lax.ppermute(block, 'tile', pairs + [(j, i) for i, j in pairs])  13.3 us
    ppermute x4, waiting for transfers between devices, swapped(): return lax.ppermute(block, 'tile', pairs + [(j, i) for i, j in pairs])  3.71 us
    pallas_call x1, Pallas kernels, body(): call(inside_kernel, [VMEM] * 12, [shape((64, 64 * USED), F32), shape((COA...  2.91 us
    pallas_call x1, Pallas kernels, body(): call(start_kernel, [HBM] * 3, [shape((ROWS, 128 * USED), BF)], 10 ** 8, [...  2.05 us
    pallas_call x1, Pallas kernels, body(): call(second_kernel, [VMEM] * 12, [shape((GROUPS, NK * EXT, 256), BF), sha...  1.59 us
    pallas_call x1, Pallas kernels, body(): call(first_kernel, [VMEM] * 7, [shape((GROUPS, NK * COARSE, 256), BF), sh...  1.31 us
    pallas_call x1, Pallas kernels, body(): call(final_kernel, [VMEM] * 8, [shape((SLOTS, ROWS, EDGE), BF), shape((SL...  1.21 us
  transfers between devices with their start and end apart: 4, of which 3 were waited for; matrix products, arithmetic and copies ran while one was open for 0% of the time, Pallas kernels for 8%

profile of v7, /device:TPU:198, one launch (start us, length us, event | category | flops | bytes accessed | tf_op | source)
XLA Modules:
  0.0 47.9 jit_solution(12060284739763025130)
XLA Ops:
  0.6 0.0 copy-start.8
  0.6 0.0 copy-start.16
  0.7 0.0 copy-start.17
  0.7 0.0 copy-start.12
  0.7 0.0 copy-start.11
  0.7 0.0 copy-start.13
  0.7 2.1 %start.1 = bf16[16,1536]{1,0:T(8,128)(2,1)} custom-call(bf16[16,16,256]{2,1,0:T(8,128)(2,1)} %mask_ref.1, bf16[16,16,256]{2,1,0:T(8,128)(2,1)} %target_ref.3, bf16[256,256]{1,0:T(8,128)(2,1)} %constant.26.clone.cols_hbm), custom_call_target="tpu_custom_call" | custom-call | flops 100000000 | bytes 98304 | tf_op jit(solution)/shard_map/start/pallas_call | solution.py:426
  2.8 20.0 %all_gather.3.all_ref = bf16[256,1536]{1,0:T(8,128)(2,1)S(1)} all-gather(bf16[16,1536]{1,0:T(8,128)(2,1)} %start.1), channel_id=1, replica_groups=mesh['segment'=16,'tile'=32] {'segment'}, dimensions={0}, use_global_device_ids=true | all-gather | bytes 835584 | tf_op jit(solution)/shard_map/all_gather | solution.py:435
  22.7 0.0 copy-done.8
  22.8 0.0 copy-done.16
  22.8 0.0 copy-done.17
  22.8 0.0 copy-done.12
  22.8 0.0 copy-done.11
  22.8 0.0 copy-done.13
  22.8 0.0 copy-start
  22.8 0.0 copy-start.1
  22.8 0.0 copy-start.3
  22.8 0.0 copy-start.4
  22.8 0.0 copy-start.6
  22.9 0.0 copy-start.7
  22.9 0.0 copy-start.10
  22.9 1.3 %first.1 = (bf16[3,768,256]{2,1,0:T(8,128)(2,1)S(1)}, bf16[64,256]{1,0:T(8,128)(2,1)S(1)}, f32[12,2,32,128]{3,2,1,0:T(8,128)S(1)}, f32[8,384]{1,0:T(8,128)S(1)}) custom-call(bf16[256,1536]{1,0:T(8,128)(2,1)S(1)} %all_gather.3.all_ref, bf16[64,256]{1,0:T(8,128)(2,1)S(1)} %copy-done.8, f32[744,31]{1,0:T(8,128)S(1)} %bitcast.11, ...), custom_call_target="tpu_custom_call" | custom-call | flops 1000000000 | bytes 3235840 | tf_op jit(solution)/shard_map/first/pallas_call | solution.py:437
  24.2 5.4 %collective-permute-start.1 = (bf16[64,256]{1,0:T(8,128)(2,1)S(1)}, bf16[64,256]{1,0:T(8,128)(2,1)S(1)}, u32[]{:S(2)}, u32[]{:S(2)}) collective-permute-start(bf16[64,256]{1,0:T(8,128)(2,1)S(1)} %get-tuple-element.18), channel_id=1, source_target_pairs={{1,2},{3,4},{5,6},{7,8},{9,10},{11,12},{13,14},{15,16},{17,18},{19... | collective-permute-start | bytes 98312 | tf_op jit(solution)/shard_map/ppermute | solution.py:418
  29.6 1.9 %collective-permute-start = (bf16[64,256]{1,0:T(8,128)(2,1)S(1)}, bf16[64,256]{1,0:T(8,128)(2,1)S(1)}, u32[]{:S(2)}, u32[]{:S(2)}) collective-permute-start(bf16[64,256]{1,0:T(8,128)(2,1)S(1)} %get-tuple-element.18), channel_id=1, source_target_pairs={{0,1},{2,3},{4,5},{6,7},{8,9},{10,11},{12,13},{14,15},{16,17},{18,... | collective-permute-start | bytes 98312 | tf_op jit(solution)/shard_map/ppermute | solution.py:418
  31.5 0.0 copy-done
  31.5 0.0 copy-done.1
  31.6 0.0 copy-done.3
  31.6 0.0 copy-done.4
  31.6 0.0 copy-done.6
  31.6 0.0 copy-done.7
  31.6 0.0 copy-done.10
  31.6 0.0 copy-start.14
  31.6 0.0 copy-start.15
  31.6 2.9 %inside.1 = (f32[64,768]{1,0:T(8,128)S(1)}, f32[64,256]{1,0:T(8,128)S(1)}, bf16[16,1536]{1,0:T(8,128)(2,1)S(1)}, bf16[512,256]{1,0:T(8,128)(2,1)S(1)}, f32[8,1536]{1,0:T(8,128)S(1)}) custom-call(bf16[3,768,256]{2,1,0:T(8,128)(2,1)S(1)} %get-tuple-element.16.held_ref, bf16[256,512]{1,0:T(8,128)(2,1)S(1)} %copy-done.3, f32[1,16]{1,0:T(1,128)S(1)} %bitcast.8, ...), custom_call_target="tpu_custom_call" | custom-call | flops 1000000000 | bytes 1245184 | tf_op jit(solution)/shard_map/inside/pallas_call | solution.py:451
  34.5 0.0 collective-permute-done.1.far_ref
  34.5 0.9 %collective-permute-done.near_ref = bf16[64,256]{1,0:T(8,128)(2,1)S(1)} collective-permute-done((bf16[64,256]{1,0:T(8,128)(2,1)S(1)}, bf16[64,256]{1,0:T(8,128)(2,1)S(1)}, u32[]{:S(2)}, u32[]{:S(2)}) %collective-permute-start) | collective-permute-done | bytes 32800 | tf_op jit(solution)/shard_map/ppermute | solution.py:418
  35.4 0.0 copy-done.14
  35.4 0.0 copy-done.15
  35.4 0.0 copy-start.2
  35.4 0.0 copy-start.5
  35.4 0.0 copy-start.9
  35.4 1.6 %second.1 = (bf16[3,384,256]{2,1,0:T(8,128)(2,1)S(1)}, bf16[32,256]{1,0:T(8,128)(2,1)S(1)}, f32[16,256]{1,0:T(8,128)S(1)}) custom-call(bf16[64,256]{1,0:T(8,128)(2,1)S(1)} %collective-permute-done.near_ref, bf16[64,256]{1,0:T(8,128)(2,1)S(1)} %collective-permute-done.1.far_ref, bf16[512,256]{1,0:T(8,128)(2,1)S(1)} %get-tuple-element.19.pick_ref, ...), custom_call_target="tpu_custom_call" | custom-call | flops 1000000000 | bytes 1245184 | tf_op jit(solution)/shard_map/second/pallas_call | solution.py:469
  37.0 4.1 %collective-permute-start.3 = (bf16[32,256]{1,0:T(8,128)(2,1)S(1)}, bf16[32,256]{1,0:T(8,128)(2,1)S(1)}, u32[]{:S(2)}, u32[]{:S(2)}) collective-permute-start(bf16[32,256]{1,0:T(8,128)(2,1)S(1)} %get-tuple-element.28), channel_id=1, source_target_pairs={{1,2},{3,4},{5,6},{7,8},{9,10},{11,12},{13,14},{15,16},{17,18},{19... | collective-permute-start | bytes 49160 | tf_op jit(solution)/shard_map/ppermute | solution.py:418
  41.1 1.9 %collective-permute-start.2 = (bf16[32,256]{1,0:T(8,128)(2,1)S(1)}, bf16[32,256]{1,0:T(8,128)(2,1)S(1)}, u32[]{:S(2)}, u32[]{:S(2)}) collective-permute-start(bf16[32,256]{1,0:T(8,128)(2,1)S(1)} %get-tuple-element.28), channel_id=1, source_target_pairs={{0,1},{2,3},{4,5},{6,7},{8,9},{10,11},{12,13},{14,15},{16,17},{18,... | collective-permute-start | bytes 49160 | tf_op jit(solution)/shard_map/ppermute | solution.py:418
  43.0 0.0 copy-done.2
  43.0 0.0 copy-done.5
  43.0 0.0 copy-done.9
  43.1 0.8 %local.1 = (f32[192,256]{1,0:T(8,128)S(1)}, bf16[16,16,256]{2,1,0:T(8,128)(2,1)S(1)}) custom-call(bf16[16,1536]{1,0:T(8,128)(2,1)S(1)} %get-tuple-element.17.mine_ref, f32[16,256]{1,0:T(8,128)S(1)} %get-tuple-element.24.mine_side_ref, bf16[3,384,256]{2,1,0:T(8,128)(2,1)S(1)} %get-tuple-element.25.held_ref, bf16[256,512]{1,0:T(8,128)(2,1)S(1)} %copy-done.3, ...), custom_call_target="tpu_custom_call" | custom-call | flops 1000000000 | bytes 655360 | tf_op jit(solution)/shard_map/local/pallas_call | solution.py:479
  43.9 2.1 %collective-permute-done.3.far_ref = bf16[32,256]{1,0:T(8,128)(2,1)S(1)} collective-permute-done((bf16[32,256]{1,0:T(8,128)(2,1)S(1)}, bf16[32,256]{1,0:T(8,128)(2,1)S(1)}, u32[]{:S(2)}, u32[]{:S(2)}) %collective-permute-start.3) | collective-permute-done | bytes 16416 | tf_op jit(solution)/shard_map/ppermute | solution.py:418
  46.0 0.7 %collective-permute-done.2.near_ref = bf16[32,256]{1,0:T(8,128)(2,1)S(1)} collective-permute-done((bf16[32,256]{1,0:T(8,128)(2,1)S(1)}, bf16[32,256]{1,0:T(8,128)(2,1)S(1)}, u32[]{:S(2)}, u32[]{:S(2)}) %collective-permute-start.2) | collective-permute-done | bytes 16416 | tf_op jit(solution)/shard_map/ppermute | solution.py:418
  46.7 1.2 %final.1 = (bf16[16,16,256]{2,1,0:T(8,128)(2,1)}, f32[16,16,256]{2,1,0:T(8,128)}) custom-call(f32[192,256]{1,0:T(8,128)S(1)} %get-tuple-element.27.inner_ref, bf16[32,256]{1,0:T(8,128)(2,1)S(1)} %collective-permute-done.2.near_ref, bf16[32,256]{1,0:T(8,128)(2,1)S(1)} %collective-permute-done.3.far_ref, bf16[512,256]{1,0:T(8,128)(2,1)S(1)} %get-tuple-element.19.pick_ref, ...), custom_call_target="tpu_custom_call" | custom-call | flops 100000000 | bytes 786432 | tf_op jit(solution)/shard_map/final/pallas_call | solution.py:487
Async XLA Ops:
  0.6 22.1 %copy-start.8 = (bf16[64,256]{1,0:T(8,128)(2,1)S(1)}, bf16[64,256]{1,0:T(8,128)(2,1)}, u32[]{:S(2)}) copy-start(bf16[64,256]{1,0:T(8,128)(2,1)} %constant.27.clone.rows_ref) | copy-start | bytes 98308
  0.6 22.1 %copy-start.16 = (bf16[256,128]{1,0:T(8,128)(2,1)S(1)}, bf16[256,128]{1,0:T(8,128)(2,1)}, u32[]{:S(2)}) copy-start(bf16[256,128]{1,0:T(8,128)(2,1)} %constant.35.clone.inv_side_ref) | copy-start | bytes 196612
  0.7 22.1 %copy-start.17 = (bf16[128,64]{1,0:T(8,128)(2,1)S(1)}, bf16[128,64]{1,0:T(8,128)(2,1)}, u32[]{:S(2)}) copy-start(bf16[128,64]{1,0:T(8,128)(2,1)} %constant.29.clone.grid_ref) | copy-start | bytes 49156
  0.7 22.1 %copy-start.12 = (s32[16]{0:T(128)S(1)}, s32[16]{0:T(128)}, u32[]{:S(2)}) copy-start(s32[16]{0:T(128)} %param.23) | copy-start | bytes 196
  0.7 22.1 %copy-start.11 = (f32[16]{0:T(128)S(1)}, f32[16]{0:T(128)}, u32[]{:S(2)}) copy-start(f32[16]{0:T(128)} %param.22) | copy-start | bytes 196
  0.7 22.1 %copy-start.13 = (f32[12,2,31,31]{3,1,2,0:T(2,128)S(1)}, f32[12,2,31,31]{3,1,2,0:T(2,128)}, u32[]{:S(2)}) copy-start(f32[12,2,31,31]{3,1,2,0:T(2,128)} %param.21) | copy-start | bytes 276772
  22.8 8.7 %copy-start = (bf16[1536,256]{1,0:T(8,128)(2,1)S(1)}, bf16[1536,256]{1,0:T(8,128)(2,1)}, u32[]{:S(2)}) copy-start(bf16[1536,256]{1,0:T(8,128)(2,1)} %constant.32.clone.own_ref) | copy-start | bytes 2359300
  22.8 8.7 %copy-start.1 = (bf16[1024,256]{1,0:T(8,128)(2,1)S(1)}, bf16[1024,256]{1,0:T(8,128)(2,1)}, u32[]{:S(2)}) copy-start(bf16[1024,256]{1,0:T(8,128)(2,1)} %constant.33.clone.inside_ref) | copy-start | bytes 1572868
  22.8 8.7 %copy-start.3 = (bf16[256,512]{1,0:T(8,128)(2,1)S(1)}, bf16[256,512]{1,0:T(8,128)(2,1)}, u32[]{:S(2)}) copy-start(bf16[256,512]{1,0:T(8,128)(2,1)} %constant.30.clone.inv_ref) | copy-start | bytes 786436
  22.8 8.7 %copy-start.4 = (bf16[512,256]{1,0:T(8,128)(2,1)S(1)}, bf16[512,256]{1,0:T(8,128)(2,1)}, u32[]{:S(2)}) copy-start(bf16[512,256]{1,0:T(8,128)(2,1)} %constant.36.clone.reach_ref) | copy-start | bytes 786436
  22.8 8.7 %copy-start.6 = (bf16[256,256]{1,0:T(8,128)(2,1)S(1)}, bf16[256,256]{1,0:T(8,128)(2,1)}, u32[]{:S(2)}) copy-start(bf16[256,256]{1,0:T(8,128)(2,1)} %constant.31.clone.across_ref) | copy-start | bytes 393220
  22.9 8.7 %copy-start.7 = (bf16[256,256]{1,0:T(8,128)(2,1)S(1)}, bf16[256,256]{1,0:T(8,128)(2,1)}, u32[]{:S(2)}) copy-start(bf16[256,256]{1,0:T(8,128)(2,1)} %constant.37.clone.tall_ref) | copy-start | bytes 393220
  22.9 8.7 %copy-start.10 = (s32[16,2]{0,1:T(2,128)S(1)}, s32[16,2]{0,1:T(2,128)}, u32[]{:S(2)}) copy-start(s32[16,2]{0,1:T(2,128)} %param.24) | copy-start | bytes 388
  24.2 10.3 %collective-permute-start.1 = (bf16[64,256]{1,0:T(8,128)(2,1)S(1)}, bf16[64,256]{1,0:T(8,128)(2,1)S(1)}, u32[]{:S(2)}, u32[]{:S(2)}) collective-permute-start(bf16[64,256]{1,0:T(8,128)(2,1)S(1)} %get-tuple-element.18), channel_id=1, source_target_pairs={{1,2},{3,4},{5,6},{7,8},{9,10},{11,12},{13,14},{15,16},{17,18},{19... | collective-permute-start | bytes 98312 | tf_op jit(solution)/shard_map/ppermute | solution.py:418
  29.6 5.8 %collective-permute-start = (bf16[64,256]{1,0:T(8,128)(2,1)S(1)}, bf16[64,256]{1,0:T(8,128)(2,1)S(1)}, u32[]{:S(2)}, u32[]{:S(2)}) collective-permute-start(bf16[64,256]{1,0:T(8,128)(2,1)S(1)} %get-tuple-element.18), channel_id=1, source_target_pairs={{0,1},{2,3},{4,5},{6,7},{8,9},{10,11},{12,13},{14,15},{16,17},{18,... | collective-permute-start | bytes 98312 | tf_op jit(solution)/shard_map/ppermute | solution.py:418
  31.6 3.8 %copy-start.14 = (bf16[256,768]{1,0:T(8,128)(2,1)S(1)}, bf16[256,768]{1,0:T(8,128)(2,1)}, u32[]{:S(2)}) copy-start(bf16[256,768]{1,0:T(8,128)(2,1)} %constant.34.clone.rim_ref) | copy-start | bytes 1179652
  31.6 3.8 %copy-start.15 = (bf16[272,128]{1,0:T(8,128)(2,1)S(1)}, bf16[272,128]{1,0:T(8,128)(2,1)}, u32[]{:S(2)}) copy-start(bf16[272,128]{1,0:T(8,128)(2,1)} %constant.28.clone.ext_ref) | copy-start | bytes 208900
  35.4 7.6 %copy-start.2 = (bf16[16,16,256]{2,1,0:T(8,128)(2,1)S(1)}, bf16[16,16,256]{2,1,0:T(8,128)(2,1)}, u32[]{:S(2)}) copy-start(bf16[16,16,256]{2,1,0:T(8,128)(2,1)} %target_ref.3) | copy-start | bytes 393220
  35.4 7.6 %copy-start.5 = (bf16[16,16,256]{2,1,0:T(8,128)(2,1)S(1)}, bf16[16,16,256]{2,1,0:T(8,128)(2,1)}, u32[]{:S(2)}) copy-start(bf16[16,16,256]{2,1,0:T(8,128)(2,1)} %mask_ref.1) | copy-start | bytes 393220
  35.4 7.6 %copy-start.9 = (bf16[32,32]{1,0:T(8,128)(2,1)S(1)}, bf16[32,32]{1,0:T(8,128)(2,1)}, u32[]{:S(2)}) copy-start(bf16[32,32]{1,0:T(8,128)(2,1)} %constant.38.clone.down_ref) | copy-start | bytes 6148
  37.0 9.0 %collective-permute-start.3 = (bf16[32,256]{1,0:T(8,128)(2,1)S(1)}, bf16[32,256]{1,0:T(8,128)(2,1)S(1)}, u32[]{:S(2)}, u32[]{:S(2)}) collective-permute-start(bf16[32,256]{1,0:T(8,128)(2,1)S(1)} %get-tuple-element.28), channel_id=1, source_target_pairs={{1,2},{3,4},{5,6},{7,8},{9,10},{11,12},{13,14},{15,16},{17,18},{19... | collective-permute-start | bytes 49160 | tf_op jit(solution)/shard_map/ppermute | solution.py:418
  41.1 5.6 %collective-permute-start.2 = (bf16[32,256]{1,0:T(8,128)(2,1)S(1)}, bf16[32,256]{1,0:T(8,128)(2,1)S(1)}, u32[]{:S(2)}, u32[]{:S(2)}) collective-permute-start(bf16[32,256]{1,0:T(8,128)(2,1)S(1)} %get-tuple-element.28), channel_id=1, source_target_pairs={{0,1},{2,3},{4,5},{6,7},{8,9},{10,11},{12,13},{14,15},{16,17},{18,... | collective-permute-start | bytes 49160 | tf_op jit(solution)/shard_map/ppermute | solution.py:418
